TPU v7x, 32 devices: a whole 2x2x4 slice. The times are simulated.
32 devices in a mesh: grp: 2 (over x), pts: 8 (over z, y), maps: 2 (over core).
Axes of the slice: x: 2, y: 2, z: 4, core: 2. Of those that a mesh axis runs over, the one named last changes fastest.
Arguments:
- features: bfloat16 [32768, 128], P(('grp', 'pts', 'maps')), parts along dimension 0, may hold values from -6 to 6
- target: bfloat16 [128, 32768], P('maps', ('grp', 'pts')), parts along dimension 1, may hold values from -6 to 6
- branch: bfloat16 [256, 1024], P(('grp', 'maps'), 'pts'), parts along dimension 0, may hold values from -6 to 6
- w_in: bfloat16 [1024, 128], P(('pts', 'maps')), may hold values from -0.5 to 0.5
- w_mid: bfloat16 [1024, 1024], P(('pts', 'maps')), may hold values from -0.1875 to 0.1875
- w_out: bfloat16 [1024, 1024], P(('pts', 'maps')), may hold values from -0.1875 to 0.1875
Outputs:
- grad_branch: float32 [1024, 256], P('pts', ('grp', 'maps')), parts along dimension 1
- grad_in: float32 [2048, 128], P(('grp', 'pts', 'maps')), parts along dimension 0
- grad_mid: float32 [2048, 1024], P(('grp', 'pts', 'maps')), parts along dimension 0
- grad_out: float32 [2048, 1024], P(('grp', 'pts', 'maps')), parts along dimension 0
There are 2 independent parts, one for each index of `grp`. A program takes and returns all parts, laid end to end along the dimension named above; an argument that names none is the same for every part. Nothing has to cross between parts.
All inputs are finite; a program needn't handle non-finite values.
Results may differ from a plain program's by a relative error of at most 0.0016.
Values may be sent and summed in bfloat16 or wider, within the bound.
No kernel may reach another device: no remote copies, remote signals or barrier semaphores. Data moves between devices by JAX's collectives and lax.ppermute only.
A program may use at most 64 MiB of HBM per device.

v0:
```python
import math

import jax
import jax.numpy as jnp
from jax import lax
from jax.sharding import PartitionSpec as P


def contract(left, right, left_dim, right_dim):
    return lax.dot_general(
        left, right, (((left_dim,), (right_dim,)), ((), ())), preferred_element_type=jnp.float32
    )


def contract_exact(left, right, left_dim, right_dim):
    return lax.dot_general(
        left.astype(jnp.float32),
        right.astype(jnp.float32),
        (((left_dim,), (right_dim,)), ((), ())),
        precision=lax.Precision.HIGHEST,
        preferred_element_type=jnp.float32,
    )


def fold_rows(left, piece):
    return jnp.dot(left, piece, preferred_element_type=jnp.float32)


def col_term(left, right):
    return contract(left, right, 0, 0)


def per_device(features, target, branch, w_in, w_mid, w_out):
    width = branch.shape[1] * lax.axis_size("pts")
    scale_b = 1.0 / math.sqrt(width)
    scale_p = 1.0 / math.sqrt(target.shape[1] * lax.axis_size("pts"))
    branch_full = lax.all_gather(branch, "pts", axis=1, tiled=True)
    first = jnp.tanh(
        contract(features, lax.all_gather(w_in, ("pts", "maps"), axis=0, tiled=True), 1, 1)
    ).astype(jnp.bfloat16)
    second = jnp.tanh(
        fold_rows(first, lax.all_gather(w_mid, ("pts", "maps"), axis=0, tiled=True))
    ).astype(jnp.bfloat16)
    trunk = fold_rows(second, lax.all_gather(w_out, ("pts", "maps"), axis=0, tiled=True)).astype(
        jnp.bfloat16
    )
    trunk_all = lax.all_gather(trunk, "maps", axis=0, tiled=True)
    field = contract(branch_full, trunk_all, 1, 1) * scale_b
    resid = (field - target.astype(jnp.float32)) * scale_p
    grad_branch = lax.psum_scatter(
        contract_exact(trunk_all, resid, 0, 1) * scale_b, "pts", scatter_dimension=0, tiled=True
    )
    d_trunk = lax.psum_scatter(
        contract_exact(resid, branch_full, 0, 0) * scale_b, "maps", scatter_dimension=0, tiled=True
    ).astype(jnp.bfloat16)
    grad_out = lax.psum_scatter(
        col_term(second, d_trunk), ("pts", "maps"), scatter_dimension=0, tiled=True
    )
    back_second = contract(
        d_trunk, lax.all_gather(w_out, ("pts", "maps"), axis=0, tiled=True), 1, 1
    )
    second_f = second.astype(jnp.float32)
    dz_second = (back_second * (1.0 - second_f * second_f)).astype(jnp.bfloat16)
    grad_mid = lax.psum_scatter(
        col_term(first, dz_second), ("pts", "maps"), scatter_dimension=0, tiled=True
    )
    back_first = contract(
        dz_second, lax.all_gather(w_mid, ("pts", "maps"), axis=0, tiled=True), 1, 1
    )
    first_f = first.astype(jnp.float32)
    dz_first = (back_first * (1.0 - first_f * first_f)).astype(jnp.bfloat16)
    grad_in = lax.psum_scatter(
        col_term(dz_first, features), ("pts", "maps"), scatter_dimension=0, tiled=True
    )
    return (grad_branch, grad_in, grad_mid, grad_out)


def solution(mesh):
    in_specs = (
        P(("grp", "pts", "maps"), None),
        P("maps", ("grp", "pts")),
        P(("grp", "maps"), "pts"),
        P(("pts", "maps"), None),
        P(("pts", "maps"), None),
        P(("pts", "maps"), None),
    )
    out_specs = (
        P("pts", ("grp", "maps")),
        P(("grp", "pts", "maps"), None),
        P(("grp", "pts", "maps"), None),
        P(("grp", "pts", "maps"), None),
    )
    return jax.shard_map(
        per_device, mesh=mesh, in_specs=in_specs, out_specs=out_specs, check_vma=False
    )
```

profile of v0, /device:TPU:0, one launch (start us, length us, event | category | flops | bytes accessed | tf_op | source)
XLA Modules:
  0.0 438.9 jit_solution(5733924302257224212)
XLA Ops:
  7.2 0.7 all-gather.4.cloned.1.call-update
  8.0 0.7 all-gather.6.cloned.1.call-update
  8.7 24.3 %all_gather.17 = bf16[1024,128]{1,0:T(8,128)(2,1)S(1)} all-gather(bf16[64,128]{1,0:T(8,128)(2,1)} %param.9), channel_id=1, replica_groups=mesh['grp'=2,'pts'=8,'maps'=2] {'pts','maps'}, dimensions={0}, use_global_device_ids=true | all-gather | bytes 278528 | tf_op jit(solution)/shard_map/all_gather | solution.py:39
  33.0 0.7 tanh_convert_fusion.1
  33.7 20.8 %all-gather.4.cloned.1.call-done = bf16[1024,1024]{1,0:T(8,128)(2,1)} async-done(((bf16[64,1024]{1,0:T(8,128)(2,1)}), bf16[1024,1024]{1,0:T(8,128)(2,1)}) %all-gather.4.cloned.1.call-update) | async-done | bytes 2097168 | tf_op jit(solution)/shard_map/all_gather | solution.py:42
  54.5 5.2 %tanh_convert_fusion = bf16[1024,1024]{1,0:T(8,128)(2,1)} fusion(bf16[1024,1024]{1,0:T(8,128)(2,1)S(1)} %tanh_convert_fusion.1, bf16[1024,1024]{1,0:T(8,128)(2,1)} %all-gather.4.cloned.1.call-done), kind=kOutput, calls=%fused_computation.3 | convolution fusion | flops 2148532224 | bytes 6291456 | tf_op jit(solution)/shard_map/dot_general | solution.py:26
  59.8 37.1 %all-gather.6.cloned.1.call-done = bf16[1024,1024]{1,0:T(8,128)(2,1)} async-done(((bf16[64,1024]{1,0:T(8,128)(2,1)}), bf16[1024,1024]{1,0:T(8,128)(2,1)}) %all-gather.6.cloned.1.call-update) | async-done | bytes 2097168 | tf_op jit(solution)/shard_map/all_gather | solution.py:44
  96.9 5.9 %convolution_convert_fusion = bf16[1024,1024]{1,0:T(8,128)(2,1)} fusion(bf16[1024,1024]{1,0:T(8,128)(2,1)} %tanh_convert_fusion, bf16[1024,1024]{1,0:T(8,128)(2,1)} %all-gather.6.cloned.1.call-done), kind=kOutput, calls=%fused_computation.9 | convolution fusion | flops 2148532224 | bytes 6291456 | tf_op jit(solution)/shard_map/dot_general | solution.py:26
  102.8 0.6 copy-done.2
  103.5 26.3 %all_gather.21 = bf16[64,1024]{1,0:T(8,128)(2,1)S(1)} all-gather(bf16[64,128]{1,0:T(8,128)(2,1)S(1)} %copy-done.2), channel_id=1, replica_groups=mesh['grp'=2,'pts'=8,'maps'=2] {'pts'}, dimensions={1}, use_global_device_ids=true | all-gather | bytes 147456 | tf_op jit(solution)/shard_map/all_gather | solution.py:37
  129.8 3.6 fusion.2
  133.3 5.7 %convolution_multiply_fusion = f32[2048,1024]{1,0:T(8,128)} fusion(f32[64,2048]{1,0:T(8,128)S(1)} %fusion.2, bf16[64,1024]{1,0:T(8,128)(2,1)S(1)} %all_gather.21), kind=kOutput, calls=%fused_computation | convolution fusion | flops 1612709888 | bytes 9043968 | tf_op jit(solution)/shard_map/dot_general | solution.py:16
  139.1 5.2 %convolution_multiply_fusion.2 = f32[1024,64]{0,1:T(8,128)} fusion(bf16[2048,1024]{1,0:T(8,128)(2,1)} %all-gather.8.cloned.1.call-done, f32[64,2048]{1,0:T(8,128)S(1)} %fusion.2), kind=kOutput, calls=%fused_computation.11 | convolution fusion | flops 1610678272 | bytes 4980736 | tf_op jit(solution)/shard_map/dot_general | solution.py:16
  144.3 0.2 reduce-scatter.10.cloned.1.call-start
  144.6 8.7 %reduce-scatter.8.cloned.1.call-done = f32[1024,1024]{1,0:T(8,128)} async-done(((f32[2048,1024]{1,0:T(8,128)}), f32[1024,1024]{1,0:T(8,128)}) %reduce-scatter.8.cloned.1.call-update) | async-done | bytes 4194320 | tf_op jit(solution)/shard_map/reduce_scatter | solution.py:53
  153.3 7.2 %multiply_convert_fusion.1 = bf16[1024,1024]{1,0:T(8,128)(2,1)} fusion(bf16[1024,1024]{1,0:T(8,128)(2,1)} %tanh_convert_fusion, bf16[1024,1024]{1,0:T(8,128)(2,1)} %all-gather.6.cloned.1.call-done, f32[1024,1024]{1,0:T(8,128)} %reduce-scatter.8.cloned.1.call-done), kind=kOutput, calls=%fused_computation.2 | convolution fusion | flops 2153775104 | bytes 10485760 | tf_op jit(solution)/shard_map/dot_general | solution.py:10
  160.5 6.8 %fusion.3 = f32[1024,128]{1,0:T(8,128)} fusion(bf16[1024,128]{1,0:T(8,128)(2,1)S(1)} %copy-done, bf16[1024,1024]{1,0:T(8,128)(2,1)S(1)} %tanh_convert_fusion.1, bf16[1024,1024]{1,0:T(8,128)(2,1)} %multiply_convert_fusion.1, bf16[1024,1024]{1,0:T(8,128)(2,1)} %all-gather.4.cloned.1.call-done), kind=kOutput, calls=%fused_computation.10 | convolution fusion | flops 2421161984 | bytes 7077888 | tf_op jit(solution)/shard_map/dot_general | solution.py:10
  167.3 5.9 %fusion.8 = f32[1024,1024]{1,0:T(8,128)} fusion(bf16[1024,1024]{1,0:T(8,128)(2,1)S(1)} %tanh_convert_fusion.1, bf16[1024,1024]{1,0:T(8,128)(2,1)} %multiply_convert_fusion.1), kind=kOutput, calls=%fused_computation.16 | convolution fusion | flops 2147483648 | bytes 8388608 | tf_op jit(solution)/shard_map/dot_general | solution.py:10
  173.3 1.5 copy-done.3
  174.9 6.5 %fusion.4 = f32[1024,1024]{1,0:T(8,128)} fusion(bf16[1024,1024]{1,0:T(8,128)(2,1)S(1)} %copy-done.3, f32[1024,1024]{1,0:T(8,128)} %reduce-scatter.8.cloned.1.call-done), kind=kOutput, calls=%fused_computation.12 | convolution fusion | flops 2148532224 | bytes 10485760 | tf_op jit(solution)/shard_map/dot_general | solution.py:10
  181.4 38.9 %reduce-scatter.6.cloned.1.call-done = f32[128,64]{0,1:T(8,128)} async-done(((f32[1024,64]{0,1:T(8,128)}), f32[128,64]{0,1:T(8,128)}) %reduce-scatter.6.cloned.1.call-update) | async-done | bytes 32784 | tf_op jit(solution)/shard_map/reduce_scatter | solution.py:50
  220.3 59.3 %reduce-scatter.10.cloned.1.call-done = f32[64,128]{1,0:T(8,128)} async-done(((f32[1024,128]{1,0:T(8,128)}), f32[64,128]{1,0:T(8,128)}) %reduce-scatter.10.cloned.1.call-update) | async-done | bytes 32784 | tf_op jit(solution)/shard_map/reduce_scatter | solution.py:72
  279.6 75.8 %reduce-scatter.12.cloned.1.call-done = f32[64,1024]{1,0:T(8,128)} async-done(((f32[1024,1024]{1,0:T(8,128)}), f32[64,1024]{1,0:T(8,128)}) %reduce-scatter.12.cloned.1.call-update) | async-done | bytes 262160 | tf_op jit(solution)/shard_map/reduce_scatter | solution.py:64
  355.4 76.7 %reduce-scatter.14.cloned.1.call-done = f32[64,1024]{1,0:T(8,128)} async-done(((f32[1024,1024]{1,0:T(8,128)}), f32[64,1024]{1,0:T(8,128)}) %reduce-scatter.14.cloned.1.call-update) | async-done | bytes 262160 | tf_op jit(solution)/shard_map/reduce_scatter | solution.py:56
  (20 shorter events, 0.4 us)
Async XLA Ops:
  7.2 25.9 %copy-start = (bf16[1024,128]{1,0:T(8,128)(2,1)S(1)}, bf16[1024,128]{1,0:T(8,128)(2,1)}, u32[]{:S(2)}) copy-start(bf16[1024,128]{1,0:T(8,128)(2,1)} %param.6) | copy-start | bytes 786436
  7.2 47.3 %all-gather.4.cloned.1.call-start = ((), (), s32[]{:S(2)}) async-start(), calls=%async_computation.5 | async-start | bytes 2228224 | tf_op jit(solution)/shard_map/all_gather | solution.py:42
  7.9 89.0 %all-gather.6.cloned.1.call-start = ((), (), s32[]{:S(2)}) async-start(), calls=%async_computation.6 | async-start | bytes 2228224 | tf_op jit(solution)/shard_map/all_gather | solution.py:44
  8.7 121.1 %all-gather.8.cloned.1.call-start = ((), (), s32[]{:S(2)}) async-start(), calls=%async_computation.7 | async-start | bytes 6291456 | tf_op jit(solution)/shard_map/all_gather | solution.py:47
  102.8 0.7 copy-start.2
  102.8 27.0 %copy-start.1 = (bf16[64,2048]{1,0:T(8,128)(2,1)S(1)}, bf16[64,2048]{1,0:T(8,128)(2,1)}, u32[]{:S(2)}) copy-start(bf16[64,2048]{1,0:T(8,128)(2,1)} %param.7) | copy-start | bytes 786436
  102.8 50.5 %reduce-scatter.8.cloned.1.call-start = ((), (), s32[]{:S(2)}) async-start(), calls=%async_computation.9 | async-start | bytes 12582912 | tf_op jit(solution)/shard_map/reduce_scatter | solution.py:53
  139.1 81.2 %reduce-scatter.6.cloned.1.call-start = ((), (), s32[]{:S(2)}) async-start(), calls=%async_computation.8 | async-start | bytes 294912 | tf_op jit(solution)/shard_map/reduce_scatter | solution.py:50
  144.3 135.3 %reduce-scatter.10.cloned.1.call-start = ((), (), s32[]{:S(2)}) async-start(), calls=%async_computation.10 | async-start | bytes 557056 | tf_op jit(solution)/shard_map/reduce_scatter | solution.py:72
  167.3 188.1 %reduce-scatter.12.cloned.1.call-start = ((), (), s32[]{:S(2)}) async-start(), calls=%async_computation.11 | async-start | bytes 4456448 | tf_op jit(solution)/shard_map/reduce_scatter | solution.py:64
  173.2 1.6 copy-start.3
  173.3 258.8 %reduce-scatter.14.cloned.1.call-start = ((), (), s32[]{:S(2)}) async-start(), calls=%async_computation.12 | async-start | bytes 4456448 | tf_op jit(solution)/shard_map/reduce_scatter | solution.py:56
Sparse Core Ops, SparseCore 0:
  10.2 44.3 all-gather.3
  56.7 40.1 all-gather.5
  102.9 12.4 all-gather.7
  139.2 14.0 reduce-scatter.7
  157.4 62.8 reduce-scatter.5
  224.7 54.8 reduce-scatter.9
  284.0 71.3 reduce-scatter.11
  360.3 71.7 reduce-scatter.13
where the time goes:
time: 439 us
  waiting for transfers between devices  319 us (73%)
  matrix products  52.8 us (12%)
  blocking collectives  50.6 us (12%)
  between operations  14.2 us (3%)
    reduce_scatter x1, waiting for transfers between devices, per_device(): lax.psum_scatter(col_term(second, d_trunk), ('pts', 'maps'), scatter_dime...  76.7 us
    reduce_scatter x1, waiting for transfers between devices, per_device(): lax.psum_scatter(col_term(first, dz_second), ('pts', 'maps'), scatter_dim...  75.8 us
    reduce_scatter x1, waiting for transfers between devices, per_device(): lax.psum_scatter(col_term(dz_first, features), ('pts', 'maps'), scatter_d...  59.3 us
    reduce_scatter x1, waiting for transfers between devices, per_device(): lax.psum_scatter(contract_exact(trunk_all, resid, 0, 1) * scale_b, 'pts',...  38.9 us
    all_gather x1, waiting for transfers between devices, per_device(): lax.all_gather(w_out, ('pts', 'maps'), axis=0, tiled=True)  37.1 us
    dot_general x6, matrix products, contract(): lax.dot_general(left, right, (((left_dim,), (right_dim,)), ((), ())), pre...  30.7 us
    all_gather x1, blocking collectives, per_device(): branch_full = lax.all_gather(branch, 'pts', axis=1, tiled=True)  26.3 us
    all_gather x1, blocking collectives, per_device(): lax.all_gather(w_in, ('pts', 'maps'), axis=0, tiled=True)  24.3 us
  transfers between devices with their start and end apart: 8, of which 7 were waited for; matrix products, arithmetic and copies ran while one was open for 9% of the time, Pallas kernels for 0%

commit v1 on v0

v1 whole, which is shorter than its diff:
```python
import functools
import math

import jax
import jax.numpy as jnp
from jax import lax
from jax.experimental import pallas as pl
from jax.experimental.pallas import tpu as pltpu
from jax.sharding import PartitionSpec as P

BF = jnp.bfloat16
F32 = jnp.float32
VMEM_BYTES = 56 * 1024 * 1024


def dot(left, right, left_dim, right_dim):
    return lax.dot_general(
        left, right, (((left_dim,), (right_dim,)), ((), ())), preferred_element_type=F32
    )


def dot_exact(left, right, left_dim, right_dim):
    return lax.dot_general(
        left.astype(F32),
        right.astype(F32),
        (((left_dim,), (right_dim,)), ((), ())),
        precision=lax.Precision.HIGHEST,
        preferred_element_type=F32,
    )


def split(value):
    high = lax.reduce_precision(value, 8, 7)
    return high.astype(BF), (value - high).astype(BF)


def encode(value):
    return (value * value * value).astype(BF)


def decode(code):
    cube = code.astype(F32)
    size = jnp.abs(cube)
    root = jnp.exp2(jnp.log2(jnp.maximum(size, 1e-37)) * (1.0 / 3.0))
    return jnp.where(size < 1e-37, 0.0, jnp.where(cube < 0.0, -root, root))


def forward_kernel(features, near, far, first, second):
    half, width = near.shape[0], second.shape[1]
    x = features[...]
    f_near = jnp.tanh(dot(x, near[:, width:], 1, 1)).astype(BF)
    f_far = jnp.tanh(dot(x, far[:, width:], 1, 1)).astype(BF)
    first[:, :half] = f_near
    first[:, half:] = f_far
    z = dot(f_near, near[:, :width], 1, 0) + dot(f_far, far[:, :width], 1, 0)
    second[...] = jnp.tanh(z).astype(BF)


def middle_kernel(
    scale_p, features, first, second, near, far, target, b_high, b_low, total, dz, g_in
):
    half, width = near.shape[0], second.shape[1]

    @pl.when(pl.program_id(0) == 0)
    def _():
        total[...] = jnp.zeros_like(total)
        g_in[...] = jnp.zeros_like(g_in)

    maps = target.shape[1]
    s = second[...]
    bh, bl = b_high[...], b_low[...]
    field = dot(s, bh, 1, 0) + dot(s, bl, 1, 0)
    resid = (field - target[...].astype(F32)) * scale_p
    rh = resid.astype(BF)
    rl = (resid - rh.astype(F32)).astype(BF)
    both = dot(s, jnp.concatenate([rh, rl], axis=1), 0, 0)
    total[...] += both[:, :maps] + both[:, maps:]
    s32 = s.astype(F32)
    back = dot(rh, bh, 1, 1) + dot(rl, bh, 1, 1) + dot(rh, bl, 1, 1)
    d = (back * (1.0 - s32 * s32)).astype(BF)
    dz[...] = d
    f = first[...].astype(F32)
    slope = 1.0 - f * f
    x = features[...]
    d_near = (dot(d, near[:, :width], 1, 1) * slope[:, :half]).astype(BF)
    d_far = (dot(d, far[:, :width], 1, 1) * slope[:, half:]).astype(BF)
    g_in[:half, :] += dot(d_near, x, 0, 0)
    g_in[half:, :] += dot(d_far, x, 0, 0)


def grad_far_kernel(first, dz, g_in, out):
    width = dz.shape[1]
    g = dot(first[...], dz[...], 0, 0)
    out[:, :width] = encode(g)
    out[:, width:] = encode(g_in[...])


def grad_near_kernel(first, dz, g_in, out):
    width = dz.shape[1]
    out[:, :width] = dot(first[...], dz[...], 0, 0)
    out[:, width:] = g_in[...]


def cost(flops, moved):
    return pl.CostEstimate(flops=int(flops), bytes_accessed=int(moved), transcendentals=0)


def params():
    return pltpu.CompilerParams(vmem_limit_bytes=VMEM_BYTES)


def forward(features, near, far):
    points, enc = features.shape
    half, both = near.shape
    width = both - enc
    step = points // 4
    whole = pl.BlockSpec((half, both), lambda i: (0, 0))
    return pl.pallas_call(
        forward_kernel,
        grid=(points // step,),
        in_specs=[pl.BlockSpec((step, enc), lambda i: (i, 0)), whole, whole],
        out_specs=[
            pl.BlockSpec((step, 2 * half), lambda i: (i, 0)),
            pl.BlockSpec((step, width), lambda i: (i, 0)),
        ],
        out_shape=[
            jax.ShapeDtypeStruct((points, 2 * half), BF),
            jax.ShapeDtypeStruct((points, width), BF),
        ],
        compiler_params=params(),
        cost_estimate=cost(2 * points * 2 * half * both, 7e6),
    )(features, near, far)


def middle(scale_p, features, first, second, near, far, target, b_high, b_low):
    points, enc = features.shape
    half, both = near.shape
    width, maps = b_high.shape
    step = points // 4
    rows = lambda n: pl.BlockSpec((step, n), lambda i: (i, 0))
    whole = lambda a, b: pl.BlockSpec((a, b), lambda i: (0, 0))
    return pl.pallas_call(
        functools.partial(middle_kernel, scale_p),
        grid=(points // step,),
        in_specs=[
            rows(enc),
            rows(2 * half),
            rows(width),
            whole(half, both),
            whole(half, both),
            rows(maps),
            whole(width, maps),
            whole(width, maps),
        ],
        out_specs=[whole(width, maps), rows(width), whole(2 * half, enc)],
        out_shape=[
            jax.ShapeDtypeStruct((width, maps), F32),
            jax.ShapeDtypeStruct((points, width), BF),
            jax.ShapeDtypeStruct((2 * half, enc), F32),
        ],
        compiler_params=params(),
        cost_estimate=cost(2 * points * 2 * half * both * 1.8, 10e6),
    )(features, first, second, near, far, target, b_high, b_low)


def grad_half(first, dz, g_in, far):
    points, hidden = first.shape
    width, enc = dz.shape[1], g_in.shape[1]
    half = hidden // 2
    step = half // 2
    base = half // step if far else 0
    return pl.pallas_call(
        grad_far_kernel if far else grad_near_kernel,
        grid=(half // step,),
        in_specs=[
            pl.BlockSpec((points, step), lambda i: (0, i + base)),
            pl.BlockSpec((points, width), lambda i: (0, 0)),
            pl.BlockSpec((step, enc), lambda i: (i + base, 0)),
        ],
        out_specs=pl.BlockSpec((step, width + enc), lambda i: (i, 0)),
        out_shape=jax.ShapeDtypeStruct((half, width + enc), BF if far else F32),
        compiler_params=params(),
        cost_estimate=cost(2 * points * half * width, 6e6),
    )(first, dz, g_in)


def shift(n, mask):
    return [(i, i ^ mask) for i in range(n)]


def per_device(features, target, branch, w_in, w_mid, w_out):
    n_pts = lax.axis_size("pts")
    core = lax.axis_index("maps")
    rows, width = w_mid.shape
    hidden = rows * n_pts * 2
    maps = 2 * branch.shape[0]
    points, enc = features.shape
    scale_b = 1.0 / math.sqrt(width)
    scale_p = 1.0 / math.sqrt(target.shape[1] * n_pts)
    swap_core = lambda v: lax.ppermute(v, "maps", [(0, 1), (1, 0)])
    move = lambda v, mask: lax.ppermute(v, "pts", shift(n_pts, mask))

    pick = lambda flag, a, b: jnp.where(flag, a, b)
    first_core = core == 0

    own = jnp.concatenate([w_mid, w_in], axis=1)
    parts = [own] + [move(own, 2 * k) for k in range(1, n_pts // 2)]
    line = jnp.concatenate(parts, axis=0)
    near = jnp.concatenate([line, move(line, 1)], axis=0)
    far = swap_core(near)

    wide = lax.all_to_all(
        jnp.broadcast_to(branch[None], (n_pts, *branch.shape)), "pts", 0, 0, tiled=True
    )
    wide = wide.transpose(1, 0, 2).reshape(maps // 2, width)
    wide_other = swap_core(wide)
    branch_full = jnp.concatenate(
        [pick(first_core, wide, wide_other), pick(first_core, wide_other, wide)], axis=0
    )
    folded = dot(w_out, branch_full, 1, 1) * scale_b
    spread = lax.all_to_all(
        jnp.broadcast_to(folded[None], (n_pts, rows, maps)), "pts", 0, 0, tiled=True
    )
    other = swap_core(spread)
    b_t = jnp.stack(
        [pick(first_core, spread, other), pick(first_core, other, spread)], axis=1
    ).reshape(hidden, maps)
    b_high, b_low = split(b_t)

    t_own = lax.dynamic_slice_in_dim(target, core * points, points, 1)
    t_other = swap_core(lax.dynamic_slice_in_dim(target, (1 - core) * points, points, 1))
    t_full = jnp.concatenate(
        [pick(first_core, t_own, t_other), pick(first_core, t_other, t_own)], axis=0
    ).T

    first, second = forward(features, near, far)
    total, dz, g_in = middle(
        scale_p, features, first, second, near, far, t_full, b_high, b_low
    )
    send = grad_half(first, dz, g_in, True)
    keep = grad_half(first, dz, g_in, False)

    by_core = total.reshape(n_pts, 2, rows, maps)
    mine = lax.dynamic_index_in_dim(by_core, core, 1, keepdims=False)
    theirs = lax.dynamic_index_in_dim(by_core, 1 - core, 1, keepdims=False)
    mine = mine + swap_core(theirs)
    got = lax.all_to_all(encode(mine), "pts", 0, 0, tiled=True)
    sums = jnp.sum(decode(got), axis=0)
    grad_out = dot_exact(sums, branch_full, 1, 0) * scale_b
    part = dot_exact(sums, w_out, 0, 0) * scale_b
    part_mine = lax.dynamic_slice_in_dim(part, core * (maps // 2), maps // 2, 0)
    part_theirs = lax.dynamic_slice_in_dim(part, (1 - core) * (maps // 2), maps // 2, 0)
    part_mine = part_mine + swap_core(part_theirs)
    blocks = part_mine.reshape(maps // 2, n_pts, width // n_pts).transpose(1, 0, 2)
    got_b = lax.all_to_all(encode(blocks), "pts", 0, 0, tiled=True)
    grad_branch = jnp.sum(decode(got_b), axis=0).T

    both = keep + decode(swap_core(send))
    quarter = hidden // 4
    both = both[:quarter] + decode(move(encode(both[quarter:]), 1))
    chunk = lambda k: both[k * rows : (k + 1) * rows]
    grads = chunk(0)
    for k in range(1, n_pts // 2):
        grads = grads + decode(move(encode(chunk(k)), 2 * k))
    return (grad_branch, grads[:, width:], grads[:, :width], grad_out)


def solution(mesh):
    in_specs = (
        P(("grp", "pts", "maps"), None),
        P("maps", ("grp", "pts")),
        P(("grp", "maps"), "pts"),
        P(("pts", "maps"), None),
        P(("pts", "maps"), None),
        P(("pts", "maps"), None),
    )
    out_specs = (
        P("pts", ("grp", "maps")),
        P(("grp", "pts", "maps"), None),
        P(("grp", "pts", "maps"), None),
        P(("grp", "pts", "maps"), None),
    )
    return jax.shard_map(
        per_device, mesh=mesh, in_specs=in_specs, out_specs=out_specs, check_vma=False
    )
```

time: 439 us -> 123 us (0.28)
  waiting for transfers between devices: 319 us -> 36.6 us
  matrix products: 52.8 us -> 1.84 us
  blocking collectives: 50.6 us -> 0 us
  starting transfers between devices: 0.5 us -> 30.9 us
  Pallas kernels: 0 us -> 27.5 us
  between operations: 14.2 us -> 0.82 us
  other arithmetic: 0 us -> 12.2 us
  local copies, waits for them, and re-layouts: 2.19 us -> 12.1 us
    reduce_scatter x5 -> x0, waiting for transfers between devices: 259 us -> none  [the longest x1 76.7 us: per_device(): lax.psum_scatter(col_term(second, d_trunk), ('pts', 'maps'), scatter_dime...]
    all_gather x3 -> x0, waiting for transfers between devices: 57.9 us -> none  [the longest x1 37.1 us: per_device(): lax.all_gather(w_out, ('pts', 'maps'), axis=0, tiled=True)]
    dot_general x10 -> x3, matrix products: 52.8 us -> 1.84 us  [the longest x2 1.57 us: dot_exact(): lax.dot_general(left.astype(F32), right.astype(F32), (((left_dim,), (righ...]
    all_gather x2 -> x0, blocking collectives: 50.6 us -> none  [the longest x1 26.3 us: per_device(): branch_full = lax.all_gather(branch, 'pts', axis=1, tiled=True)]
    pallas_call x0 -> x4, Pallas kernels: none -> 27.5 us  [the longest x1 12.4 us: middle(): pl.pallas_call(functools.partial(middle_kernel, scale_p), grid=(points //...]
    ppermute x0 -> x15, waiting for transfers between devices: none -> 24.7 us  [the longest x8 18.6 us: per_device(): move = lambda v, mask: lax.ppermute(v, 'pts', shift(n_pts, mask))]
    all_to_all x0 -> x4, starting transfers between devices: none -> 18.1 us  [the longest x1 6.05 us: per_device(): lax.all_to_all(jnp.broadcast_to(branch[None], (n_pts, *branch.shape)), 'p...]
    ppermute x0 -> x15, starting transfers between devices: none -> 12.8 us  [the longest x8 12 us: per_device(): move = lambda v, mask: lax.ppermute(v, 'pts', shift(n_pts, mask))]
  transfers between devices with their start and end apart: 8 -> 19, of which waited for: 7 -> 11; matrix products, arithmetic and copies ran while one was open for 9% -> 13% of each run, Pallas kernels for 0% -> 4%
where the time goes in v1:
time: 123 us; the launch traced here: 122 us
  waiting for transfers between devices  36.6 us (30%)
  starting transfers between devices  30.9 us (25%)
  Pallas kernels  27.5 us (22%)
  other arithmetic  12.2 us (10%)
  local copies, waits for them, and re-layouts  12.1 us (10%)
  matrix products  1.84 us (1%)
    ppermute x8, waiting for transfers between devices, per_device(): move = lambda v, mask: lax.ppermute(v, 'pts', shift(n_pts, mask))  18.6 us
    pallas_call x1, Pallas kernels, middle(): pl.pallas_call(functools.partial(middle_kernel, scale_p), grid=(points //...  12.4 us
    ppermute x8, starting transfers between devices, per_device(): move = lambda v, mask: lax.ppermute(v, 'pts', shift(n_pts, mask))  12 us
    pallas_call x2, Pallas kernels, grad_half(): pl.pallas_call(grad_far_kernel if far else grad_near_kernel, grid=(half /...  8.76 us
    all_to_all x1, waiting for transfers between devices, per_device(): lax.all_to_all(jnp.broadcast_to(folded[None], (n_pts, rows, maps)), 'pts'...  6.91 us
    pallas_call x1, Pallas kernels, forward(): pl.pallas_call(forward_kernel, grid=(points // step,), in_specs=[pl.Block...  6.3 us
    all_to_all x1, starting transfers between devices, per_device(): lax.all_to_all(jnp.broadcast_to(branch[None], (n_pts, *branch.shape)), 'p...  6.05 us
    ppermute x7, waiting for transfers between devices, per_device(): swap_core = lambda v: lax.ppermute(v, 'maps', [(0, 1), (1, 0)])  6.03 us
  transfers between devices with their start and end apart: 19, of which 11 were waited for; matrix products, arithmetic and copies ran while one was open for 13% of the time, Pallas kernels for 4%

profile of v1, /device:TPU:0, one launch (start us, length us, event | category | flops | bytes accessed | tf_op | source)
XLA Modules:
  0.0 122.0 jit_solution(9451380013043201752)
XLA Ops:
  0.7 1.7 %constant_dynamic-update-slice_fusion.1 = (bf16[64,1152]{1,0:T(8,128)(2,1)S(1)}, bf16[512,1152]{1,0:T(8,128)(2,1)}) fusion(bf16[64,1024]{1,0:T(8,128)(2,1)} %param.10), kind=kLoop, calls=%fused_computation.104 | loop fusion | bytes 393216
  3.6 3.0 %collective-permute-start = (bf16[64,1152]{1,0:T(8,128)(2,1)S(1)}, bf16[64,1152]{1,0:T(8,128)(2,1)S(1)}, u32[]{:S(2)}, u32[]{:S(2)}) collective-permute-start(bf16[64,1152]{1,0:T(8,128)(2,1)S(1)} %get-tuple-element.29), channel_id=1, source_target_pairs={{0,4},{2,6},{4,0},{6,2},{8,12},{10,14},{12,8},{14,10},{1,5},{3,7},... | collective-permute-start | bytes 442376 | tf_op jit(solution)/shard_map/ppermute | solution.py:201
  6.7 2.6 %collective-permute-start.1 = (bf16[64,1152]{1,0:T(8,128)(2,1)S(1)}, bf16[64,1152]{1,0:T(8,128)(2,1)S(1)}, u32[]{:S(2)}, u32[]{:S(2)}) collective-permute-start(bf16[64,1152]{1,0:T(8,128)(2,1)S(1)} %get-tuple-element.29), channel_id=1, source_target_pairs={{0,8},{2,10},{4,12},{6,14},{8,0},{10,2},{12,4},{14,6},{1,9},{3,11}... | collective-permute-start | bytes 442376 | tf_op jit(solution)/shard_map/ppermute | solution.py:201
  11.2 6.1 %all-to-all-start = ((bf16[8,64,128]{2,1,0:T(8,128)(2,1)}), bf16[8,64,128]{2,1,0:T(8,128)(2,1)S(1)}, u32[]{:S(2)}, u32[]{:S(2)}) async-start(bf16[8,64,128]{2,1,0:T(8,128)(2,1)} %broadcast_in_dim.31), calls=%async_computation | async-start | bytes 262144 | tf_op jit(solution)/shard_map/all_to_all | solution.py:212
  17.4 3.2 %collective-permute-done.1 = bf16[64,1152]{1,0:T(8,128)(2,1)S(1)} collective-permute-done((bf16[64,1152]{1,0:T(8,128)(2,1)S(1)}, bf16[64,1152]{1,0:T(8,128)(2,1)S(1)}, u32[]{:S(2)}, u32[]{:S(2)}) %collective-permute-start.1) | collective-permute-done | bytes 147488 | tf_op jit(solution)/shard_map/ppermute | solution.py:201
  23.7 2.1 %all-to-all-done = bf16[8,64,128]{2,1,0:T(8,128)(2,1)S(1)} async-done(((bf16[8,64,128]{2,1,0:T(8,128)(2,1)}), bf16[8,64,128]{2,1,0:T(8,128)(2,1)S(1)}, u32[]{:S(2)}, u32[]{:S(2)}) %all-to-all-start) | async-done | bytes 131104 | tf_op jit(solution)/shard_map/all_to_all | solution.py:212
  28.6 4.6 %all-to-all-start.1 = ((f32[8,64,128]{2,1,0:T(8,128)}), f32[8,64,128]{2,1,0:T(8,128)S(1)}, u32[]{:S(2)}, u32[]{:S(2)}) async-start(f32[8,64,128]{2,1,0:T(8,128)} %broadcast_in_dim.32), calls=%async_computation.1 | async-start | bytes 524288 | tf_op jit(solution)/shard_map/all_to_all | solution.py:221
  35.6 6.9 %all-to-all-done.1 = f32[8,64,128]{2,1,0:T(8,128)S(1)} async-done(((f32[8,64,128]{2,1,0:T(8,128)}), f32[8,64,128]{2,1,0:T(8,128)S(1)}, u32[]{:S(2)}, u32[]{:S(2)}) %all-to-all-start.1) | async-done | bytes 262176 | tf_op jit(solution)/shard_map/all_to_all | solution.py:221
  45.0 6.3 %shard_map.93 = (bf16[1024,1024]{1,0:T(8,128)(2,1)}, bf16[1024,1024]{1,0:T(8,128)(2,1)}) custom-call(bf16[1024,128]{1,0:T(8,128)(2,1)} %features.3, bf16[512,1152]{1,0:T(8,128)(2,1)} %constant_dynamic-update-slice_fusion.2.near, bf16[512,1152]{1,0:T(8,128)(2,1)} %collective-permute-done.4.far), custom_call_target="tpu_custom_call" | custom-call | flops 2415919104 | bytes 7000000 | tf_op jit(solution)/shard_map/pallas_call | solution.py:118
  51.3 12.4 %shard_map.94 = (f32[1024,128]{1,0:T(8,128)}, bf16[1024,1024]{1,0:T(8,128)(2,1)}, f32[1024,128]{1,0:T(8,128)}) custom-call(bf16[1024,128]{1,0:T(8,128)(2,1)} %features.3, bf16[1024,1024]{1,0:T(8,128)(2,1)} %get-tuple-element.9.first, bf16[1024,1024]{1,0:T(8,128)(2,1)} %get-tuple-element.10.second, ...), custom_call_target="tpu_custom_call" | custom-call | flops 4348654592 | bytes 10000000 | tf_op jit(solution)/shard_map/pallas_call | solution.py:142
  63.7 4.2 %shard_map.96 = bf16[512,1152]{1,0:T(8,128)(2,1)} custom-call(bf16[1024,1024]{1,0:T(8,128)(2,1)} %get-tuple-element.9.first, bf16[1024,1024]{1,0:T(8,128)(2,1)} %get-tuple-element.12.dz, f32[1024,128]{1,0:T(8,128)} %get-tuple-element.13.g_in), custom_call_target="tpu_custom_call" | custom-call | flops 1073741824 | bytes 6000000 | tf_op jit(solution)/shard_map/pallas_call | solution.py:172
  68.5 2.6 %collective-permute-done.8 = f32[8,64,128]{2,1,0:T(8,128)S(1)} collective-permute-done((f32[8,64,128]{2,1,0:T(8,128)S(1)}, f32[8,64,128]{2,1,0:T(8,128)S(1)}, u32[]{:S(2)}, u32[]{:S(2)}) %collective-permute-start.8) | collective-permute-done | bytes 262176 | tf_op jit(solution)/shard_map/ppermute | solution.py:200
  71.9 4.1 %all-to-all-start.2 = ((bf16[8,64,128]{2,1,0:T(8,128)(2,1)}), bf16[8,64,128]{2,1,0:T(8,128)(2,1)S(1)}, u32[]{:S(2)}, u32[]{:S(2)}) async-start(bf16[8,64,128]{2,1,0:T(8,128)(2,1)} %fusion.51), calls=%async_computation.2 | async-start | bytes 262144 | tf_op jit(solution)/shard_map/all_to_all | solution.py:247
  76.0 4.5 %shard_map.95 = f32[512,1152]{1,0:T(8,128)} custom-call(bf16[1024,1024]{1,0:T(8,128)(2,1)} %get-tuple-element.9.first, bf16[1024,1024]{1,0:T(8,128)(2,1)} %get-tuple-element.12.dz, f32[1024,128]{1,0:T(8,128)} %get-tuple-element.13.g_in), custom_call_target="tpu_custom_call" | custom-call | flops 1073741824 | bytes 6000000 | tf_op jit(solution)/shard_map/pallas_call | solution.py:172
  80.5 3.0 %all-to-all-done.2 = bf16[8,64,128]{2,1,0:T(8,128)(2,1)S(1)} async-done(((bf16[8,64,128]{2,1,0:T(8,128)(2,1)}), bf16[8,64,128]{2,1,0:T(8,128)(2,1)S(1)}, u32[]{:S(2)}, u32[]{:S(2)}) %all-to-all-start.2) | async-done | bytes 131104 | tf_op jit(solution)/shard_map/all_to_all | solution.py:247
  84.2 3.1 %fusion.6 = f32[512,1152]{1,0:T(8,128)S(1)} fusion(f32[512,1152]{1,0:T(8,128)} %shard_map.95, bf16[512,1152]{1,0:T(8,128)(2,1)} %collective-permute-done.10), kind=kLoop, calls=%fused_computation.9 | loop fusion | flops 5898240 | bytes 5898240 | tf_op jit(solution)/shard_map/add | solution.py:258
  89.3 1.9 %collective-permute-done.9 = f32[64,1024]{1,0:T(8,128)} collective-permute-done((f32[64,1024]{1,0:T(8,128)}, f32[64,1024]{1,0:T(8,128)}, u32[]{:S(2)}, u32[]{:S(2)}) %collective-permute-start.9) | collective-permute-done | bytes 262176 | tf_op jit(solution)/shard_map/ppermute | solution.py:200
  91.2 1.6 %fusion.54 = bf16[8,64,128]{2,1,0:T(8,128)(2,1)} fusion(f32[64,1024]{1,0:T(8,128)} %collective-permute-done.9, f32[128,1024]{1,0:T(8,128)S(1)} %convolution_multiply_fusion, s32[]{:T(128)S(6)} %select_n.115), kind=kLoop, calls=%fused_computation.88 | loop fusion | flops 262144 | bytes 655364 | tf_op jit(solution)/shard_map/convert_element_type | solution.py:38
  92.8 3.4 %all-to-all-start.3 = ((bf16[8,64,128]{2,1,0:T(8,128)(2,1)}), bf16[8,64,128]{2,1,0:T(8,128)(2,1)S(1)}, u32[]{:S(2)}, u32[]{:S(2)}) async-start(bf16[8,64,128]{2,1,0:T(8,128)(2,1)} %fusion.54), calls=%async_computation.3 | async-start | bytes 262144 | tf_op jit(solution)/shard_map/all_to_all | solution.py:255
  96.2 7.4 %collective-permute-done.11 = bf16[256,1152]{1,0:T(8,128)(2,1)} collective-permute-done((bf16[256,1152]{1,0:T(8,128)(2,1)}, bf16[256,1152]{1,0:T(8,128)(2,1)}, u32[]{:S(2)}, u32[]{:S(2)}) %collective-permute-start.11) | collective-permute-done | bytes 589856 | tf_op jit(solution)/shard_map/ppermute | solution.py:201
  103.6 1.6 %fusion.14 = f32[256,1152]{1,0:T(8,128)S(1)} fusion(bf16[256,1152]{1,0:T(8,128)(2,1)} %collective-permute-done.11, f32[512,1152]{1,0:T(8,128)S(1)} %fusion.6), kind=kLoop, calls=%fused_computation.22 | loop fusion | flops 2949120 | bytes 2949120 | tf_op jit(solution)/shard_map/add | solution.py:260
  106.6 2.3 %collective-permute-start.13 = (bf16[64,1152]{1,0:T(8,128)(2,1)S(1)}, bf16[64,1152]{1,0:T(8,128)(2,1)S(1)}, u32[]{:S(2)}, u32[]{:S(2)}) collective-permute-start(bf16[64,1152]{1,0:T(8,128)(2,1)S(1)} %get-tuple-element.15), channel_id=1, source_target_pairs={{0,8},{2,10},{4,12},{6,14},{8,0},{10,2},{12,4},{14,6},{1,9},{3,11}... | collective-permute-start | bytes 442376 | tf_op jit(solution)/shard_map/ppermute | solution.py:201
  109.0 1.8 %collective-permute-start.14 = (bf16[64,1152]{1,0:T(8,128)(2,1)S(1)}, bf16[64,1152]{1,0:T(8,128)(2,1)S(1)}, u32[]{:S(2)}, u32[]{:S(2)}) collective-permute-start(bf16[64,1152]{1,0:T(8,128)(2,1)S(1)} %get-tuple-element.14), channel_id=1, source_target_pairs={{0,12},{2,14},{4,8},{6,10},{8,4},{10,6},{12,0},{14,2},{1,13},{3,15... | collective-permute-start | bytes 442376 | tf_op jit(solution)/shard_map/ppermute | solution.py:201
  112.7 6.7 %collective-permute-done.13 = bf16[64,1152]{1,0:T(8,128)(2,1)S(1)} collective-permute-done((bf16[64,1152]{1,0:T(8,128)(2,1)S(1)}, bf16[64,1152]{1,0:T(8,128)(2,1)S(1)}, u32[]{:S(2)}, u32[]{:S(2)}) %collective-permute-start.13) | collective-permute-done | bytes 147488 | tf_op jit(solution)/shard_map/ppermute | solution.py:201
  (64 shorter events, 24.2 us)
Async XLA Ops:
  0.6 27.0 %copy-start = (bf16[64,1024]{1,0:T(8,128)(2,1)S(1)}, bf16[64,1024]{1,0:T(8,128)(2,1)}, u32[]{:S(2)}) copy-start(bf16[64,1024]{1,0:T(8,128)(2,1)} %param.11) | copy-start | bytes 393220
  0.6 9.8 %copy-start.5 = (bf16[64,128]{1,0:T(8,128)(2,1)S(1)}, bf16[64,128]{1,0:T(8,128)(2,1)}, u32[]{:S(2)}) copy-start(bf16[64,128]{1,0:T(8,128)(2,1)} %param.8) | copy-start | bytes 49156
  3.6 13.8 %collective-permute-start = (bf16[64,1152]{1,0:T(8,128)(2,1)S(1)}, bf16[64,1152]{1,0:T(8,128)(2,1)S(1)}, u32[]{:S(2)}, u32[]{:S(2)}) collective-permute-start(bf16[64,1152]{1,0:T(8,128)(2,1)S(1)} %get-tuple-element.29), channel_id=1, source_target_pairs={{0,4},{2,6},{4,0},{6,2},{8,12},{10,14},{12,8},{14,10},{1,5},{3,7},... | collective-permute-start | bytes 442376 | tf_op jit(solution)/shard_map/ppermute | solution.py:201
  6.7 14.0 %collective-permute-start.1 = (bf16[64,1152]{1,0:T(8,128)(2,1)S(1)}, bf16[64,1152]{1,0:T(8,128)(2,1)S(1)}, u32[]{:S(2)}, u32[]{:S(2)}) collective-permute-start(bf16[64,1152]{1,0:T(8,128)(2,1)S(1)} %get-tuple-element.29), channel_id=1, source_target_pairs={{0,8},{2,10},{4,12},{6,14},{8,0},{10,2},{12,4},{14,6},{1,9},{3,11}... | collective-permute-start | bytes 442376 | tf_op jit(solution)/shard_map/ppermute | solution.py:201
  9.2 11.4 %collective-permute-start.2 = (bf16[64,1152]{1,0:T(8,128)(2,1)S(1)}, bf16[64,1152]{1,0:T(8,128)(2,1)S(1)}, u32[]{:S(2)}, u32[]{:S(2)}) collective-permute-start(bf16[64,1152]{1,0:T(8,128)(2,1)S(1)} %get-tuple-element.29), channel_id=1, source_target_pairs={{0,12},{2,14},{4,8},{6,10},{8,4},{10,6},{12,0},{14,2},{1,13},{3,15... | collective-permute-start | bytes 442376 | tf_op jit(solution)/shard_map/ppermute | solution.py:201
  10.4 16.3 %collective-permute-start.5 = (bf16[64,1024]{0,1:T(8,128)(2,1)S(1)}, bf16[64,1024]{0,1:T(8,128)(2,1)S(1)}, u32[]{:S(2)}, u32[]{:S(2)}) collective-permute-start(bf16[64,1024]{0,1:T(8,128)(2,1)S(1)} %copy.29), channel_id=1, source_target_pairs={{0,1},{1,0},{2,3},{3,2},{4,5},{5,4},{6,7},{7,6},{8,9},{9,8},{10,11... | collective-permute-start | bytes 393224 | tf_op jit(solution)/shard_map/ppermute | solution.py:200
  11.2 14.6 %all-to-all-start = ((bf16[8,64,128]{2,1,0:T(8,128)(2,1)}), bf16[8,64,128]{2,1,0:T(8,128)(2,1)S(1)}, u32[]{:S(2)}, u32[]{:S(2)}) async-start(bf16[8,64,128]{2,1,0:T(8,128)(2,1)} %broadcast_in_dim.31), calls=%async_computation | async-start | bytes 262144 | tf_op jit(solution)/shard_map/all_to_all | solution.py:212
  20.7 13.9 %collective-permute-start.3 = (bf16[256,1152]{1,0:T(8,128)(2,1)S(1)}, bf16[256,1152]{1,0:T(8,128)(2,1)S(1)}, u32[]{:S(2)}, u32[]{:S(2)}) collective-permute-start(bf16[256,1152]{1,0:T(8,128)(2,1)S(1)} %pad_maximum_fusion), channel_id=1, source_target_pairs={{0,2},{2,0},{4,6},{6,4},{8,10},{10,8},{12,14},{14,12},{1,3},{3,1},... | collective-permute-start | bytes 1769480 | tf_op jit(solution)/shard_map/ppermute | solution.py:201
  25.9 1.6 %collective-permute-start.6 = (bf16[64,1024]{0,1:T(8,128)(2,1)S(1)}, bf16[64,1024]{0,1:T(8,128)(2,1)S(1)}, u32[]{:S(2)}, u32[]{:S(2)}) collective-permute-start(bf16[64,1024]{0,1:T(8,128)(2,1)S(1)} %bitcast.44), channel_id=1, source_target_pairs={{0,1},{1,0},{2,3},{3,2},{4,5},{5,4},{6,7},{7,6},{8,9},{9,8},{10,11... | collective-permute-start | bytes 393224 | tf_op jit(solution)/shard_map/ppermute | solution.py:200
  28.6 13.8 %all-to-all-start.1 = ((f32[8,64,128]{2,1,0:T(8,128)}), f32[8,64,128]{2,1,0:T(8,128)S(1)}, u32[]{:S(2)}, u32[]{:S(2)}) async-start(f32[8,64,128]{2,1,0:T(8,128)} %broadcast_in_dim.32), calls=%async_computation.1 | async-start | bytes 524288 | tf_op jit(solution)/shard_map/all_to_all | solution.py:221
  35.5 9.4 %collective-permute-start.4 = (bf16[512,1152]{1,0:T(8,128)(2,1)}, bf16[512,1152]{1,0:T(8,128)(2,1)}, u32[]{:S(2)}, u32[]{:S(2)}) collective-permute-start(bf16[512,1152]{1,0:T(8,128)(2,1)} %constant_dynamic-update-slice_fusion.2.near), channel_id=1, source_target_pairs={{0,1},{1,0},{2,3},{3,2},{4,5},{5,4},{6,7},{7,6},{8,9},{9,8},{10,11... | collective-permute-start | bytes 3538952 | tf_op jit(solution)/shard_map/ppermute | solution.py:200
  42.5 1.5 %collective-permute-start.7 = (f32[8,64,128]{2,1,0:T(8,128)S(1)}, f32[8,64,128]{2,1,0:T(8,128)S(1)}, u32[]{:S(2)}, u32[]{:S(2)}) collective-permute-start(f32[8,64,128]{2,1,0:T(8,128)S(1)} %all-to-all-done.1), channel_id=1, source_target_pairs={{0,1},{1,0},{2,3},{3,2},{4,5},{5,4},{6,7},{7,6},{8,9},{9,8},{10,11... | collective-permute-start | bytes 786440 | tf_op jit(solution)/shard_map/ppermute | solution.py:200
  63.7 4.4 %copy-start.2 = (f32[1024,128]{1,0:T(8,128)S(1)}, f32[1024,128]{1,0:T(8,128)}, u32[]{:S(2)}) copy-start(f32[1024,128]{1,0:T(8,128)} %get-tuple-element.11) | copy-start | bytes 1572868
  67.9 16.3 %collective-permute-start.10 = (bf16[512,1152]{1,0:T(8,128)(2,1)}, bf16[512,1152]{1,0:T(8,128)(2,1)}, u32[]{:S(2)}, u32[]{:S(2)}) collective-permute-start(bf16[512,1152]{1,0:T(8,128)(2,1)} %shard_map.96), channel_id=1, source_target_pairs={{0,1},{1,0},{2,3},{3,2},{4,5},{5,4},{6,7},{7,6},{8,9},{9,8},{10,11... | collective-permute-start | bytes 3538952 | tf_op jit(solution)/shard_map/ppermute | solution.py:200
  68.1 3.0 %collective-permute-start.8 = (f32[8,64,128]{2,1,0:T(8,128)S(1)}, f32[8,64,128]{2,1,0:T(8,128)S(1)}, u32[]{:S(2)}, u32[]{:S(2)}) collective-permute-start(f32[8,64,128]{2,1,0:T(8,128)S(1)} %dynamic-slice_bitcast_fusion), channel_id=1, source_target_pairs={{0,1},{1,0},{2,3},{3,2},{4,5},{5,4},{6,7},{7,6},{8,9},{9,8},{10,11... | collective-permute-start | bytes 786440 | tf_op jit(solution)/shard_map/ppermute | solution.py:200
  71.9 11.6 %all-to-all-start.2 = ((bf16[8,64,128]{2,1,0:T(8,128)(2,1)}), bf16[8,64,128]{2,1,0:T(8,128)(2,1)S(1)}, u32[]{:S(2)}, u32[]{:S(2)}) async-start(bf16[8,64,128]{2,1,0:T(8,128)(2,1)} %fusion.51), calls=%async_computation.2 | async-start | bytes 262144 | tf_op jit(solution)/shard_map/all_to_all | solution.py:247
  88.2 15.4 %collective-permute-start.11 = (bf16[256,1152]{1,0:T(8,128)(2,1)}, bf16[256,1152]{1,0:T(8,128)(2,1)}, u32[]{:S(2)}, u32[]{:S(2)}) collective-permute-start(bf16[256,1152]{1,0:T(8,128)(2,1)} %fusion.12), channel_id=1, source_target_pairs={{0,2},{2,0},{4,6},{6,4},{8,10},{10,8},{12,14},{14,12},{1,3},{3,1},... | collective-permute-start | bytes 1769480 | tf_op jit(solution)/shard_map/ppermute | solution.py:201
  89.3 1.9 %collective-permute-start.9 = (f32[64,1024]{1,0:T(8,128)}, f32[64,1024]{1,0:T(8,128)}, u32[]{:S(2)}, u32[]{:S(2)}) collective-permute-start(f32[64,1024]{1,0:T(8,128)} %constant_dynamic-slice_fusion), channel_id=1, source_target_pairs={{0,1},{1,0},{2,3},{3,2},{4,5},{5,4},{6,7},{7,6},{8,9},{9,8},{10,11... | collective-permute-start | bytes 786440 | tf_op jit(solution)/shard_map/ppermute | solution.py:200
  92.8 19.1 %all-to-all-start.3 = ((bf16[8,64,128]{2,1,0:T(8,128)(2,1)}), bf16[8,64,128]{2,1,0:T(8,128)(2,1)S(1)}, u32[]{:S(2)}, u32[]{:S(2)}) async-start(bf16[8,64,128]{2,1,0:T(8,128)(2,1)} %fusion.54), calls=%async_computation.3 | async-start | bytes 262144 | tf_op jit(solution)/shard_map/all_to_all | solution.py:255
  105.2 1.0 copy-start.1
  106.2 4.5 %copy-start.4 = (f32[64,128]{1,0:T(8,128)S(1)}, f32[64,128]{1,0:T(8,128)}, u32[]{:S(2)}) copy-start(f32[64,128]{1,0:T(8,128)} %copy-done.3) | copy-start | bytes 98308
  106.3 6.4 %collective-permute-start.12 = (bf16[64,1152]{1,0:T(8,128)(2,1)S(1)}, bf16[64,1152]{1,0:T(8,128)(2,1)S(1)}, u32[]{:S(2)}, u32[]{:S(2)}) collective-permute-start(bf16[64,1152]{1,0:T(8,128)(2,1)S(1)} %get-tuple-element.16), channel_id=1, source_target_pairs={{0,4},{2,6},{4,0},{6,2},{8,12},{10,14},{12,8},{14,10},{1,5},{3,7},... | collective-permute-start | bytes 442376 | tf_op jit(solution)/shard_map/ppermute | solution.py:201
  106.6 12.7 %collective-permute-start.13 = (bf16[64,1152]{1,0:T(8,128)(2,1)S(1)}, bf16[64,1152]{1,0:T(8,128)(2,1)S(1)}, u32[]{:S(2)}, u32[]{:S(2)}) collective-permute-start(bf16[64,1152]{1,0:T(8,128)(2,1)S(1)} %get-tuple-element.15), channel_id=1, source_target_pairs={{0,8},{2,10},{4,12},{6,14},{8,0},{10,2},{12,4},{14,6},{1,9},{3,11}... | collective-permute-start | bytes 442376 | tf_op jit(solution)/shard_map/ppermute | solution.py:201
  109.0 10.3 %collective-permute-start.14 = (bf16[64,1152]{1,0:T(8,128)(2,1)S(1)}, bf16[64,1152]{1,0:T(8,128)(2,1)S(1)}, u32[]{:S(2)}, u32[]{:S(2)}) collective-permute-start(bf16[64,1152]{1,0:T(8,128)(2,1)S(1)} %get-tuple-element.14), channel_id=1, source_target_pairs={{0,12},{2,14},{4,8},{6,10},{8,4},{10,6},{12,0},{14,2},{1,13},{3,15... | collective-permute-start | bytes 442376 | tf_op jit(solution)/shard_map/ppermute | solution.py:201
  (1 other events, 0.6 us)

commit v2 on v0

v2 whole, which is shorter than its diff:
```python
import functools
import math

import jax
import jax.numpy as jnp
from jax import lax
from jax.experimental import pallas as pl
from jax.experimental.pallas import tpu as pltpu
from jax.sharding import PartitionSpec as P

BF = jnp.bfloat16
F32 = jnp.float32
MIB = 1024 * 1024
KERNEL_MIB = 44


def dot(left, right, left_dim, right_dim):
    return lax.dot_general(
        left, right, (((left_dim,), (right_dim,)), ((), ())), preferred_element_type=F32
    )


def split(value):
    high = value.astype(BF)
    return high, (value - high.astype(F32)).astype(BF)


def encode(value):
    return (value * value * value).astype(BF)


def decode(code):
    cube = code.astype(F32)
    size = jnp.abs(cube)
    root = jnp.exp2(jnp.log2(jnp.maximum(size, 1e-37)) * (1.0 / 3.0))
    return jnp.where(size < 1e-37, 0.0, jnp.where(cube < 0.0, -root, root))


def stack_kernel(*refs):
    *parts, out, small = refs
    rows, width = parts[0].shape[0], out.shape[1]
    for k, part in enumerate(parts):
        out[k * rows : (k + 1) * rows, :] = part[:, :width]
        small[k * rows : (k + 1) * rows, :] = part[:, width:]


def both_kernel(core_ref, own, other, after, out):
    rows = own.shape[0]
    zero = core_ref[0] == 0
    a, b = own[...], other[...]
    out[:rows] = jnp.where(zero, a, b)
    out[rows:] = jnp.where(zero, b, a)


def fold_branch_kernel(scale_b, place_ref, w_both, branch, out, wide):
    if branch.shape == wide.shape:
        wide[...] = branch[...]
    else:
        maps, n_pts = wide.shape[0], out.shape[0]
        each = branch.shape[1] // 2
        for j in range(n_pts):
            at = pl.multiple_of(place_ref[j] * each, each)
            wide[:, pl.ds(at, each)] = branch[j * maps : (j + 1) * maps, :each]
    code = encode(dot(wide[...], w_both[...], 1, 1) * scale_b)
    for p in range(out.shape[0]):
        out[p] = code


def main_kernel(
    scale_p, core_ref, features, small, small_other, near_a, near_b, far_a, far_b,
    b_own, b_other, target,
    far, near, s_mine, s_theirs, first_out, dz_out,
    first, second, dz, w_in, w_mid, pairs, b_all, branch, near_all, far_all, in_sem, out_sem,
):
    points, hidden = first.shape
    n_pts, rows, maps = s_mine.shape
    enc = features.shape[1]
    quarter, half, step = hidden // 4, hidden // 2, points // 4
    loads = [
        pltpu.make_async_copy(part, w_mid.at[pl.ds(j * quarter, quarter), :], in_sem.at[j])
        for j, part in enumerate((near_a, near_b, far_a, far_b))
    ]
    for load in loads:
        load.start()
    core = core_ref[0]
    w_in[:half, :] = small[:, enc:]
    w_in[half:, :] = small_other[:, enc:]
    for i in range(4):
        block = slice(i * step, (i + 1) * step)
        first[block, :] = jnp.tanh(dot(features[block, :], w_in[...], 1, 1)).astype(BF)
    save_first = pltpu.make_async_copy(first, first_out, out_sem.at[0])
    save_first.start()
    few = maps // 2
    for p in range(n_pts):
        cols = slice(2 * p * rows, 2 * (p + 1) * rows)
        branch[pl.ds(core * few, few), cols] = decode(b_own[p])
        branch[pl.ds((1 - core) * few, few), cols] = decode(b_other[p])
    bh, bl = split(branch[...])
    b_pair = jnp.concatenate([bh, bl], axis=0)
    b_three = jnp.concatenate([bh, bh, bl], axis=0)
    for load in loads:
        load.wait()
    for i in range(4):
        block = slice(i * step, (i + 1) * step)
        s = jnp.tanh(dot(first[block, :], w_mid[...], 1, 0)).astype(BF)
        second[block, :] = s
        pair = dot(s, b_pair, 1, 1)
        field = pair[:, :maps] + pair[:, maps:]
        resid = (field - target[block, :].astype(F32)) * scale_p
        rh, rl = split(resid)
        pairs[block, :] = jnp.concatenate([rh, rl], axis=1)
        s32 = s.astype(F32)
        back = dot(jnp.concatenate([rh, rl, rh], axis=1), b_three, 1, 0)
        dz[block, :] = (back * (1.0 - s32 * s32)).astype(BF)
    save_dz = pltpu.make_async_copy(dz, dz_out, out_sem.at[1])
    save_dz.start()
    both = dot(second[...], pairs[...], 0, 0)
    b_all[...] = both[:, :maps] + both[:, maps:]
    for p in range(n_pts):
        at = 2 * p * rows
        s_mine[p] = b_all[pl.ds(at + core * rows, rows), :]
        s_theirs[p] = encode(b_all[pl.ds(at + (1 - core) * rows, rows), :])
    saves = [save_first, save_dz]
    for i in range(4):
        block = slice(i * quarter, (i + 1) * quarter)
        g = dot(first[:, block], dz[...], 0, 0)
        if i < 2:
            source, target_ref, part = near_all, near, block
            near_all[part, :] = g
        else:
            source, target_ref, part = far_all, far, slice((i - 2) * quarter, (i - 1) * quarter)
            far_all[part, :] = encode(g)
        saves.append(
            pltpu.make_async_copy(source.at[part, :], target_ref.at[part, :], out_sem.at[2 + i])
        )
        saves[-1].start()
    for save in saves:
        save.wait()


def send_kernel(near, got, low):
    quarter = low.shape[0]
    low[...] = encode(near[quarter:] + decode(got[quarter:]))


def keep_kernel(near, got, after, own):
    quarter = own.shape[0]
    own[...] = near[:quarter] + decode(got[:quarter])


def pack_sums_kernel(mine, got, after, out):
    out[...] = encode(mine[...] + decode(got[...]))


def sums_kernel(scale_b, core_ref, got, own, other, w_out, after, grad_out, mine, theirs):
    total = decode(got[0])
    for p in range(1, got.shape[0]):
        total += decode(got[p])
    sh, sl = split(total)
    w = w_out[...]
    zero = core_ref[0] == 0
    top, bottom = jnp.where(zero, own[...], other[...]), jnp.where(zero, other[...], own[...])
    b = jnp.concatenate([top, bottom], axis=0)
    grad_out[...] = (dot(sh, b, 1, 0) + dot(sl, b, 1, 0)) * scale_b
    part = (dot(sh, w, 0, 0) + dot(sl, w, 0, 0)) * scale_b
    half = part.shape[0] // 2
    mine[...] = jnp.where(zero, part[:half], part[half:])
    theirs[...] = encode(jnp.where(zero, part[half:], part[:half]))


def input_kernel(
    place_ref, features_in, first_in, near_a, near_b, far_a, far_b, dz_in, after, mine, theirs,
    features, grads, first, w_mid, dz, sem,
):
    points, hidden = first.shape
    quarter, half, step = hidden // 4, hidden // 2, points // 4
    weights = [
        pltpu.make_async_copy(part, w_mid.at[pl.ds(j * quarter, quarter), :], sem.at[j])
        for j, part in enumerate((near_a, near_b, far_a, far_b))
    ]
    block = lambda i: slice(i * step, (i + 1) * step)
    values = [
        [
            pltpu.make_async_copy(source.at[block(i), :], to.at[block(i), :], sem.at[4 + 2 * i + k])
            for k, (source, to) in enumerate(((dz_in, dz), (first_in, first)))
        ]
        for i in range(4)
    ]
    load_features = pltpu.make_async_copy(features_in, features, sem.at[12])
    for load in (values[0][0], weights[0], values[0][1], *weights[1:]):
        load.start()
    for load in (*values[1], *values[2], *values[3], load_features):
        load.start()
    for i in range(4):
        values[i][0].wait()
        values[i][1].wait()
        d = dz[block(i), :]
        for j in range(4):
            if i == 0:
                weights[j].wait()
            cols = slice(j * quarter, (j + 1) * quarter)
            f = first[block(i), cols].astype(F32)
            back = dot(d, w_mid[cols, :], 1, 1)
            grads[block(i), cols] = (back * (1.0 - f * f)).astype(BF)
    load_features.wait()
    g = dot(features[...], grads[...], 0, 0).T
    n_pts, rows, _ = mine.shape
    for j in range(n_pts):
        p = place_ref[j]
        mine[p] = g[j * rows : (j + 1) * rows]
        theirs[p] = encode(g[half + j * rows : half + (j + 1) * rows])


def pack_last_kernel(part, mine, got, after, out):
    enc = part.shape[2]
    out[:, :, :enc] = encode(part[...])
    out[:, :, enc:] = encode(mine[...] + decode(got[...]))


def fold_kernel(own, got, keep, *codes):
    rows = keep.shape[0]
    keep[...] = own[:rows] + decode(got[:rows])
    for k, code in enumerate(codes):
        block = slice((k + 1) * rows, (k + 2) * rows)
        code[...] = encode(own[block] + decode(got[block]))


def hold_kernel(value, after, out):
    out[...] = value[...]


def last_kernel(keep, *refs):
    *codes, grad_mid = refs
    total = keep[...]
    for code in codes:
        total += decode(code[...])
    grad_mid[...] = total


def last_small_kernel(got, grad_branch, grad_in):
    total = decode(got[0])
    for p in range(1, got.shape[0]):
        total += decode(got[p])
    enc = grad_in.shape[1]
    part = total[:, :enc]
    grad_branch[...] = part.T if grad_branch.shape != part.shape else part
    grad_in[...] = total[:, enc:]


def cost(flops, moved):
    return pl.CostEstimate(flops=int(flops), bytes_accessed=int(moved), transcendentals=0)


def call(kernel, outs, scratch, estimate, spaces, *args, mib=KERNEL_MIB):
    kinds = {"s": pltpu.SMEM, "v": pltpu.VMEM, "h": pltpu.HBM, "a": pl.ANY}
    specs = [pl.BlockSpec(memory_space=kinds[c]) for c in spaces]
    return pl.pallas_call(
        kernel,
        in_specs=specs[: len(args)],
        out_specs=specs[len(args) :],
        out_shape=[jax.ShapeDtypeStruct(shape, dtype) for shape, dtype in outs],
        scratch_shapes=scratch,
        compiler_params=pltpu.CompilerParams(vmem_limit_bytes=mib * MIB),
        cost_estimate=estimate,
    )(*args)


def per_device(features, target, branch, w_in, w_mid, w_out):
    n_pts = lax.axis_size("pts")
    core = lax.axis_index("maps")
    point = lax.axis_index("pts")
    rows, width = w_mid.shape
    hidden = rows * n_pts * 2
    quarter, half = hidden // 4, hidden // 2
    n_hi = n_pts // 2
    maps = 2 * branch.shape[0]
    points, enc = features.shape
    scale_b = 1.0 / math.sqrt(width)
    scale_p = 1.0 / math.sqrt(target.shape[1] * n_pts)
    swap_core = lambda v: lax.ppermute(v, "maps", [(0, 1), (1, 0)])
    move = lambda v, mask: lax.ppermute(v, "pts", [(i, i ^ mask) for i in range(n_pts)])
    exchange = lambda v: lax.all_to_all(v, "pts", 0, 0, tiled=True)
    pick = lambda flag, a, b: jnp.where(flag, a, b)
    first_core = core == 0
    core_ref = core.reshape(1)
    masks = [2 * k + y for y in range(2) for k in range(n_hi)]
    place = point ^ jnp.array(masks, jnp.int32)

    own = jnp.concatenate([w_mid, branch.reshape(rows, enc), w_in], axis=1)
    parts = [own] + [move(own, 2 * k) for k in range(1, n_hi)]
    line, small = call(
        stack_kernel, [((quarter, width), BF), ((quarter, 2 * enc), BF)], [], cost(1, 1e6),
        "v" * n_hi + "vv", *parts,
    )
    small = jnp.concatenate([small, move(small, 1)], axis=0)
    small_other = swap_core(small)
    other = move(line, 1)
    mid = (line, other, swap_core(line), swap_core(other))
    square = width // n_pts == enc
    unmask = point ^ jnp.arange(n_pts, dtype=jnp.int32)
    unmask = (unmask % 2) * n_hi + unmask // 2
    wide = lambda v: (
        v[:, :enc].reshape(n_pts, *branch.shape)[unmask].transpose(1, 0, 2)
    ).reshape(maps // 2, width)
    wide_own = None if square else wide(small)

    (w_both,) = call(
        both_kernel, [((2 * rows, width), BF)], [], cost(5e10, 1), "svva" + "v",
        core_ref, w_out, swap_core(w_out), line,
    )
    folded, wide_own = call(
        functools.partial(fold_branch_kernel, scale_b),
        [((n_pts, maps // 2, 2 * rows), BF), ((maps // 2, width), BF)], [],
        cost(1, 1), "svv" + "vv", place, w_both, small if square else wide_own,
    )
    b_own = exchange(folded)
    b_other = swap_core(b_own)
    wide_other = swap_core(wide_own)

    t_own = lax.dynamic_slice_in_dim(target, core * points, points, 1)
    t_other = swap_core(lax.dynamic_slice_in_dim(target, (1 - core) * points, points, 1))
    t_full = jnp.concatenate(
        [pick(first_core, t_own, t_other), pick(first_core, t_other, t_own)], axis=0
    ).T

    dma = pltpu.SemaphoreType.DMA
    far, near, s_mine, s_theirs, first, dz = call(
        functools.partial(main_kernel, scale_p),
        [((half, width), BF), ((half, width), F32), ((n_pts, rows, maps), F32)]
        + [((n_pts, rows, maps), BF), ((points, hidden), BF), ((points, width), BF)],
        [
            pltpu.VMEM((points, hidden), BF), pltpu.VMEM((points, width), BF),
            pltpu.VMEM((points, width), BF), pltpu.VMEM((hidden, enc), BF),
            pltpu.VMEM((hidden, width), BF), pltpu.VMEM((points, 2 * maps), BF),
            pltpu.VMEM((width, maps), F32), pltpu.VMEM((maps, width), F32),
            pltpu.VMEM((half, width), F32), pltpu.VMEM((half, width), BF),
            dma((4,)), dma((6,)),
        ],
        cost(5e10, 8e6), "svvvhhhhvvv" + "hhvvhh",
        core_ref, features, small, small_other, *mid, b_own, b_other, t_full,
        mib=56,
    )

    far_got = swap_core(far)
    (low,) = call(
        send_kernel, [((quarter, width), BF)], [], cost(1, 1), "vv" + "v", near, far_got
    )
    (own,) = call(
        keep_kernel, [((quarter, width), F32)], [], cost(5e10, 1e6), "vva" + "v", near, far_got, low
    )

    (s_code,) = call(
        pack_sums_kernel, [((n_pts, rows, maps), BF)], [], cost(1, 1), "vva" + "v",
        s_mine, swap_core(s_theirs), own,
    )
    in_mine, in_theirs = call(
        input_kernel, [((n_pts, rows, enc), F32), ((n_pts, rows, enc), BF)],
        [
            pltpu.VMEM((points, enc), BF), pltpu.VMEM((points, hidden), BF),
            pltpu.VMEM((points, hidden), BF), pltpu.VMEM((hidden, width), BF),
            pltpu.VMEM((points, width), BF), dma((13,)),
        ],
        cost(5e10, 8e6), "shhhhhhha" + "vv", place, features, first, *mid, dz, own,
        mib=58,
    )
    strip = (maps // 2, width)
    grad_out, p_mine, p_theirs = call(
        functools.partial(sums_kernel, scale_b), [((rows, width), F32), (strip, F32), (strip, BF)],
        [], cost(1, 1), "svvvva" + "vvv",
        core_ref, exchange(s_code), wide_own, wide_other, w_out, in_mine,
    )
    part = p_mine + decode(swap_core(p_theirs))
    part = part.reshape(maps // 2, n_pts, width // n_pts).transpose(1, 0, 2)
    part = part.reshape(n_pts, rows, enc)

    wide_row = (rows, width)
    keep, *codes = call(
        fold_kernel, [(wide_row, F32)] + [(wide_row, BF)] * (n_hi - 1), [], cost(1, 1),
        "vv" + "v" * n_hi, own, move(low, 1),
    )
    (keep,) = call(hold_kernel, [(wide_row, F32)], [], cost(5e10, 1), "va" + "v", keep, codes[0])
    (last,) = call(
        pack_last_kernel, [((n_pts, rows, 2 * enc), BF)], [], cost(1, 1), "vvva" + "v",
        part, in_mine, swap_core(in_theirs), keep,
    )
    (keep,) = call(hold_kernel, [(wide_row, F32)], [], cost(5e10, 1), "va" + "v", keep, last)
    codes = [move(code, 2 * (k + 1)) for k, code in enumerate(codes)]
    (grad_mid,) = call(
        last_kernel, [(wide_row, F32)], [], cost(1, 1), "v" * n_hi + "v", keep, *codes
    )
    grad_branch, grad_in = call(
        last_small_kernel, [((enc, rows) if square else (rows, enc), F32), ((rows, enc), F32)],
        [], cost(1, 1), "v" + "vv", exchange(last),
    )
    if not square:
        grad_branch = grad_branch.reshape(maps // 2, width // n_pts).T
    return (grad_branch, grad_in, grad_mid, grad_out)


def solution(mesh):
    in_specs = (
        P(("grp", "pts", "maps"), None),
        P("maps", ("grp", "pts")),
        P(("grp", "maps"), "pts"),
        P(("pts", "maps"), None),
        P(("pts", "maps"), None),
        P(("pts", "maps"), None),
    )
    out_specs = (
        P("pts", ("grp", "maps")),
        P(("grp", "pts", "maps"), None),
        P(("grp", "pts", "maps"), None),
        P(("grp", "pts", "maps"), None),
    )
    return jax.shard_map(
        per_device, mesh=mesh, in_specs=in_specs, out_specs=out_specs, check_vma=False
    )
```

time: 439 us -> 105 us (0.24)
  waiting for transfers between devices: 319 us -> 38.5 us
  matrix products: 52.8 us -> 0 us
  blocking collectives: 50.6 us -> 0 us
  Pallas kernels: 0 us -> 27.4 us
  starting transfers between devices: 0.5 us -> 27.7 us
  between operations: 14.2 us -> 0.92 us
  local copies, waits for them, and re-layouts: 2.19 us -> 7.74 us
    reduce_scatter x5 -> x0, waiting for transfers between devices: 259 us -> none  [the longest x1 76.7 us: per_device(): lax.psum_scatter(col_term(second, d_trunk), ('pts', 'maps'), scatter_dime...]
    all_gather x3 -> x0, waiting for transfers between devices: 57.9 us -> none  [the longest x1 37.1 us: per_device(): lax.all_gather(w_out, ('pts', 'maps'), axis=0, tiled=True)]
    dot_general x10 -> x0, matrix products: 52.8 us -> none  [the longest x6 30.7 us: contract(): lax.dot_general(left, right, (((left_dim,), (right_dim,)), ((), ())), pre...]
    all_gather x2 -> x0, blocking collectives: 50.6 us -> none  [the longest x1 26.3 us: per_device(): branch_full = lax.all_gather(branch, 'pts', axis=1, tiled=True)]
    pallas_call x0 -> x15, Pallas kernels: none -> 27.4 us  [call(): pl.pallas_call(kernel, in_specs=specs[:len(args)], out_specs=specs[len(ar...]
    ppermute x0 -> x20, waiting for transfers between devices: none -> 23.1 us  [the longest x9 19.5 us: per_device(): lax.ppermute(v, 'pts', [(i, i ^ mask) for i in range(n_pts)])]
    all_to_all x0 -> x3, waiting for transfers between devices: none -> 15.4 us  [per_device(): exchange = lambda v: lax.all_to_all(v, 'pts', 0, 0, tiled=True)]
    ppermute x0 -> x20, starting transfers between devices: none -> 14.7 us  [the longest x9 12.5 us: per_device(): lax.ppermute(v, 'pts', [(i, i ^ mask) for i in range(n_pts)])]
  transfers between devices with their start and end apart: 8 -> 23, of which waited for: 7 -> 11; matrix products, arithmetic and copies ran while one was open for 9% -> 2% of each run, Pallas kernels for 0% -> 14%
where the time goes in v2:
time: 105 us; the launch traced here: 104 us
  waiting for transfers between devices  38.5 us (37%)
  starting transfers between devices  27.7 us (26%)
  Pallas kernels  27.4 us (26%)
  local copies, waits for them, and re-layouts  7.74 us (7%)
  other arithmetic  1.7 us (2%)
    pallas_call x15, Pallas kernels, call(): pl.pallas_call(kernel, in_specs=specs[:len(args)], out_specs=specs[len(ar...  27.4 us
    ppermute x9, waiting for transfers between devices, per_device(): lax.ppermute(v, 'pts', [(i, i ^ mask) for i in range(n_pts)])  19.5 us
    all_to_all x3, waiting for transfers between devices, per_device(): exchange = lambda v: lax.all_to_all(v, 'pts', 0, 0, tiled=True)  15.4 us
    all_to_all x3, starting transfers between devices, per_device(): exchange = lambda v: lax.all_to_all(v, 'pts', 0, 0, tiled=True)  13 us
    ppermute x9, starting transfers between devices, per_device(): lax.ppermute(v, 'pts', [(i, i ^ mask) for i in range(n_pts)])  12.5 us
    unnamed x38, local copies, waits for them, and re-layouts  6.99 us
    ppermute x11, waiting for transfers between devices, per_device(): swap_core = lambda v: lax.ppermute(v, 'maps', [(0, 1), (1, 0)])  3.61 us
    ppermute x11, starting transfers between devices, per_device(): swap_core = lambda v: lax.ppermute(v, 'maps', [(0, 1), (1, 0)])  2.14 us
  transfers between devices with their start and end apart: 23, of which 11 were waited for; matrix products, arithmetic and copies ran while one was open for 2% of the time, Pallas kernels for 14%

profile of v2, /device:TPU:0, one launch (start us, length us, event | category | flops | bytes accessed | tf_op | source)
XLA Modules:
  0.0 103.9 jit_solution(132833178331165530)
XLA Ops:
  3.0 3.0 %collective-permute-start = (bf16[64,1280]{1,0:T(8,128)(2,1)S(1)}, bf16[64,1280]{1,0:T(8,128)(2,1)S(1)}, u32[]{:S(2)}, u32[]{:S(2)}) collective-permute-start(bf16[64,1280]{1,0:T(8,128)(2,1)S(1)} %constant_dynamic-update-slice_fusion.refs_0_), channel_id=1, source_target_pairs={{0,4},{2,6},{4,0},{6,2},{8,12},{10,14},{12,8},{14,10},{1,5},{3,7},... | collective-permute-start | bytes 491528 | tf_op jit(solution)/shard_map/ppermute | solution.py:281
  6.0 2.6 %collective-permute-start.1 = (bf16[64,1280]{1,0:T(8,128)(2,1)S(1)}, bf16[64,1280]{1,0:T(8,128)(2,1)S(1)}, u32[]{:S(2)}, u32[]{:S(2)}) collective-permute-start(bf16[64,1280]{1,0:T(8,128)(2,1)S(1)} %constant_dynamic-update-slice_fusion.refs_0_), channel_id=1, source_target_pairs={{0,8},{2,10},{4,12},{6,14},{8,0},{10,2},{12,4},{14,6},{1,9},{3,11}... | collective-permute-start | bytes 491528 | tf_op jit(solution)/shard_map/ppermute | solution.py:281
  9.3 3.4 %collective-permute-done.refs_1_ = bf16[64,1280]{1,0:T(8,128)(2,1)S(1)} collective-permute-done((bf16[64,1280]{1,0:T(8,128)(2,1)S(1)}, bf16[64,1280]{1,0:T(8,128)(2,1)S(1)}, u32[]{:S(2)}, u32[]{:S(2)}) %collective-permute-start) | collective-permute-done | bytes 163872 | tf_op jit(solution)/shard_map/ppermute | solution.py:281
  12.7 8.4 %collective-permute-done.1.refs_2_ = bf16[64,1280]{1,0:T(8,128)(2,1)S(1)} collective-permute-done((bf16[64,1280]{1,0:T(8,128)(2,1)S(1)}, bf16[64,1280]{1,0:T(8,128)(2,1)S(1)}, u32[]{:S(2)}, u32[]{:S(2)}) %collective-permute-start.1) | collective-permute-done | bytes 163872 | tf_op jit(solution)/shard_map/ppermute | solution.py:281
  21.1 1.6 %collective-permute-start.3 = (bf16[256,256]{1,0:T(8,128)(2,1)S(1)}, bf16[256,256]{1,0:T(8,128)(2,1)S(1)}, u32[]{:S(2)}, u32[]{:S(2)}) collective-permute-start(bf16[256,256]{1,0:T(8,128)(2,1)S(1)} %get-tuple-element.25), channel_id=1, source_target_pairs={{0,2},{2,0},{4,6},{6,4},{8,10},{10,8},{12,14},{14,12},{1,3},{3,1},... | collective-permute-start | bytes 393224 | tf_op jit(solution)/shard_map/ppermute | solution.py:281
  24.2 3.5 %collective-permute-done.3 = bf16[256,256]{1,0:T(8,128)(2,1)S(1)} collective-permute-done((bf16[256,256]{1,0:T(8,128)(2,1)S(1)}, bf16[256,256]{1,0:T(8,128)(2,1)S(1)}, u32[]{:S(2)}, u32[]{:S(2)}) %collective-permute-start.3) | collective-permute-done | bytes 131104 | tf_op jit(solution)/shard_map/ppermute | solution.py:281
  27.8 1.4 %shard_map.104 = (bf16[8,64,128]{2,1,0:T(8,128)(2,1)}, bf16[64,1024]{1,0:T(8,128)(2,1)S(1)}) custom-call(s32[8]{0:T(128)S(1)} %broadcast_xor_fusion.place_ref, bf16[128,1024]{1,0:T(8,128)(2,1)S(1)} %shard_map.103.w_both, bf16[512,256]{1,0:T(8,128)(2,1)S(1)} %constant_dynamic-update-slice_fusion.3.branch.small), custom_call_target="tpu_custom_call" | custom-call | flops 1 | bytes 1 | tf_op jit(solution)/shard_map/pallas_call | solution.py:257
  29.2 5.9 %all-to-all-start = ((bf16[8,64,128]{2,1,0:T(8,128)(2,1)}), bf16[8,64,128]{2,1,0:T(8,128)(2,1)S(1)}, u32[]{:S(2)}, u32[]{:S(2)}) async-start(bf16[8,64,128]{2,1,0:T(8,128)(2,1)} %get-tuple-element.27), calls=%async_computation | async-start | bytes 262144 | tf_op jit(solution)/shard_map/all_to_all | solution.py:282
  36.4 6.3 %all-to-all-done.b_own = bf16[8,64,128]{2,1,0:T(8,128)(2,1)S(1)} async-done(((bf16[8,64,128]{2,1,0:T(8,128)(2,1)}), bf16[8,64,128]{2,1,0:T(8,128)(2,1)S(1)}, u32[]{:S(2)}, u32[]{:S(2)}) %all-to-all-start) | async-done | bytes 131104 | tf_op jit(solution)/shard_map/all_to_all | solution.py:282
  44.7 12.3 %shard_map.105 = (bf16[512,1024]{1,0:T(8,128)(2,1)}, f32[512,1024]{1,0:T(8,128)}, f32[8,64,128]{2,1,0:T(8,128)}, bf16[8,64,128]{2,1,0:T(8,128)(2,1)}, bf16[1024,...) custom-call(s32[1]{0:T(128)} %bitcast.core_ref, bf16[1024,128]{1,0:T(8,128)(2,1)} %features_in.1, ...), custom_call_target="tpu_custom_call" | custom-call | flops 49999998976 | bytes 8000000 | tf_op jit(solution)/shard_map/pallas_call | solution.py:257
  57.8 2.2 %collective-permute-done.12.got = bf16[512,1024]{1,0:T(8,128)(2,1)S(1)} collective-permute-done((bf16[512,1024]{1,0:T(8,128)(2,1)}, bf16[512,1024]{1,0:T(8,128)(2,1)S(1)}, u32[]{:S(2)}, u32[]{:S(2)}) %collective-permute-start.12) | collective-permute-done | bytes 1048608 | tf_op jit(solution)/shard_map/ppermute | solution.py:280
  60.0 1.6 %copy-done.2 = f32[512,1024]{1,0:T(8,128)S(1)} copy-done((f32[512,1024]{1,0:T(8,128)S(1)}, f32[512,1024]{1,0:T(8,128)}, u32[]{:S(2)}) %copy-start.2) | copy-done | bytes 2097176
  63.8 3.6 %all-to-all-start.1 = ((bf16[8,64,128]{2,1,0:T(8,128)(2,1)}), bf16[8,64,128]{2,1,0:T(8,128)(2,1)S(1)}, u32[]{:S(2)}, u32[]{:S(2)}) async-start(bf16[8,64,128]{2,1,0:T(8,128)(2,1)} %shard_map.108), calls=%async_computation.1 | async-start | bytes 262144 | tf_op jit(solution)/shard_map/all_to_all | solution.py:282
  67.4 7.6 %shard_map.109 = (f32[8,64,128]{2,1,0:T(8,128)}, bf16[8,64,128]{2,1,0:T(8,128)(2,1)}) custom-call(s32[8]{0:T(128)} %copy-done.9, bf16[1024,128]{1,0:T(8,128)(2,1)} %features_in.1, bf16[1024,1024]{1,0:T(8,128)(2,1)} %get-tuple-element.33.first_in, bf16[256,1024]{1,0:T(8,128)(2,1)} %copy-done.10, bf16[256,1024]{1,0:T(8,128)(2,1)} %copy-done.13, ...), custom_call_target="tpu_custom_call" | custom-call | flops 49999998976 | bytes 8000000 | tf_op jit(solution)/shard_map/pallas_call | solution.py:257
  75.0 2.5 %all-to-all-done.1.got = bf16[8,64,128]{2,1,0:T(8,128)(2,1)S(1)} async-done(((bf16[8,64,128]{2,1,0:T(8,128)(2,1)}), bf16[8,64,128]{2,1,0:T(8,128)(2,1)S(1)}, u32[]{:S(2)}, u32[]{:S(2)}) %all-to-all-start.1) | async-done | bytes 131104 | tf_op jit(solution)/shard_map/all_to_all | solution.py:282
  77.6 0.9 copy-done.3
  78.5 1.0 shard_map.110
  80.0 1.0 collective-permute-done.14
  81.8 2.0 %collective-permute-start.18 = (bf16[64,1024]{1,0:T(8,128)(2,1)S(1)}, bf16[64,1024]{1,0:T(8,128)(2,1)S(1)}, u32[]{:S(2)}, u32[]{:S(2)}) collective-permute-start(bf16[64,1024]{1,0:T(8,128)(2,1)S(1)} %get-tuple-element.43), channel_id=1, source_target_pairs={{0,8},{2,10},{4,12},{6,14},{8,0},{10,2},{12,4},{14,6},{1,9},{3,11}... | collective-permute-start | bytes 393224 | tf_op jit(solution)/shard_map/ppermute | solution.py:281
  83.8 2.4 %collective-permute-start.19 = (bf16[64,1024]{1,0:T(8,128)(2,1)S(1)}, bf16[64,1024]{1,0:T(8,128)(2,1)S(1)}, u32[]{:S(2)}, u32[]{:S(2)}) collective-permute-start(bf16[64,1024]{1,0:T(8,128)(2,1)S(1)} %get-tuple-element.44), channel_id=1, source_target_pairs={{0,12},{2,14},{4,8},{6,10},{8,4},{10,6},{12,0},{14,2},{1,13},{3,15... | collective-permute-start | bytes 393224 | tf_op jit(solution)/shard_map/ppermute | solution.py:281
  87.1 3.6 %all-to-all-start.2 = ((bf16[8,64,256]{2,1,0:T(8,128)(2,1)}), bf16[8,64,256]{2,1,0:T(8,128)(2,1)S(1)}, u32[]{:S(2)}, u32[]{:S(2)}) async-start(bf16[8,64,256]{2,1,0:T(8,128)(2,1)} %shard_map.113.after), calls=%async_computation.2 | async-start | bytes 524288 | tf_op jit(solution)/shard_map/all_to_all | solution.py:282
  90.7 4.1 %collective-permute-done.18.refs_1_ = bf16[64,1024]{1,0:T(8,128)(2,1)S(1)} collective-permute-done((bf16[64,1024]{1,0:T(8,128)(2,1)S(1)}, bf16[64,1024]{1,0:T(8,128)(2,1)S(1)}, u32[]{:S(2)}, u32[]{:S(2)}) %collective-permute-start.18) | collective-permute-done | bytes 131104 | tf_op jit(solution)/shard_map/ppermute | solution.py:281
  94.8 1.0 shard_map.116
  95.8 6.6 %all-to-all-done.2.got = bf16[8,64,256]{2,1,0:T(8,128)(2,1)S(1)} async-done(((bf16[8,64,256]{2,1,0:T(8,128)(2,1)}), bf16[8,64,256]{2,1,0:T(8,128)(2,1)S(1)}, u32[]{:S(2)}, u32[]{:S(2)}) %all-to-all-start.2) | async-done | bytes 262176 | tf_op jit(solution)/shard_map/all_to_all | solution.py:282
  (82 shorter events, 14.5 us)
Async XLA Ops:
  3.0 9.7 %collective-permute-start = (bf16[64,1280]{1,0:T(8,128)(2,1)S(1)}, bf16[64,1280]{1,0:T(8,128)(2,1)S(1)}, u32[]{:S(2)}, u32[]{:S(2)}) collective-permute-start(bf16[64,1280]{1,0:T(8,128)(2,1)S(1)} %constant_dynamic-update-slice_fusion.refs_0_), channel_id=1, source_target_pairs={{0,4},{2,6},{4,0},{6,2},{8,12},{10,14},{12,8},{14,10},{1,5},{3,7},... | collective-permute-start | bytes 491528 | tf_op jit(solution)/shard_map/ppermute | solution.py:281
  6.0 15.0 %collective-permute-start.1 = (bf16[64,1280]{1,0:T(8,128)(2,1)S(1)}, bf16[64,1280]{1,0:T(8,128)(2,1)S(1)}, u32[]{:S(2)}, u32[]{:S(2)}) collective-permute-start(bf16[64,1280]{1,0:T(8,128)(2,1)S(1)} %constant_dynamic-update-slice_fusion.refs_0_), channel_id=1, source_target_pairs={{0,8},{2,10},{4,12},{6,14},{8,0},{10,2},{12,4},{14,6},{1,9},{3,11}... | collective-permute-start | bytes 491528 | tf_op jit(solution)/shard_map/ppermute | solution.py:281
  8.6 12.5 %collective-permute-start.2 = (bf16[64,1280]{1,0:T(8,128)(2,1)S(1)}, bf16[64,1280]{1,0:T(8,128)(2,1)S(1)}, u32[]{:S(2)}, u32[]{:S(2)}) collective-permute-start(bf16[64,1280]{1,0:T(8,128)(2,1)S(1)} %constant_dynamic-update-slice_fusion.refs_0_), channel_id=1, source_target_pairs={{0,12},{2,14},{4,8},{6,10},{8,4},{10,6},{12,0},{14,2},{1,13},{3,15... | collective-permute-start | bytes 491528 | tf_op jit(solution)/shard_map/ppermute | solution.py:281
  8.6 14.6 %collective-permute-start.8 = (bf16[64,1024]{1,0:T(8,128)(2,1)}, bf16[64,1024]{1,0:T(8,128)(2,1)S(1)}, u32[]{:S(2)}, u32[]{:S(2)}) collective-permute-start(bf16[64,1024]{1,0:T(8,128)(2,1)} %w_out.1), channel_id=1, source_target_pairs={{0,1},{1,0},{2,3},{3,2},{4,5},{5,4},{6,7},{7,6},{8,9},{9,8},{10,11... | collective-permute-start | bytes 393224 | tf_op jit(solution)/shard_map/ppermute | solution.py:280
  9.3 18.5 %copy-start.9 = (s32[8]{0:T(128)}, s32[8]{0:T(128)S(1)}, u32[]{:S(2)}) copy-start(s32[8]{0:T(128)S(1)} %broadcast_xor_fusion.place_ref) | copy-start | bytes 100
  21.1 6.5 %collective-permute-start.3 = (bf16[256,256]{1,0:T(8,128)(2,1)S(1)}, bf16[256,256]{1,0:T(8,128)(2,1)S(1)}, u32[]{:S(2)}, u32[]{:S(2)}) collective-permute-start(bf16[256,256]{1,0:T(8,128)(2,1)S(1)} %get-tuple-element.25), channel_id=1, source_target_pairs={{0,2},{2,0},{4,6},{6,4},{8,10},{10,8},{12,14},{14,12},{1,3},{3,1},... | collective-permute-start | bytes 393224 | tf_op jit(solution)/shard_map/ppermute | solution.py:281
  22.7 12.5 %collective-permute-start.5 = (bf16[256,1024]{1,0:T(8,128)(2,1)S(1)}, bf16[256,1024]{1,0:T(8,128)(2,1)S(1)}, u32[]{:S(2)}, u32[]{:S(2)}) collective-permute-start(bf16[256,1024]{1,0:T(8,128)(2,1)S(1)} %get-tuple-element.26.after.near_a), channel_id=1, source_target_pairs={{0,2},{2,0},{4,6},{6,4},{8,10},{10,8},{12,14},{14,12},{1,3},{3,1},... | collective-permute-start | bytes 1572872 | tf_op jit(solution)/shard_map/ppermute | solution.py:281
  27.7 16.4 %collective-permute-start.6 = (bf16[256,1024]{1,0:T(8,128)(2,1)S(1)}, bf16[256,1024]{1,0:T(8,128)(2,1)}, u32[]{:S(2)}, u32[]{:S(2)}) collective-permute-start(bf16[256,1024]{1,0:T(8,128)(2,1)S(1)} %get-tuple-element.26.after.near_a), channel_id=1, source_target_pairs={{0,1},{1,0},{2,3},{3,2},{4,5},{5,4},{6,7},{7,6},{8,9},{9,8},{10,11... | collective-permute-start | bytes 1572872 | tf_op jit(solution)/shard_map/ppermute | solution.py:280
  29.2 13.5 %all-to-all-start = ((bf16[8,64,128]{2,1,0:T(8,128)(2,1)}), bf16[8,64,128]{2,1,0:T(8,128)(2,1)S(1)}, u32[]{:S(2)}, u32[]{:S(2)}) async-start(bf16[8,64,128]{2,1,0:T(8,128)(2,1)} %get-tuple-element.27), calls=%async_computation | async-start | bytes 262144 | tf_op jit(solution)/shard_map/all_to_all | solution.py:282
  35.2 8.9 %collective-permute-start.7 = (bf16[256,1024]{1,0:T(8,128)(2,1)S(1)}, bf16[256,1024]{1,0:T(8,128)(2,1)}, u32[]{:S(2)}, u32[]{:S(2)}) collective-permute-start(bf16[256,1024]{1,0:T(8,128)(2,1)S(1)} %collective-permute-done.5.near_b), channel_id=1, source_target_pairs={{0,1},{1,0},{2,3},{3,2},{4,5},{5,4},{6,7},{7,6},{8,9},{9,8},{10,11... | collective-permute-start | bytes 1572872 | tf_op jit(solution)/shard_map/ppermute | solution.py:280
  35.6 7.2 %collective-permute-start.10 = (bf16[64,1024]{0,1:T(8,128)(2,1)S(1)}, bf16[64,1024]{0,1:T(8,128)(2,1)S(1)}, u32[]{:S(2)}, u32[]{:S(2)}) collective-permute-start(bf16[64,1024]{0,1:T(8,128)(2,1)S(1)} %copy.19), channel_id=1, source_target_pairs={{0,1},{1,0},{2,3},{3,2},{4,5},{5,4},{6,7},{7,6},{8,9},{9,8},{10,11... | collective-permute-start | bytes 393224 | tf_op jit(solution)/shard_map/ppermute | solution.py:280
  36.2 7.5 %collective-permute-start.4 = (bf16[512,256]{1,0:T(8,128)(2,1)S(1)}, bf16[512,256]{1,0:T(8,128)(2,1)S(1)}, u32[]{:S(2)}, u32[]{:S(2)}) collective-permute-start(bf16[512,256]{1,0:T(8,128)(2,1)S(1)} %constant_dynamic-update-slice_fusion.3.branch.small), channel_id=1, source_target_pairs={{0,1},{1,0},{2,3},{3,2},{4,5},{5,4},{6,7},{7,6},{8,9},{9,8},{10,11... | collective-permute-start | bytes 786440 | tf_op jit(solution)/shard_map/ppermute | solution.py:280
  42.7 1.3 %collective-permute-start.9 = (bf16[8,64,128]{2,1,0:T(8,128)(2,1)S(1)}, bf16[8,64,128]{2,1,0:T(8,128)(2,1)S(1)}, u32[]{:S(2)}, u32[]{:S(2)}) collective-permute-start(bf16[8,64,128]{2,1,0:T(8,128)(2,1)S(1)} %all-to-all-done.b_own), channel_id=1, source_target_pairs={{0,1},{1,0},{2,3},{3,2},{4,5},{5,4},{6,7},{7,6},{8,9},{9,8},{10,11... | collective-permute-start | bytes 393224 | tf_op jit(solution)/shard_map/ppermute | solution.py:280
  57.0 2.9 %collective-permute-start.12 = (bf16[512,1024]{1,0:T(8,128)(2,1)}, bf16[512,1024]{1,0:T(8,128)(2,1)S(1)}, u32[]{:S(2)}, u32[]{:S(2)}) collective-permute-start(bf16[512,1024]{1,0:T(8,128)(2,1)} %get-tuple-element.31), channel_id=1, source_target_pairs={{0,1},{1,0},{2,3},{3,2},{4,5},{5,4},{6,7},{7,6},{8,9},{9,8},{10,11... | collective-permute-start | bytes 3145736 | tf_op jit(solution)/shard_map/ppermute | solution.py:280
  57.3 17.8 %collective-permute-start.13 = (bf16[64,1024]{1,0:T(8,128)(2,1)S(1)}, bf16[64,1024]{1,0:T(8,128)(2,1)S(1)}, u32[]{:S(2)}, u32[]{:S(2)}) collective-permute-start(bf16[64,1024]{1,0:T(8,128)(2,1)S(1)} %get-tuple-element.32.own), channel_id=1, source_target_pairs={{0,1},{1,0},{2,3},{3,2},{4,5},{5,4},{6,7},{7,6},{8,9},{9,8},{10,11... | collective-permute-start | bytes 393224 | tf_op jit(solution)/shard_map/ppermute | solution.py:280
  57.6 5.2 %collective-permute-start.11 = (bf16[8,64,128]{2,1,0:T(8,128)(2,1)}, bf16[8,64,128]{2,1,0:T(8,128)(2,1)S(1)}, u32[]{:S(2)}, u32[]{:S(2)}) collective-permute-start(bf16[8,64,128]{2,1,0:T(8,128)(2,1)} %get-tuple-element.29), channel_id=1, source_target_pairs={{0,1},{1,0},{2,3},{3,2},{4,5},{5,4},{6,7},{7,6},{8,9},{9,8},{10,11... | collective-permute-start | bytes 393224 | tf_op jit(solution)/shard_map/ppermute | solution.py:280
  62.1 19.1 %collective-permute-start.16 = (bf16[256,1024]{1,0:T(8,128)(2,1)S(1)}, bf16[256,1024]{1,0:T(8,128)(2,1)S(1)}, u32[]{:S(2)}, u32[]{:S(2)}) collective-permute-start(bf16[256,1024]{1,0:T(8,128)(2,1)S(1)} %shard_map.106.after), channel_id=1, source_target_pairs={{0,2},{2,0},{4,6},{6,4},{8,10},{10,8},{12,14},{14,12},{1,3},{3,1},... | collective-permute-start | bytes 1572872 | tf_op jit(solution)/shard_map/ppermute | solution.py:281
  63.8 13.7 %all-to-all-start.1 = ((bf16[8,64,128]{2,1,0:T(8,128)(2,1)}), bf16[8,64,128]{2,1,0:T(8,128)(2,1)S(1)}, u32[]{:S(2)}, u32[]{:S(2)}) async-start(bf16[8,64,128]{2,1,0:T(8,128)(2,1)} %shard_map.108), calls=%async_computation.1 | async-start | bytes 262144 | tf_op jit(solution)/shard_map/all_to_all | solution.py:282
  79.5 1.5 %collective-permute-start.14 = (bf16[64,1024]{1,0:T(8,128)(2,1)S(1)}, bf16[64,1024]{1,0:T(8,128)(2,1)S(1)}, u32[]{:S(2)}, u32[]{:S(2)}) collective-permute-start(bf16[64,1024]{1,0:T(8,128)(2,1)S(1)} %get-tuple-element.37), channel_id=1, source_target_pairs={{0,1},{1,0},{2,3},{3,2},{4,5},{5,4},{6,7},{7,6},{8,9},{9,8},{10,11... | collective-permute-start | bytes 393224 | tf_op jit(solution)/shard_map/ppermute | solution.py:280
  79.5 6.7 %collective-permute-start.15 = (bf16[8,64,128]{2,1,0:T(8,128)(2,1)}, bf16[8,64,128]{2,1,0:T(8,128)(2,1)S(1)}, u32[]{:S(2)}, u32[]{:S(2)}) collective-permute-start(bf16[8,64,128]{2,1,0:T(8,128)(2,1)} %get-tuple-element.38), channel_id=1, source_target_pairs={{0,1},{1,0},{2,3},{3,2},{4,5},{5,4},{6,7},{7,6},{8,9},{9,8},{10,11... | collective-permute-start | bytes 393224 | tf_op jit(solution)/shard_map/ppermute | solution.py:280
  81.7 9.0 %collective-permute-start.17 = (bf16[64,1024]{1,0:T(8,128)(2,1)S(1)}, bf16[64,1024]{1,0:T(8,128)(2,1)S(1)}, u32[]{:S(2)}, u32[]{:S(2)}) collective-permute-start(bf16[64,1024]{1,0:T(8,128)(2,1)S(1)} %get-tuple-element.40.after), channel_id=1, source_target_pairs={{0,4},{2,6},{4,0},{6,2},{8,12},{10,14},{12,8},{14,10},{1,5},{3,7},... | collective-permute-start | bytes 393224 | tf_op jit(solution)/shard_map/ppermute | solution.py:281
  81.8 13.0 %collective-permute-start.18 = (bf16[64,1024]{1,0:T(8,128)(2,1)S(1)}, bf16[64,1024]{1,0:T(8,128)(2,1)S(1)}, u32[]{:S(2)}, u32[]{:S(2)}) collective-permute-start(bf16[64,1024]{1,0:T(8,128)(2,1)S(1)} %get-tuple-element.43), channel_id=1, source_target_pairs={{0,8},{2,10},{4,12},{6,14},{8,0},{10,2},{12,4},{14,6},{1,9},{3,11}... | collective-permute-start | bytes 393224 | tf_op jit(solution)/shard_map/ppermute | solution.py:281
  83.8 11.0 %collective-permute-start.19 = (bf16[64,1024]{1,0:T(8,128)(2,1)S(1)}, bf16[64,1024]{1,0:T(8,128)(2,1)S(1)}, u32[]{:S(2)}, u32[]{:S(2)}) collective-permute-start(bf16[64,1024]{1,0:T(8,128)(2,1)S(1)} %get-tuple-element.44), channel_id=1, source_target_pairs={{0,12},{2,14},{4,8},{6,10},{8,4},{10,6},{12,0},{14,2},{1,13},{3,15... | collective-permute-start | bytes 393224 | tf_op jit(solution)/shard_map/ppermute | solution.py:281
  87.1 15.3 %all-to-all-start.2 = ((bf16[8,64,256]{2,1,0:T(8,128)(2,1)}), bf16[8,64,256]{2,1,0:T(8,128)(2,1)S(1)}, u32[]{:S(2)}, u32[]{:S(2)}) async-start(bf16[8,64,256]{2,1,0:T(8,128)(2,1)} %shard_map.113.after), calls=%async_computation.2 | async-start | bytes 524288 | tf_op jit(solution)/shard_map/all_to_all | solution.py:282
  (15 other events, 75.6 us)

commit v3 on v2

--- a/solution.py
+++ b/solution.py
@@ -11,7 +11,7 @@
 BF = jnp.bfloat16
 F32 = jnp.float32
 MIB = 1024 * 1024
-KERNEL_MIB = 44
+KERNEL_MIB = 12
 
 
 def dot(left, right, left_dim, right_dim):
@@ -34,6 +34,13 @@
     size = jnp.abs(cube)
     root = jnp.exp2(jnp.log2(jnp.maximum(size, 1e-37)) * (1.0 / 3.0))
     return jnp.where(size < 1e-37, 0.0, jnp.where(cube < 0.0, -root, root))
+
+
+def beside_kernel(w_mid, branch, w_in, out):
+    width, enc = w_mid.shape[1], w_in.shape[1]
+    out[:, :width] = w_mid[...]
+    out[:, width : width + enc] = branch[...]
+    out[:, width + enc :] = w_in[...]
 
 
 def stack_kernel(*refs):
@@ -70,7 +77,7 @@
     scale_p, core_ref, features, small, small_other, near_a, near_b, far_a, far_b,
     b_own, b_other, target,
     far, near, s_mine, s_theirs, first_out, dz_out,
-    first, second, dz, w_in, w_mid, pairs, b_all, branch, near_all, far_all, in_sem, out_sem,
+    first, second, dz, w_in, w_mid, pairs, b_all, branch, far_all, in_sem, out_sem,
 ):
     points, hidden = first.shape
     n_pts, rows, maps = s_mine.shape
@@ -125,13 +132,12 @@
         block = slice(i * quarter, (i + 1) * quarter)
         g = dot(first[:, block], dz[...], 0, 0)
         if i < 2:
-            source, target_ref, part = near_all, near, block
-            near_all[part, :] = g
-        else:
-            source, target_ref, part = far_all, far, slice((i - 2) * quarter, (i - 1) * quarter)
-            far_all[part, :] = encode(g)
+            near[block, :] = g
+            continue
+        part = slice((i - 2) * quarter, (i - 1) * quarter)
+        far_all[part, :] = encode(g)
         saves.append(
-            pltpu.make_async_copy(source.at[part, :], target_ref.at[part, :], out_sem.at[2 + i])
+            pltpu.make_async_copy(far_all.at[part, :], far.at[part, :], out_sem.at[i])
         )
         saves[-1].start()
     for save in saves:
@@ -242,8 +248,7 @@
     for p in range(1, got.shape[0]):
         total += decode(got[p])
     enc = grad_in.shape[1]
-    part = total[:, :enc]
-    grad_branch[...] = part.T if grad_branch.shape != part.shape else part
+    grad_branch[...] = total[:, :enc]
     grad_in[...] = total[:, enc:]
 
 
@@ -286,7 +291,10 @@
     masks = [2 * k + y for y in range(2) for k in range(n_hi)]
     place = point ^ jnp.array(masks, jnp.int32)
 
-    own = jnp.concatenate([w_mid, branch.reshape(rows, enc), w_in], axis=1)
+    (own,) = call(
+        beside_kernel, [((rows, width + 2 * enc), BF)], [], cost(1, 1), "vvv" + "v",
+        w_mid, branch.reshape(rows, enc), w_in,
+    )
     parts = [own] + [move(own, 2 * k) for k in range(1, n_hi)]
     line, small = call(
         stack_kernel, [((quarter, width), BF), ((quarter, 2 * enc), BF)], [], cost(1, 1e6),
@@ -333,12 +341,11 @@
             pltpu.VMEM((points, width), BF), pltpu.VMEM((hidden, enc), BF),
             pltpu.VMEM((hidden, width), BF), pltpu.VMEM((points, 2 * maps), BF),
             pltpu.VMEM((width, maps), F32), pltpu.VMEM((maps, width), F32),
-            pltpu.VMEM((half, width), F32), pltpu.VMEM((half, width), BF),
-            dma((4,)), dma((6,)),
+            pltpu.VMEM((half, width), BF), dma((4,)), dma((4,)),
         ],
-        cost(5e10, 8e6), "svvvhhhhvvv" + "hhvvhh",
+        cost(5e10, 8e6), "svvvhhhhvvv" + "hvvvhh",
         core_ref, features, small, small_other, *mid, b_own, b_other, t_full,
-        mib=56,
+        mib=44,
     )
 
     far_got = swap_core(far)
@@ -389,11 +396,10 @@
         last_kernel, [(wide_row, F32)], [], cost(1, 1), "v" * n_hi + "v", keep, *codes
     )
     grad_branch, grad_in = call(
-        last_small_kernel, [((enc, rows) if square else (rows, enc), F32), ((rows, enc), F32)],
+        last_small_kernel, [((rows, enc), F32), ((rows, enc), F32)],
         [], cost(1, 1), "v" + "vv", exchange(last),
     )
-    if not square:
-        grad_branch = grad_branch.reshape(maps // 2, width // n_pts).T
+    grad_branch = grad_branch.reshape(maps // 2, width // n_pts).T
     return (grad_branch, grad_in, grad_mid, grad_out)
 
 

time: 105 us -> 98.8 us (0.941)
  Pallas kernels: 27.4 us -> 24.7 us
  local copies, waits for them, and re-layouts: 7.74 us -> 5.29 us
  waiting for transfers between devices: 38.5 us -> 36.5 us
  starting transfers between devices: 27.7 us -> 28.8 us
    pallas_call x15 -> x16, Pallas kernels: 27.4 us -> 24.7 us  [call(): pl.pallas_call(kernel, in_specs=specs[:len(args)], out_specs=specs[len(ar...]
    unnamed x38 -> x37, local copies, waits for them, and re-layouts: 6.99 us -> 5.26 us
  transfers between devices with their start and end apart: 23 -> 23, of which waited for: 11 -> 11; matrix products, arithmetic and copies ran while one was open for 2% -> 3% of each run, Pallas kernels for 14% -> 15%
where the time goes in v3:
time: 98.8 us; the launch traced here: 98.2 us
  waiting for transfers between devices  36.5 us (37%)
  starting transfers between devices  28.8 us (29%)
  Pallas kernels  24.7 us (25%)
  local copies, waits for them, and re-layouts  5.29 us (5%)
  other arithmetic  1.93 us (2%)
    pallas_call x16, Pallas kernels, call(): pl.pallas_call(kernel, in_specs=specs[:len(args)], out_specs=specs[len(ar...  24.7 us
    ppermute x9, waiting for transfers between devices, per_device(): lax.ppermute(v, 'pts', [(i, i ^ mask) for i in range(n_pts)])  19.1 us
    all_to_all x3, waiting for transfers between devices, per_device(): exchange = lambda v: lax.all_to_all(v, 'pts', 0, 0, tiled=True)  14.5 us
    all_to_all x3, starting transfers between devices, per_device(): exchange = lambda v: lax.all_to_all(v, 'pts', 0, 0, tiled=True)  14 us
    ppermute x9, starting transfers between devices, per_device(): lax.ppermute(v, 'pts', [(i, i ^ mask) for i in range(n_pts)])  12.6 us
    unnamed x37, local copies, waits for them, and re-layouts  5.26 us
    ppermute x11, waiting for transfers between devices, per_device(): swap_core = lambda v: lax.ppermute(v, 'maps', [(0, 1), (1, 0)])  2.99 us
    ppermute x11, starting transfers between devices, per_device(): swap_core = lambda v: lax.ppermute(v, 'maps', [(0, 1), (1, 0)])  2.23 us
  transfers between devices with their start and end apart: 23, of which 11 were waited for; matrix products, arithmetic and copies ran while one was open for 3% of the time, Pallas kernels for 15%

profile of v3, /device:TPU:0, one launch (start us, length us, event | category | flops | bytes accessed | tf_op | source)
XLA Modules:
  0.0 98.2 jit_solution(16984532211031536027)
XLA Ops:
  3.0 3.1 %collective-permute-start = (bf16[64,1280]{1,0:T(8,128)(2,1)S(1)}, bf16[64,1280]{1,0:T(8,128)(2,1)S(1)}, u32[]{:S(2)}, u32[]{:S(2)}) collective-permute-start(bf16[64,1280]{1,0:T(8,128)(2,1)S(1)} %shard_map.102.refs_0_), channel_id=1, source_target_pairs={{0,4},{2,6},{4,0},{6,2},{8,12},{10,14},{12,8},{14,10},{1,5},{3,7},... | collective-permute-start | bytes 491528 | tf_op jit(solution)/shard_map/ppermute | solution.py:286
  6.1 2.6 %collective-permute-start.1 = (bf16[64,1280]{1,0:T(8,128)(2,1)S(1)}, bf16[64,1280]{1,0:T(8,128)(2,1)S(1)}, u32[]{:S(2)}, u32[]{:S(2)}) collective-permute-start(bf16[64,1280]{1,0:T(8,128)(2,1)S(1)} %shard_map.102.refs_0_), channel_id=1, source_target_pairs={{0,8},{2,10},{4,12},{6,14},{8,0},{10,2},{12,4},{14,6},{1,9},{3,11}... | collective-permute-start | bytes 491528 | tf_op jit(solution)/shard_map/ppermute | solution.py:286
  9.3 3.4 %collective-permute-done.refs_1_ = bf16[64,1280]{1,0:T(8,128)(2,1)S(1)} collective-permute-done((bf16[64,1280]{1,0:T(8,128)(2,1)S(1)}, bf16[64,1280]{1,0:T(8,128)(2,1)S(1)}, u32[]{:S(2)}, u32[]{:S(2)}) %collective-permute-start) | collective-permute-done | bytes 163872 | tf_op jit(solution)/shard_map/ppermute | solution.py:286
  12.8 8.4 %collective-permute-done.1.refs_2_ = bf16[64,1280]{1,0:T(8,128)(2,1)S(1)} collective-permute-done((bf16[64,1280]{1,0:T(8,128)(2,1)S(1)}, bf16[64,1280]{1,0:T(8,128)(2,1)S(1)}, u32[]{:S(2)}, u32[]{:S(2)}) %collective-permute-start.1) | collective-permute-done | bytes 163872 | tf_op jit(solution)/shard_map/ppermute | solution.py:286
  21.2 1.6 %collective-permute-start.3 = (bf16[256,256]{1,0:T(8,128)(2,1)S(1)}, bf16[256,256]{1,0:T(8,128)(2,1)S(1)}, u32[]{:S(2)}, u32[]{:S(2)}) collective-permute-start(bf16[256,256]{1,0:T(8,128)(2,1)S(1)} %get-tuple-element.25), channel_id=1, source_target_pairs={{0,2},{2,0},{4,6},{6,4},{8,10},{10,8},{12,14},{14,12},{1,3},{3,1},... | collective-permute-start | bytes 393224 | tf_op jit(solution)/shard_map/ppermute | solution.py:286
  24.2 3.4 %collective-permute-done.3 = bf16[256,256]{1,0:T(8,128)(2,1)S(1)} collective-permute-done((bf16[256,256]{1,0:T(8,128)(2,1)S(1)}, bf16[256,256]{1,0:T(8,128)(2,1)S(1)}, u32[]{:S(2)}, u32[]{:S(2)}) %collective-permute-start.3) | collective-permute-done | bytes 131104 | tf_op jit(solution)/shard_map/ppermute | solution.py:286
  27.8 1.4 %shard_map.105 = (bf16[8,64,128]{2,1,0:T(8,128)(2,1)}, bf16[64,1024]{1,0:T(8,128)(2,1)S(1)}) custom-call(s32[8]{0:T(128)S(1)} %broadcast_xor_fusion.place_ref, bf16[128,1024]{1,0:T(8,128)(2,1)S(1)} %shard_map.104.w_both, bf16[512,256]{1,0:T(8,128)(2,1)S(1)} %constant_dynamic-update-slice_fusion.branch.small), custom_call_target="tpu_custom_call" | custom-call | flops 1 | bytes 1 | tf_op jit(solution)/shard_map/pallas_call | solution.py:262
  29.2 5.9 %all-to-all-start = ((bf16[8,64,128]{2,1,0:T(8,128)(2,1)}), bf16[8,64,128]{2,1,0:T(8,128)(2,1)S(1)}, u32[]{:S(2)}, u32[]{:S(2)}) async-start(bf16[8,64,128]{2,1,0:T(8,128)(2,1)} %get-tuple-element.27), calls=%async_computation | async-start | bytes 262144 | tf_op jit(solution)/shard_map/all_to_all | solution.py:287
  37.0 5.7 %all-to-all-done.b_own = bf16[8,64,128]{2,1,0:T(8,128)(2,1)S(1)} async-done(((bf16[8,64,128]{2,1,0:T(8,128)(2,1)}), bf16[8,64,128]{2,1,0:T(8,128)(2,1)S(1)}, u32[]{:S(2)}, u32[]{:S(2)}) %all-to-all-start) | async-done | bytes 131104 | tf_op jit(solution)/shard_map/all_to_all | solution.py:287
  42.8 1.0 %broadcast_select_fusion.1 = (bf16[64,1024]{0,1:T(8,128)(2,1)S(1)}, bf16[64,1024]{0,1:T(8,128)(2,1)S(1)}) fusion(bf16[64,1024]{0,1:T(8,128)(2,1)S(1)} %copy.16, bf16[64,1024]{0,1:T(8,128)(2,1)} %collective-permute-done.10, pred[]{:T(512)S(6)} %eq.3), kind=kLoop, calls=%fused_computation.14 | loop fusion | flops 131072 | bytes 524289 | tf_op jit(solution)/shard_map/jit(_where)/select_n | solution.py:288
  44.1 9.4 %shard_map.106 = (bf16[512,1024]{1,0:T(8,128)(2,1)S(1)}, f32[512,1024]{1,0:T(8,128)S(1)}, f32[8,64,128]{2,1,0:T(8,128)S(1)}, bf16[8,64,128]{2,1,0:T(8,128)(2,1)S...) custom-call(s32[1]{0:T(128)} %bitcast.core_ref, bf16[1024,128]{1,0:T(8,128)(2,1)S(1)} %copy-done.14, ...), custom_call_target="tpu_custom_call" | custom-call | flops 49999998976 | bytes 8000000 | tf_op jit(solution)/shard_map/pallas_call | solution.py:262
  54.6 1.8 %collective-permute-done.12.got = bf16[512,1024]{1,0:T(8,128)(2,1)S(1)} collective-permute-done((bf16[512,1024]{1,0:T(8,128)(2,1)S(1)}, bf16[512,1024]{1,0:T(8,128)(2,1)S(1)}, u32[]{:S(2)}, u32[]{:S(2)}) %collective-permute-start.12) | collective-permute-done | bytes 1048608 | tf_op jit(solution)/shard_map/ppermute | solution.py:285
  58.6 4.2 %all-to-all-start.1 = ((bf16[8,64,128]{2,1,0:T(8,128)(2,1)}), bf16[8,64,128]{2,1,0:T(8,128)(2,1)S(1)}, u32[]{:S(2)}, u32[]{:S(2)}) async-start(bf16[8,64,128]{2,1,0:T(8,128)(2,1)} %shard_map.109), calls=%async_computation.1 | async-start | bytes 262144 | tf_op jit(solution)/shard_map/all_to_all | solution.py:287
  62.8 7.6 %shard_map.110 = (f32[8,64,128]{2,1,0:T(8,128)}, bf16[8,64,128]{2,1,0:T(8,128)(2,1)}) custom-call(s32[8]{0:T(128)} %copy-done.9, bf16[1024,128]{1,0:T(8,128)(2,1)} %features_in.1, bf16[1024,1024]{1,0:T(8,128)(2,1)} %copy-done.15, bf16[256,1024]{1,0:T(8,128)(2,1)} %copy-done.10, bf16[256,1024]{1,0:T(8,128)(2,1)} %copy-done.11, bf16[256,1024]{1,0:T(8,128)(2,1)} %copy-done.12, ...), custom_call_target="tpu_custom_call" | custom-call | flops 49999998976 | bytes 8000000 | tf_op jit(solution)/shard_map/pallas_call | solution.py:262
  70.4 2.1 %all-to-all-done.1.got = bf16[8,64,128]{2,1,0:T(8,128)(2,1)S(1)} async-done(((bf16[8,64,128]{2,1,0:T(8,128)(2,1)}), bf16[8,64,128]{2,1,0:T(8,128)(2,1)S(1)}, u32[]{:S(2)}, u32[]{:S(2)}) %all-to-all-start.1) | async-done | bytes 131104 | tf_op jit(solution)/shard_map/all_to_all | solution.py:287
  72.5 0.9 copy-done.2
  73.5 1.0 %shard_map.111 = (f32[64,1024]{1,0:T(8,128)}, f32[64,1024]{1,0:T(8,128)S(1)}, bf16[64,1024]{1,0:T(8,128)(2,1)S(1)}) custom-call(s32[1]{0:T(128)} %bitcast.core_ref, bf16[8,64,128]{2,1,0:T(8,128)(2,1)S(1)} %all-to-all-done.1.got, bf16[64,1024]{1,0:T(8,128)(2,1)S(1)} %get-tuple-element.32.own, bf16[64,1024]{1,0:T(8,128)(2,1)S(1)} %collective-permute-done.13.other, ...), custom_call_target="tpu_custom_call" | custom-call | flops 1 | bytes 1 | tf_op jit(solution)/shard_map/pallas_call | solution.py:262
  75.0 1.0 %collective-permute-done.14 = bf16[64,1024]{1,0:T(8,128)(2,1)S(1)} collective-permute-done((bf16[64,1024]{1,0:T(8,128)(2,1)S(1)}, bf16[64,1024]{1,0:T(8,128)(2,1)S(1)}, u32[]{:S(2)}, u32[]{:S(2)}) %collective-permute-start.14) | collective-permute-done | bytes 131104 | tf_op jit(solution)/shard_map/ppermute | solution.py:285
  76.8 2.4 %collective-permute-start.18 = (bf16[64,1024]{1,0:T(8,128)(2,1)S(1)}, bf16[64,1024]{1,0:T(8,128)(2,1)S(1)}, u32[]{:S(2)}, u32[]{:S(2)}) collective-permute-start(bf16[64,1024]{1,0:T(8,128)(2,1)S(1)} %get-tuple-element.43), channel_id=1, source_target_pairs={{0,8},{2,10},{4,12},{6,14},{8,0},{10,2},{12,4},{14,6},{1,9},{3,11}... | collective-permute-start | bytes 393224 | tf_op jit(solution)/shard_map/ppermute | solution.py:286
  79.2 2.0 %collective-permute-start.19 = (bf16[64,1024]{1,0:T(8,128)(2,1)S(1)}, bf16[64,1024]{1,0:T(8,128)(2,1)S(1)}, u32[]{:S(2)}, u32[]{:S(2)}) collective-permute-start(bf16[64,1024]{1,0:T(8,128)(2,1)S(1)} %get-tuple-element.44), channel_id=1, source_target_pairs={{0,12},{2,14},{4,8},{6,10},{8,4},{10,6},{12,0},{14,2},{1,13},{3,15... | collective-permute-start | bytes 393224 | tf_op jit(solution)/shard_map/ppermute | solution.py:286
  82.1 4.0 %all-to-all-start.2 = ((bf16[8,64,256]{2,1,0:T(8,128)(2,1)}), bf16[8,64,256]{2,1,0:T(8,128)(2,1)S(1)}, u32[]{:S(2)}, u32[]{:S(2)}) async-start(bf16[8,64,256]{2,1,0:T(8,128)(2,1)} %shard_map.114.after), calls=%async_computation.2 | async-start | bytes 524288 | tf_op jit(solution)/shard_map/all_to_all | solution.py:287
  86.1 3.7 %collective-permute-done.18.refs_1_ = bf16[64,1024]{1,0:T(8,128)(2,1)S(1)} collective-permute-done((bf16[64,1024]{1,0:T(8,128)(2,1)S(1)}, bf16[64,1024]{1,0:T(8,128)(2,1)S(1)}, u32[]{:S(2)}, u32[]{:S(2)}) %collective-permute-start.18) | collective-permute-done | bytes 131104 | tf_op jit(solution)/shard_map/ppermute | solution.py:286
  89.7 1.0 %shard_map.117 = f32[64,1024]{1,0:T(8,128)} custom-call(f32[64,1024]{1,0:T(8,128)S(1)} %shard_map.116.keep, bf16[64,1024]{1,0:T(8,128)(2,1)S(1)} %collective-permute-done.17.refs_0_, bf16[64,1024]{1,0:T(8,128)(2,1)S(1)} %collective-permute-done.18.refs_1_, bf16[64,1024]{1,0:T(8,128)(2,1)S(1)} %collective-permute-done.19.refs_2_), custom_call_target="tpu_custom_call" | custom-call | flops 1 | bytes 1 | tf_op jit(solution)/shard_map/pallas_call | solution.py:262
  90.8 6.6 %all-to-all-done.2.got = bf16[8,64,256]{2,1,0:T(8,128)(2,1)S(1)} async-done(((bf16[8,64,256]{2,1,0:T(8,128)(2,1)}), bf16[8,64,256]{2,1,0:T(8,128)(2,1)S(1)}, u32[]{:S(2)}, u32[]{:S(2)}) %all-to-all-start.2) | async-done | bytes 262176 | tf_op jit(solution)/shard_map/all_to_all | solution.py:287
  (81 shorter events, 12.9 us)
Async XLA Ops:
  3.0 9.8 %collective-permute-start = (bf16[64,1280]{1,0:T(8,128)(2,1)S(1)}, bf16[64,1280]{1,0:T(8,128)(2,1)S(1)}, u32[]{:S(2)}, u32[]{:S(2)}) collective-permute-start(bf16[64,1280]{1,0:T(8,128)(2,1)S(1)} %shard_map.102.refs_0_), channel_id=1, source_target_pairs={{0,4},{2,6},{4,0},{6,2},{8,12},{10,14},{12,8},{14,10},{1,5},{3,7},... | collective-permute-start | bytes 491528 | tf_op jit(solution)/shard_map/ppermute | solution.py:286
  6.1 15.0 %collective-permute-start.1 = (bf16[64,1280]{1,0:T(8,128)(2,1)S(1)}, bf16[64,1280]{1,0:T(8,128)(2,1)S(1)}, u32[]{:S(2)}, u32[]{:S(2)}) collective-permute-start(bf16[64,1280]{1,0:T(8,128)(2,1)S(1)} %shard_map.102.refs_0_), channel_id=1, source_target_pairs={{0,8},{2,10},{4,12},{6,14},{8,0},{10,2},{12,4},{14,6},{1,9},{3,11}... | collective-permute-start | bytes 491528 | tf_op jit(solution)/shard_map/ppermute | solution.py:286
  8.7 12.5 %collective-permute-start.2 = (bf16[64,1280]{1,0:T(8,128)(2,1)S(1)}, bf16[64,1280]{1,0:T(8,128)(2,1)S(1)}, u32[]{:S(2)}, u32[]{:S(2)}) collective-permute-start(bf16[64,1280]{1,0:T(8,128)(2,1)S(1)} %shard_map.102.refs_0_), channel_id=1, source_target_pairs={{0,12},{2,14},{4,8},{6,10},{8,4},{10,6},{12,0},{14,2},{1,13},{3,15... | collective-permute-start | bytes 491528 | tf_op jit(solution)/shard_map/ppermute | solution.py:286
  8.7 14.6 %collective-permute-start.8 = (bf16[64,1024]{1,0:T(8,128)(2,1)}, bf16[64,1024]{1,0:T(8,128)(2,1)S(1)}, u32[]{:S(2)}, u32[]{:S(2)}) collective-permute-start(bf16[64,1024]{1,0:T(8,128)(2,1)} %w_out.1), channel_id=1, source_target_pairs={{0,1},{1,0},{2,3},{3,2},{4,5},{5,4},{6,7},{7,6},{8,9},{9,8},{10,11... | collective-permute-start | bytes 393224 | tf_op jit(solution)/shard_map/ppermute | solution.py:285
  21.2 22.9 %copy-start.10 = (bf16[256,1024]{1,0:T(8,128)(2,1)}, bf16[256,1024]{1,0:T(8,128)(2,1)S(1)}, u32[]{:S(2)}) copy-start(bf16[256,1024]{1,0:T(8,128)(2,1)S(1)} %get-tuple-element.26.after.near_a) | copy-start | bytes 1572868
  21.2 6.5 %collective-permute-start.3 = (bf16[256,256]{1,0:T(8,128)(2,1)S(1)}, bf16[256,256]{1,0:T(8,128)(2,1)S(1)}, u32[]{:S(2)}, u32[]{:S(2)}) collective-permute-start(bf16[256,256]{1,0:T(8,128)(2,1)S(1)} %get-tuple-element.25), channel_id=1, source_target_pairs={{0,2},{2,0},{4,6},{6,4},{8,10},{10,8},{12,14},{14,12},{1,3},{3,1},... | collective-permute-start | bytes 393224 | tf_op jit(solution)/shard_map/ppermute | solution.py:286
  22.8 12.5 %collective-permute-start.5 = (bf16[256,1024]{1,0:T(8,128)(2,1)S(1)}, bf16[256,1024]{1,0:T(8,128)(2,1)S(1)}, u32[]{:S(2)}, u32[]{:S(2)}) collective-permute-start(bf16[256,1024]{1,0:T(8,128)(2,1)S(1)} %get-tuple-element.26.after.near_a), channel_id=1, source_target_pairs={{0,2},{2,0},{4,6},{6,4},{8,10},{10,8},{12,14},{14,12},{1,3},{3,1},... | collective-permute-start | bytes 1572872 | tf_op jit(solution)/shard_map/ppermute | solution.py:286
  27.7 16.4 %collective-permute-start.6 = (bf16[256,1024]{1,0:T(8,128)(2,1)S(1)}, bf16[256,1024]{1,0:T(8,128)(2,1)S(1)}, u32[]{:S(2)}, u32[]{:S(2)}) collective-permute-start(bf16[256,1024]{1,0:T(8,128)(2,1)S(1)} %get-tuple-element.26.after.near_a), channel_id=1, source_target_pairs={{0,1},{1,0},{2,3},{3,2},{4,5},{5,4},{6,7},{7,6},{8,9},{9,8},{10,11... | collective-permute-start | bytes 1572872 | tf_op jit(solution)/shard_map/ppermute | solution.py:285
  29.2 13.5 %all-to-all-start = ((bf16[8,64,128]{2,1,0:T(8,128)(2,1)}), bf16[8,64,128]{2,1,0:T(8,128)(2,1)S(1)}, u32[]{:S(2)}, u32[]{:S(2)}) async-start(bf16[8,64,128]{2,1,0:T(8,128)(2,1)} %get-tuple-element.27), calls=%async_computation | async-start | bytes 262144 | tf_op jit(solution)/shard_map/all_to_all | solution.py:287
  35.3 8.8 %collective-permute-start.7 = (bf16[256,1024]{1,0:T(8,128)(2,1)S(1)}, bf16[256,1024]{1,0:T(8,128)(2,1)S(1)}, u32[]{:S(2)}, u32[]{:S(2)}) collective-permute-start(bf16[256,1024]{1,0:T(8,128)(2,1)S(1)} %collective-permute-done.5.near_b), channel_id=1, source_target_pairs={{0,1},{1,0},{2,3},{3,2},{4,5},{5,4},{6,7},{7,6},{8,9},{9,8},{10,11... | collective-permute-start | bytes 1572872 | tf_op jit(solution)/shard_map/ppermute | solution.py:285
  36.3 6.5 %collective-permute-start.10 = (bf16[64,1024]{0,1:T(8,128)(2,1)}, bf16[64,1024]{0,1:T(8,128)(2,1)}, u32[]{:S(2)}, u32[]{:S(2)}) collective-permute-start(bf16[64,1024]{0,1:T(8,128)(2,1)} %copy.17), channel_id=1, source_target_pairs={{0,1},{1,0},{2,3},{3,2},{4,5},{5,4},{6,7},{7,6},{8,9},{9,8},{10,11... | collective-permute-start | bytes 393224 | tf_op jit(solution)/shard_map/ppermute | solution.py:285
  36.8 7.1 %collective-permute-start.4 = (bf16[512,256]{1,0:T(8,128)(2,1)S(1)}, bf16[512,256]{1,0:T(8,128)(2,1)S(1)}, u32[]{:S(2)}, u32[]{:S(2)}) collective-permute-start(bf16[512,256]{1,0:T(8,128)(2,1)S(1)} %constant_dynamic-update-slice_fusion.branch.small), channel_id=1, source_target_pairs={{0,1},{1,0},{2,3},{3,2},{4,5},{5,4},{6,7},{7,6},{8,9},{9,8},{10,11... | collective-permute-start | bytes 786440 | tf_op jit(solution)/shard_map/ppermute | solution.py:285
  42.7 1.3 %collective-permute-start.9 = (bf16[8,64,128]{2,1,0:T(8,128)(2,1)S(1)}, bf16[8,64,128]{2,1,0:T(8,128)(2,1)S(1)}, u32[]{:S(2)}, u32[]{:S(2)}) collective-permute-start(bf16[8,64,128]{2,1,0:T(8,128)(2,1)S(1)} %all-to-all-done.b_own), channel_id=1, source_target_pairs={{0,1},{1,0},{2,3},{3,2},{4,5},{5,4},{6,7},{7,6},{8,9},{9,8},{10,11... | collective-permute-start | bytes 393224 | tf_op jit(solution)/shard_map/ppermute | solution.py:285
  53.6 2.7 %collective-permute-start.12 = (bf16[512,1024]{1,0:T(8,128)(2,1)S(1)}, bf16[512,1024]{1,0:T(8,128)(2,1)S(1)}, u32[]{:S(2)}, u32[]{:S(2)}) collective-permute-start(bf16[512,1024]{1,0:T(8,128)(2,1)S(1)} %get-tuple-element.31), channel_id=1, source_target_pairs={{0,1},{1,0},{2,3},{3,2},{4,5},{5,4},{6,7},{7,6},{8,9},{9,8},{10,11... | collective-permute-start | bytes 3145736 | tf_op jit(solution)/shard_map/ppermute | solution.py:285
  54.0 16.3 %collective-permute-start.13 = (bf16[64,1024]{1,0:T(8,128)(2,1)S(1)}, bf16[64,1024]{1,0:T(8,128)(2,1)S(1)}, u32[]{:S(2)}, u32[]{:S(2)}) collective-permute-start(bf16[64,1024]{1,0:T(8,128)(2,1)S(1)} %get-tuple-element.32.own), channel_id=1, source_target_pairs={{0,1},{1,0},{2,3},{3,2},{4,5},{5,4},{6,7},{7,6},{8,9},{9,8},{10,11... | collective-permute-start | bytes 393224 | tf_op jit(solution)/shard_map/ppermute | solution.py:285
  54.2 3.4 %collective-permute-start.11 = (bf16[8,64,128]{2,1,0:T(8,128)(2,1)S(1)}, bf16[8,64,128]{2,1,0:T(8,128)(2,1)S(1)}, u32[]{:S(2)}, u32[]{:S(2)}) collective-permute-start(bf16[8,64,128]{2,1,0:T(8,128)(2,1)S(1)} %get-tuple-element.29), channel_id=1, source_target_pairs={{0,1},{1,0},{2,3},{3,2},{4,5},{5,4},{6,7},{7,6},{8,9},{9,8},{10,11... | collective-permute-start | bytes 393224 | tf_op jit(solution)/shard_map/ppermute | solution.py:285
  56.9 19.3 %collective-permute-start.16 = (bf16[256,1024]{1,0:T(8,128)(2,1)S(1)}, bf16[256,1024]{1,0:T(8,128)(2,1)S(1)}, u32[]{:S(2)}, u32[]{:S(2)}) collective-permute-start(bf16[256,1024]{1,0:T(8,128)(2,1)S(1)} %shard_map.107.after), channel_id=1, source_target_pairs={{0,2},{2,0},{4,6},{6,4},{8,10},{10,8},{12,14},{14,12},{1,3},{3,1},... | collective-permute-start | bytes 1572872 | tf_op jit(solution)/shard_map/ppermute | solution.py:286
  58.6 14.0 %all-to-all-start.1 = ((bf16[8,64,128]{2,1,0:T(8,128)(2,1)}), bf16[8,64,128]{2,1,0:T(8,128)(2,1)S(1)}, u32[]{:S(2)}, u32[]{:S(2)}) async-start(bf16[8,64,128]{2,1,0:T(8,128)(2,1)} %shard_map.109), calls=%async_computation.1 | async-start | bytes 262144 | tf_op jit(solution)/shard_map/all_to_all | solution.py:287
  74.5 1.5 %collective-permute-start.14 = (bf16[64,1024]{1,0:T(8,128)(2,1)S(1)}, bf16[64,1024]{1,0:T(8,128)(2,1)S(1)}, u32[]{:S(2)}, u32[]{:S(2)}) collective-permute-start(bf16[64,1024]{1,0:T(8,128)(2,1)S(1)} %get-tuple-element.37), channel_id=1, source_target_pairs={{0,1},{1,0},{2,3},{3,2},{4,5},{5,4},{6,7},{7,6},{8,9},{9,8},{10,11... | collective-permute-start | bytes 393224 | tf_op jit(solution)/shard_map/ppermute | solution.py:285
  74.5 6.7 %collective-permute-start.15 = (bf16[8,64,128]{2,1,0:T(8,128)(2,1)}, bf16[8,64,128]{2,1,0:T(8,128)(2,1)S(1)}, u32[]{:S(2)}, u32[]{:S(2)}) collective-permute-start(bf16[8,64,128]{2,1,0:T(8,128)(2,1)} %get-tuple-element.38), channel_id=1, source_target_pairs={{0,1},{1,0},{2,3},{3,2},{4,5},{5,4},{6,7},{7,6},{8,9},{9,8},{10,11... | collective-permute-start | bytes 393224 | tf_op jit(solution)/shard_map/ppermute | solution.py:285
  76.7 9.4 %collective-permute-start.17 = (bf16[64,1024]{1,0:T(8,128)(2,1)S(1)}, bf16[64,1024]{1,0:T(8,128)(2,1)S(1)}, u32[]{:S(2)}, u32[]{:S(2)}) collective-permute-start(bf16[64,1024]{1,0:T(8,128)(2,1)S(1)} %get-tuple-element.40.after), channel_id=1, source_target_pairs={{0,4},{2,6},{4,0},{6,2},{8,12},{10,14},{12,8},{14,10},{1,5},{3,7},... | collective-permute-start | bytes 393224 | tf_op jit(solution)/shard_map/ppermute | solution.py:286
  76.8 13.0 %collective-permute-start.18 = (bf16[64,1024]{1,0:T(8,128)(2,1)S(1)}, bf16[64,1024]{1,0:T(8,128)(2,1)S(1)}, u32[]{:S(2)}, u32[]{:S(2)}) collective-permute-start(bf16[64,1024]{1,0:T(8,128)(2,1)S(1)} %get-tuple-element.43), channel_id=1, source_target_pairs={{0,8},{2,10},{4,12},{6,14},{8,0},{10,2},{12,4},{14,6},{1,9},{3,11}... | collective-permute-start | bytes 393224 | tf_op jit(solution)/shard_map/ppermute | solution.py:286
  79.2 10.6 %collective-permute-start.19 = (bf16[64,1024]{1,0:T(8,128)(2,1)S(1)}, bf16[64,1024]{1,0:T(8,128)(2,1)S(1)}, u32[]{:S(2)}, u32[]{:S(2)}) collective-permute-start(bf16[64,1024]{1,0:T(8,128)(2,1)S(1)} %get-tuple-element.44), channel_id=1, source_target_pairs={{0,12},{2,14},{4,8},{6,10},{8,4},{10,6},{12,0},{14,2},{1,13},{3,15... | collective-permute-start | bytes 393224 | tf_op jit(solution)/shard_map/ppermute | solution.py:286
  82.1 15.3 %all-to-all-start.2 = ((bf16[8,64,256]{2,1,0:T(8,128)(2,1)}), bf16[8,64,256]{2,1,0:T(8,128)(2,1)S(1)}, u32[]{:S(2)}, u32[]{:S(2)}) async-start(bf16[8,64,256]{2,1,0:T(8,128)(2,1)} %shard_map.114.after), calls=%async_computation.2 | async-start | bytes 524288 | tf_op jit(solution)/shard_map/all_to_all | solution.py:287
  (16 other events, 120.2 us)

commit v4 on v3

--- a/solution.py
+++ b/solution.py
@@ -36,19 +36,25 @@
     return jnp.where(size < 1e-37, 0.0, jnp.where(cube < 0.0, -root, root))
 
 
-def beside_kernel(w_mid, branch, w_in, out):
-    width, enc = w_mid.shape[1], w_in.shape[1]
-    out[:, :width] = w_mid[...]
-    out[:, width : width + enc] = branch[...]
-    out[:, width + enc :] = w_in[...]
+def beside_kernel(*refs):
+    *parts, out = refs
+    at = 0
+    for part in parts:
+        out[:, at : at + part.shape[1]] = part[...]
+        at += part.shape[1]
 
 
 def stack_kernel(*refs):
-    *parts, out, small = refs
-    rows, width = parts[0].shape[0], out.shape[1]
+    *parts, out = refs
+    rows = parts[0].shape[0]
     for k, part in enumerate(parts):
-        out[k * rows : (k + 1) * rows, :] = part[:, :width]
-        small[k * rows : (k + 1) * rows, :] = part[:, width:]
+        out[k * rows : (k + 1) * rows, :] = part[...]
+
+
+def pair_kernel(own, got, out):
+    rows = own.shape[0]
+    out[:rows] = own[...]
+    out[rows:] = got[...]
 
 
 def both_kernel(core_ref, own, other, after, out):
@@ -59,44 +65,50 @@
     out[rows:] = jnp.where(zero, b, a)
 
 
-def fold_branch_kernel(scale_b, place_ref, w_both, branch, out, wide):
-    if branch.shape == wide.shape:
-        wide[...] = branch[...]
+def fold_branch_kernel(scale_b, place_ref, w_both, *refs):
+    *pairs, out, wide = refs
+    if pairs[0].shape == wide.shape:
+        wide[...] = pairs[0][...]
     else:
-        maps, n_pts = wide.shape[0], out.shape[0]
-        each = branch.shape[1] // 2
-        for j in range(n_pts):
-            at = pl.multiple_of(place_ref[j] * each, each)
-            wide[:, pl.ds(at, each)] = branch[j * maps : (j + 1) * maps, :each]
+        maps = wide.shape[0]
+        for k, pair in enumerate(pairs):
+            each = pair.shape[1]
+            for y in range(2):
+                at = pl.multiple_of(place_ref[y * len(pairs) + k] * each, each)
+                wide[:, pl.ds(at, each)] = pair[y * maps : (y + 1) * maps]
     code = encode(dot(wide[...], w_both[...], 1, 1) * scale_b)
     for p in range(out.shape[0]):
         out[p] = code
 
 
 def main_kernel(
-    scale_p, core_ref, features, small, small_other, near_a, near_b, far_a, far_b,
+    scale_p, core_ref, features, near_a, near_b, far_a, far_b,
     b_own, b_other, target,
-    far, near, s_mine, s_theirs, first_out, dz_out,
+    far, near, s_mine, s_theirs, dz_out,
     first, second, dz, w_in, w_mid, pairs, b_all, branch, far_all, in_sem, out_sem,
 ):
     points, hidden = first.shape
     n_pts, rows, maps = s_mine.shape
     enc = features.shape[1]
     quarter, half, step = hidden // 4, hidden // 2, points // 4
-    loads = [
-        pltpu.make_async_copy(part, w_mid.at[pl.ds(j * quarter, quarter), :], in_sem.at[j])
-        for j, part in enumerate((near_a, near_b, far_a, far_b))
-    ]
-    for load in loads:
+    width = w_mid.shape[1]
+    loads, loads_in = [], []
+    for j, part in enumerate((near_a, near_b, far_a, far_b)):
+        to = pl.ds(j * quarter, quarter)
+        loads_in.append(
+            pltpu.make_async_copy(part.at[:, pl.ds(width, enc)], w_in.at[to, :], in_sem.at[4 + j])
+        )
+        loads.append(
+            pltpu.make_async_copy(part.at[:, pl.ds(0, width)], w_mid.at[to, :], in_sem.at[j])
+        )
+    for load in loads_in + loads:
         load.start()
     core = core_ref[0]
-    w_in[:half, :] = small[:, enc:]
-    w_in[half:, :] = small_other[:, enc:]
+    for load in loads_in:
+        load.wait()
     for i in range(4):
         block = slice(i * step, (i + 1) * step)
         first[block, :] = jnp.tanh(dot(features[block, :], w_in[...], 1, 1)).astype(BF)
-    save_first = pltpu.make_async_copy(first, first_out, out_sem.at[0])
-    save_first.start()
     few = maps // 2
     for p in range(n_pts):
         cols = slice(2 * p * rows, 2 * (p + 1) * rows)
@@ -127,7 +139,7 @@
         at = 2 * p * rows
         s_mine[p] = b_all[pl.ds(at + core * rows, rows), :]
         s_theirs[p] = encode(b_all[pl.ds(at + (1 - core) * rows, rows), :])
-    saves = [save_first, save_dz]
+    saves = [save_dz]
     for i in range(4):
         block = slice(i * quarter, (i + 1) * quarter)
         g = dot(first[:, block], dz[...], 0, 0)
@@ -175,41 +187,47 @@
 
 
 def input_kernel(
-    place_ref, features_in, first_in, near_a, near_b, far_a, far_b, dz_in, after, mine, theirs,
-    features, grads, first, w_mid, dz, sem,
+    place_ref, features_in, near_a, near_b, far_a, far_b, dz_in, after, mine, theirs, done,
+    features, grads, w_in, w_mid, dz, sem,
 ):
-    points, hidden = first.shape
+    points, hidden = grads.shape
+    width, enc = dz.shape[1], features.shape[1]
     quarter, half, step = hidden // 4, hidden // 2, points // 4
-    weights = [
-        pltpu.make_async_copy(part, w_mid.at[pl.ds(j * quarter, quarter), :], sem.at[j])
-        for j, part in enumerate((near_a, near_b, far_a, far_b))
+    block = lambda i: slice(i * step, (i + 1) * step)
+    load_features = pltpu.make_async_copy(features_in, features, sem.at[12])
+    load_features.start()
+    parts = (near_a, near_b, far_a, far_b)
+    to = lambda j: pl.ds(j * quarter, quarter)
+    small = [
+        pltpu.make_async_copy(part.at[:, pl.ds(width, enc)], w_in.at[to(j), :], sem.at[4 + j])
+        for j, part in enumerate(parts)
     ]
-    block = lambda i: slice(i * step, (i + 1) * step)
+    large = [
+        pltpu.make_async_copy(part.at[:, pl.ds(0, width)], w_mid.at[to(j), :], sem.at[j])
+        for j, part in enumerate(parts)
+    ]
     values = [
-        [
-            pltpu.make_async_copy(source.at[block(i), :], to.at[block(i), :], sem.at[4 + 2 * i + k])
-            for k, (source, to) in enumerate(((dz_in, dz), (first_in, first)))
-        ]
+        pltpu.make_async_copy(dz_in.at[block(i), :], dz.at[block(i), :], sem.at[8 + i])
         for i in range(4)
     ]
-    load_features = pltpu.make_async_copy(features_in, features, sem.at[12])
-    for load in (values[0][0], weights[0], values[0][1], *weights[1:]):
+    for load in (*small, values[0], *large, *values[1:]):
         load.start()
-    for load in (*values[1], *values[2], *values[3], load_features):
-        load.start()
+    load_features.wait()
+    for load in small:
+        load.wait()
     for i in range(4):
-        values[i][0].wait()
-        values[i][1].wait()
+        f = jnp.tanh(dot(features[block(i), :], w_in[...], 1, 1)).astype(BF).astype(F32)
+        slope = 1.0 - f * f
+        values[i].wait()
         d = dz[block(i), :]
         for j in range(4):
             if i == 0:
-                weights[j].wait()
+                large[j].wait()
             cols = slice(j * quarter, (j + 1) * quarter)
-            f = first[block(i), cols].astype(F32)
             back = dot(d, w_mid[cols, :], 1, 1)
-            grads[block(i), cols] = (back * (1.0 - f * f)).astype(BF)
-    load_features.wait()
+            grads[block(i), cols] = (back * slope[:, cols]).astype(BF)
     g = dot(features[...], grads[...], 0, 0).T
+    done[...] = g[: done.shape[0]]
     n_pts, rows, _ = mine.shape
     for j in range(n_pts):
         p = place_ref[j]
@@ -291,35 +309,37 @@
     masks = [2 * k + y for y in range(2) for k in range(n_hi)]
     place = point ^ jnp.array(masks, jnp.int32)
 
+    branch_own = branch.reshape(rows, enc)
+    (pair,) = call(
+        pair_kernel, [((2 * rows, enc), BF)], [], cost(1, 1), "vv" + "v",
+        branch_own, move(branch_own, 1),
+    )
+
     (own,) = call(
-        beside_kernel, [((rows, width + 2 * enc), BF)], [], cost(1, 1), "vvv" + "v",
-        w_mid, branch.reshape(rows, enc), w_in,
-    )
-    parts = [own] + [move(own, 2 * k) for k in range(1, n_hi)]
-    line, small = call(
-        stack_kernel, [((quarter, width), BF), ((quarter, 2 * enc), BF)], [], cost(1, 1e6),
-        "v" * n_hi + "vv", *parts,
-    )
-    small = jnp.concatenate([small, move(small, 1)], axis=0)
-    small_other = swap_core(small)
+        beside_kernel, [((rows, width + enc), BF)], [], cost(1, 1), "vv" + "v", w_mid, w_in,
+        mib=58,
+    )
+    (line,) = call(
+        stack_kernel, [((quarter, width + enc), BF)], [], cost(1, 1e6), "v" * n_hi + "v",
+        own, *[move(own, 2 * k) for k in range(1, n_hi)],
+    )
     other = move(line, 1)
     mid = (line, other, swap_core(line), swap_core(other))
+
     square = width // n_pts == enc
-    unmask = point ^ jnp.arange(n_pts, dtype=jnp.int32)
-    unmask = (unmask % 2) * n_hi + unmask // 2
-    wide = lambda v: (
-        v[:, :enc].reshape(n_pts, *branch.shape)[unmask].transpose(1, 0, 2)
-    ).reshape(maps // 2, width)
-    wide_own = None if square else wide(small)
-
+    pairs = [pair] + [move(pair, 2 * k) for k in range(1, n_hi)]
+    if not square:
+        unmask = point ^ jnp.arange(n_pts, dtype=jnp.int32)
+        small = jnp.stack(pairs).reshape(n_pts, *branch.shape)[unmask]
+        pairs = [small.transpose(1, 0, 2).reshape(maps // 2, width)]
     (w_both,) = call(
         both_kernel, [((2 * rows, width), BF)], [], cost(5e10, 1), "svva" + "v",
-        core_ref, w_out, swap_core(w_out), line,
+        core_ref, w_out, swap_core(w_out), own,
     )
     folded, wide_own = call(
         functools.partial(fold_branch_kernel, scale_b),
         [((n_pts, maps // 2, 2 * rows), BF), ((maps // 2, width), BF)], [],
-        cost(1, 1), "svv" + "vv", place, w_both, small if square else wide_own,
+        cost(1, 1), "sv" + "v" * len(pairs) + "vv", place, w_both, *pairs,
     )
     b_own = exchange(folded)
     b_other = swap_core(b_own)
@@ -332,20 +352,20 @@
     ).T
 
     dma = pltpu.SemaphoreType.DMA
-    far, near, s_mine, s_theirs, first, dz = call(
+    far, near, s_mine, s_theirs, dz = call(
         functools.partial(main_kernel, scale_p),
         [((half, width), BF), ((half, width), F32), ((n_pts, rows, maps), F32)]
-        + [((n_pts, rows, maps), BF), ((points, hidden), BF), ((points, width), BF)],
+        + [((n_pts, rows, maps), BF), ((points, width), BF)],
         [
             pltpu.VMEM((points, hidden), BF), pltpu.VMEM((points, width), BF),
             pltpu.VMEM((points, width), BF), pltpu.VMEM((hidden, enc), BF),
             pltpu.VMEM((hidden, width), BF), pltpu.VMEM((points, 2 * maps), BF),
             pltpu.VMEM((width, maps), F32), pltpu.VMEM((maps, width), F32),
-            pltpu.VMEM((half, width), BF), dma((4,)), dma((4,)),
+            pltpu.VMEM((half, width), BF), dma((8,)), dma((4,)),
         ],
-        cost(5e10, 8e6), "svvvhhhhvvv" + "hvvvhh",
-        core_ref, features, small, small_other, *mid, b_own, b_other, t_full,
-        mib=44,
+        cost(5e10, 8e6), "svhhhhvvv" + "hvvvh",
+        core_ref, features, *mid, b_own, b_other, t_full,
+        mib=47,
     )
 
     far_got = swap_core(far)
@@ -360,21 +380,21 @@
         pack_sums_kernel, [((n_pts, rows, maps), BF)], [], cost(1, 1), "vva" + "v",
         s_mine, swap_core(s_theirs), own,
     )
-    in_mine, in_theirs = call(
-        input_kernel, [((n_pts, rows, enc), F32), ((n_pts, rows, enc), BF)],
+    in_mine, in_theirs, in_done = call(
+        input_kernel, [((n_pts, rows, enc), F32), ((n_pts, rows, enc), BF), ((8, enc), F32)],
         [
             pltpu.VMEM((points, enc), BF), pltpu.VMEM((points, hidden), BF),
-            pltpu.VMEM((points, hidden), BF), pltpu.VMEM((hidden, width), BF),
+            pltpu.VMEM((hidden, enc), BF), pltpu.VMEM((hidden, width), BF),
             pltpu.VMEM((points, width), BF), dma((13,)),
         ],
-        cost(5e10, 8e6), "shhhhhhha" + "vv", place, features, first, *mid, dz, own,
-        mib=58,
+        cost(5e10, 8e6), "shhhhhha" + "vvv", place, features, *mid, dz, own,
+        mib=54,
     )
     strip = (maps // 2, width)
     grad_out, p_mine, p_theirs = call(
         functools.partial(sums_kernel, scale_b), [((rows, width), F32), (strip, F32), (strip, BF)],
         [], cost(1, 1), "svvvva" + "vvv",
-        core_ref, exchange(s_code), wide_own, wide_other, w_out, in_mine,
+        core_ref, exchange(s_code), wide_own, wide_other, w_out, in_done,
     )
     part = p_mine + decode(swap_core(p_theirs))
     part = part.reshape(maps // 2, n_pts, width // n_pts).transpose(1, 0, 2)

time: 98.8 us -> 97.7 us (0.989)
  waiting for transfers between devices: 36.5 us -> 26.1 us
  starting transfers between devices: 28.8 us -> 36.9 us
  Pallas kernels: 24.7 us -> 26.4 us
    ppermute x9 -> x12, waiting for transfers between devices: 19.1 us -> 12.7 us  [per_device(): lax.ppermute(v, 'pts', [(i, i ^ mask) for i in range(n_pts)])]
    ppermute x9 -> x12, starting transfers between devices: 12.6 us -> 17.9 us  [per_device(): lax.ppermute(v, 'pts', [(i, i ^ mask) for i in range(n_pts)])]
    all_to_all x3, waiting for transfers between devices: 14.5 us -> 10.4 us  [per_device(): exchange = lambda v: lax.all_to_all(v, 'pts', 0, 0, tiled=True)]
    all_to_all x3, starting transfers between devices: 14 us -> 17 us  [per_device(): exchange = lambda v: lax.all_to_all(v, 'pts', 0, 0, tiled=True)]
    pallas_call x16 -> x17, Pallas kernels: 24.7 us -> 26.4 us  [call(): pl.pallas_call(kernel, in_specs=specs[:len(args)], out_specs=specs[len(ar...]
    unnamed x37 -> x32, local copies, waits for them, and re-layouts: 5.26 us -> 4.81 us
    ppermute x11 -> x10, starting transfers between devices: 2.23 us -> 1.99 us  [per_device(): swap_core = lambda v: lax.ppermute(v, 'maps', [(0, 1), (1, 0)])]
    ppermute x11 -> x10, waiting for transfers between devices: 2.99 us -> 3.01 us  [per_device(): swap_core = lambda v: lax.ppermute(v, 'maps', [(0, 1), (1, 0)])]
  transfers between devices with their start and end apart: 23 -> 25, of which waited for: 11 -> 10; matrix products, arithmetic and copies ran while one was open for 3% -> 2% of each run, Pallas kernels for 15% -> 15%
where the time goes in v4:
time: 97.7 us; the launch traced here: 97.1 us
  starting transfers between devices  36.9 us (38%)
  Pallas kernels  26.4 us (27%)
  waiting for transfers between devices  26.1 us (27%)
  local copies, waits for them, and re-layouts  4.84 us (5%)
  other arithmetic  1.93 us (2%)
    pallas_call x17, Pallas kernels, call(): pl.pallas_call(kernel, in_specs=specs[:len(args)], out_specs=specs[len(ar...  26.4 us
    ppermute x12, starting transfers between devices, per_device(): lax.ppermute(v, 'pts', [(i, i ^ mask) for i in range(n_pts)])  17.9 us
    all_to_all x3, starting transfers between devices, per_device(): exchange = lambda v: lax.all_to_all(v, 'pts', 0, 0, tiled=True)  17 us
    ppermute x12, waiting for transfers between devices, per_device(): lax.ppermute(v, 'pts', [(i, i ^ mask) for i in range(n_pts)])  12.7 us
    all_to_all x3, waiting for transfers between devices, per_device(): exchange = lambda v: lax.all_to_all(v, 'pts', 0, 0, tiled=True)  10.4 us
    unnamed x32, local copies, waits for them, and re-layouts  4.81 us
    ppermute x10, waiting for transfers between devices, per_device(): swap_core = lambda v: lax.ppermute(v, 'maps', [(0, 1), (1, 0)])  3.01 us
    ppermute x10, starting transfers between devices, per_device(): swap_core = lambda v: lax.ppermute(v, 'maps', [(0, 1), (1, 0)])  1.99 us
  transfers between devices with their start and end apart: 25, of which 10 were waited for; matrix products, arithmetic and copies ran while one was open for 2% of the time, Pallas kernels for 15%

profile of v4, /device:TPU:0, one launch (start us, length us, event | category | flops | bytes accessed | tf_op | source)
XLA Modules:
  0.0 97.1 jit_solution(13384506500358939539)
XLA Ops:
  0.6 1.6 %shard_map.102.refs_0_.after = bf16[64,1152]{1,0:T(8,128)(2,1)} custom-call(bf16[64,1024]{1,0:T(8,128)(2,1)} %refs_0_.1, bf16[64,128]{1,0:T(8,128)(2,1)} %refs_1_.1), custom_call_target="tpu_custom_call" | custom-call | flops 1 | bytes 1 | tf_op jit(solution)/shard_map/pallas_call | solution.py:280
  2.2 3.0 %collective-permute-start = (bf16[64,1152]{1,0:T(8,128)(2,1)}, bf16[64,1152]{1,0:T(8,128)(2,1)S(1)}, u32[]{:S(2)}, u32[]{:S(2)}) collective-permute-start(bf16[64,1152]{1,0:T(8,128)(2,1)} %shard_map.102.refs_0_.after), channel_id=1, source_target_pairs={{0,4},{2,6},{4,0},{6,2},{8,12},{10,14},{12,8},{14,10},{1,5},{3,7},... | collective-permute-start | bytes 442376 | tf_op jit(solution)/shard_map/ppermute | solution.py:304
  5.2 2.6 %collective-permute-start.1 = (bf16[64,1152]{1,0:T(8,128)(2,1)}, bf16[64,1152]{1,0:T(8,128)(2,1)S(1)}, u32[]{:S(2)}, u32[]{:S(2)}) collective-permute-start(bf16[64,1152]{1,0:T(8,128)(2,1)} %shard_map.102.refs_0_.after), channel_id=1, source_target_pairs={{0,8},{2,10},{4,12},{6,14},{8,0},{10,2},{12,4},{14,6},{1,9},{3,11}... | collective-permute-start | bytes 442376 | tf_op jit(solution)/shard_map/ppermute | solution.py:304
  7.8 1.7 %collective-permute-start.7 = (bf16[64,128]{1,0:T(8,128)(2,1)}, bf16[64,128]{1,0:T(8,128)(2,1)S(1)}, u32[]{:S(2)}, u32[]{:S(2)}) collective-permute-start(bf16[64,128]{1,0:T(8,128)(2,1)} %own.3), channel_id=1, source_target_pairs={{0,2},{2,0},{4,6},{6,4},{8,10},{10,8},{12,14},{14,12},{1,3},{3,1},... | collective-permute-start | bytes 49160 | tf_op jit(solution)/shard_map/ppermute | solution.py:304
  10.2 1.6 %collective-permute-done.7.got = bf16[64,128]{1,0:T(8,128)(2,1)S(1)} collective-permute-done((bf16[64,128]{1,0:T(8,128)(2,1)}, bf16[64,128]{1,0:T(8,128)(2,1)S(1)}, u32[]{:S(2)}, u32[]{:S(2)}) %collective-permute-start.7) | collective-permute-done | bytes 16416 | tf_op jit(solution)/shard_map/ppermute | solution.py:304
  12.5 3.8 %collective-permute-start.10 = (bf16[128,128]{1,0:T(8,128)(2,1)S(1)}, bf16[128,128]{1,0:T(8,128)(2,1)S(1)}, u32[]{:S(2)}, u32[]{:S(2)}) collective-permute-start(bf16[128,128]{1,0:T(8,128)(2,1)S(1)} %shard_map.105.refs_0_), channel_id=1, source_target_pairs={{0,12},{2,14},{4,8},{6,10},{8,4},{10,6},{12,0},{14,2},{1,13},{3,15... | collective-permute-start | bytes 98312 | tf_op jit(solution)/shard_map/ppermute | solution.py:304
  16.3 3.8 %collective-permute-done.1.refs_2_ = bf16[64,1152]{1,0:T(8,128)(2,1)S(1)} collective-permute-done((bf16[64,1152]{1,0:T(8,128)(2,1)}, bf16[64,1152]{1,0:T(8,128)(2,1)S(1)}, u32[]{:S(2)}, u32[]{:S(2)}) %collective-permute-start.1) | collective-permute-done | bytes 147488 | tf_op jit(solution)/shard_map/ppermute | solution.py:304
  21.1 1.6 %collective-permute-start.3 = (bf16[256,1152]{1,0:T(8,128)(2,1)S(1)}, bf16[256,1152]{1,0:T(8,128)(2,1)S(1)}, u32[]{:S(2)}, u32[]{:S(2)}) collective-permute-start(bf16[256,1152]{1,0:T(8,128)(2,1)S(1)} %shard_map.103.near_a), channel_id=1, source_target_pairs={{0,2},{2,0},{4,6},{6,4},{8,10},{10,8},{12,14},{14,12},{1,3},{3,1},... | collective-permute-start | bytes 1769480 | tf_op jit(solution)/shard_map/ppermute | solution.py:304
  23.7 1.3 %collective-permute-done.9.refs_2_ = bf16[128,128]{1,0:T(8,128)(2,1)S(1)} collective-permute-done((bf16[128,128]{1,0:T(8,128)(2,1)S(1)}, bf16[128,128]{1,0:T(8,128)(2,1)S(1)}, u32[]{:S(2)}, u32[]{:S(2)}) %collective-permute-start.9) | collective-permute-done | bytes 32800 | tf_op jit(solution)/shard_map/ppermute | solution.py:304
  25.0 1.4 %shard_map.106 = (bf16[8,64,128]{2,1,0:T(8,128)(2,1)}, bf16[64,1024]{1,0:T(8,128)(2,1)S(1)}) custom-call(s32[8]{0:T(128)S(1)} %broadcast_xor_fusion.place_ref, bf16[128,1024]{1,0:T(8,128)(2,1)S(1)} %shard_map.104.w_both, bf16[128,128]{1,0:T(8,128)(2,1)S(1)} %shard_map.105.refs_0_, bf16[128,128]{1,0:T(8,128)(2,1)S(1)} %collective-permute-done.8.refs_1_, ...), custom_call_target="tpu_custom_call" | custom-call | flops 1 | bytes 1 | tf_op jit(solution)/shard_map/pallas_call | solution.py:280
  26.4 4.8 %all-to-all-start = ((bf16[8,64,128]{2,1,0:T(8,128)(2,1)}), bf16[8,64,128]{2,1,0:T(8,128)(2,1)S(1)}, u32[]{:S(2)}, u32[]{:S(2)}) async-start(bf16[8,64,128]{2,1,0:T(8,128)(2,1)} %get-tuple-element.23), calls=%async_computation | async-start | bytes 262144 | tf_op jit(solution)/shard_map/all_to_all | solution.py:305
  31.2 2.4 %collective-permute-done.3.near_b = bf16[256,1152]{1,0:T(8,128)(2,1)S(1)} collective-permute-done((bf16[256,1152]{1,0:T(8,128)(2,1)S(1)}, bf16[256,1152]{1,0:T(8,128)(2,1)S(1)}, u32[]{:S(2)}, u32[]{:S(2)}) %collective-permute-start.3) | collective-permute-done | bytes 589856 | tf_op jit(solution)/shard_map/ppermute | solution.py:304
  34.6 4.0 %all-to-all-done.b_own = bf16[8,64,128]{2,1,0:T(8,128)(2,1)S(1)} async-done(((bf16[8,64,128]{2,1,0:T(8,128)(2,1)}), bf16[8,64,128]{2,1,0:T(8,128)(2,1)S(1)}, u32[]{:S(2)}, u32[]{:S(2)}) %all-to-all-start) | async-done | bytes 131104 | tf_op jit(solution)/shard_map/all_to_all | solution.py:305
  40.0 9.3 %shard_map.107 = (bf16[512,1024]{1,0:T(8,128)(2,1)S(1)}, f32[512,1024]{1,0:T(8,128)S(1)}, f32[8,64,128]{2,1,0:T(8,128)S(1)}, bf16[8,64,128]{2,1,0:T(8,128)(2,1)S(1)}, bf16[1024,1024]{1,0:T(8,128)(2,1)}) custom-call(s32[1]{0:T(128)} %bitcast.core_ref, bf16[1024,128]{1,0:T(8,128)(2,1)S(1)} %copy-done.13, bf16[256,1152]{1,0:T(8,128)(2,1)S(1)} %shard_map.103.near_a, ...), custom_call_target="tpu_custom_call" | custom-call | flops 49999998976 | bytes 8000000 | tf_op jit(solution)/shard_map/pallas_call | solution.py:280
  50.2 1.8 %collective-permute-done.14.got = bf16[512,1024]{1,0:T(8,128)(2,1)S(1)} collective-permute-done((bf16[512,1024]{1,0:T(8,128)(2,1)S(1)}, bf16[512,1024]{1,0:T(8,128)(2,1)S(1)}, u32[]{:S(2)}, u32[]{:S(2)}) %collective-permute-start.14) | collective-permute-done | bytes 1048608 | tf_op jit(solution)/shard_map/ppermute | solution.py:303
  54.2 6.5 %all-to-all-start.1 = ((bf16[8,64,128]{2,1,0:T(8,128)(2,1)}), bf16[8,64,128]{2,1,0:T(8,128)(2,1)S(1)}, u32[]{:S(2)}, u32[]{:S(2)}) async-start(bf16[8,64,128]{2,1,0:T(8,128)(2,1)} %shard_map.110), calls=%async_computation.1 | async-start | bytes 262144 | tf_op jit(solution)/shard_map/all_to_all | solution.py:305
  60.7 8.0 %shard_map.111 = (f32[8,64,128]{2,1,0:T(8,128)}, bf16[8,64,128]{2,1,0:T(8,128)(2,1)}, f32[8,128]{1,0:T(8,128)}) custom-call(s32[8]{0:T(128)} %copy-done.9, bf16[1024,128]{1,0:T(8,128)(2,1)} %features_in.1, bf16[256,1152]{1,0:T(8,128)(2,1)} %copy-done.3, bf16[256,1152]{1,0:T(8,128)(2,1)} %copy-done.10, bf16[256,1152]{1,0:T(8,128)(2,1)} %copy-done.11, ...), custom_call_target="tpu_custom_call" | custom-call | flops 49999998976 | bytes 8000000 | tf_op jit(solution)/shard_map/pallas_call | solution.py:280
  69.4 1.0 %shard_map.112 = (f32[64,1024]{1,0:T(8,128)}, f32[64,1024]{1,0:T(8,128)S(1)}, bf16[64,1024]{1,0:T(8,128)(2,1)S(1)}) custom-call(s32[1]{0:T(128)} %bitcast.core_ref, bf16[8,64,128]{2,1,0:T(8,128)(2,1)S(1)} %all-to-all-done.1.got, bf16[64,1024]{1,0:T(8,128)(2,1)S(1)} %get-tuple-element.28.own, bf16[64,1024]{1,0:T(8,128)(2,1)S(1)} %collective-permute-done.15.other, ...), custom_call_target="tpu_custom_call" | custom-call | flops 1 | bytes 1 | tf_op jit(solution)/shard_map/pallas_call | solution.py:280
  72.1 1.2 %copy-done.1 = f32[256,1024]{1,0:T(8,128)S(1)} copy-done((f32[256,1024]{1,0:T(8,128)S(1)}, f32[256,1024]{1,0:T(8,128)}, u32[]{:S(2)}) %copy-start.1) | copy-done | bytes 1048600
  73.8 2.1 %collective-permute-start.19 = (bf16[64,1024]{1,0:T(8,128)(2,1)S(1)}, bf16[64,1024]{1,0:T(8,128)(2,1)S(1)}, u32[]{:S(2)}, u32[]{:S(2)}) collective-permute-start(bf16[64,1024]{1,0:T(8,128)(2,1)S(1)} %get-tuple-element.36.after), channel_id=1, source_target_pairs={{0,4},{2,6},{4,0},{6,2},{8,12},{10,14},{12,8},{14,10},{1,5},{3,7},... | collective-permute-start | bytes 393224 | tf_op jit(solution)/shard_map/ppermute | solution.py:304
  75.9 2.4 %collective-permute-start.20 = (bf16[64,1024]{1,0:T(8,128)(2,1)S(1)}, bf16[64,1024]{1,0:T(8,128)(2,1)S(1)}, u32[]{:S(2)}, u32[]{:S(2)}) collective-permute-start(bf16[64,1024]{1,0:T(8,128)(2,1)S(1)} %get-tuple-element.39), channel_id=1, source_target_pairs={{0,8},{2,10},{4,12},{6,14},{8,0},{10,2},{12,4},{14,6},{1,9},{3,11}... | collective-permute-start | bytes 393224 | tf_op jit(solution)/shard_map/ppermute | solution.py:304
  79.6 5.7 %all-to-all-start.2 = ((bf16[8,64,256]{2,1,0:T(8,128)(2,1)}), bf16[8,64,256]{2,1,0:T(8,128)(2,1)S(1)}, u32[]{:S(2)}, u32[]{:S(2)}) async-start(bf16[8,64,256]{2,1,0:T(8,128)(2,1)} %shard_map.115.after), calls=%async_computation.2 | async-start | bytes 524288 | tf_op jit(solution)/shard_map/all_to_all | solution.py:305
  85.2 3.6 %collective-permute-done.20.refs_1_ = bf16[64,1024]{1,0:T(8,128)(2,1)S(1)} collective-permute-done((bf16[64,1024]{1,0:T(8,128)(2,1)S(1)}, bf16[64,1024]{1,0:T(8,128)(2,1)S(1)}, u32[]{:S(2)}, u32[]{:S(2)}) %collective-permute-start.20) | collective-permute-done | bytes 131104 | tf_op jit(solution)/shard_map/ppermute | solution.py:304
  89.9 6.3 %all-to-all-done.2.got = bf16[8,64,256]{2,1,0:T(8,128)(2,1)S(1)} async-done(((bf16[8,64,256]{2,1,0:T(8,128)(2,1)}), bf16[8,64,256]{2,1,0:T(8,128)(2,1)S(1)}, u32[]{:S(2)}, u32[]{:S(2)}) %all-to-all-start.2) | async-done | bytes 262176 | tf_op jit(solution)/shard_map/all_to_all | solution.py:305
  (80 shorter events, 14.5 us)
Async XLA Ops:
  2.2 14.1 %collective-permute-start = (bf16[64,1152]{1,0:T(8,128)(2,1)}, bf16[64,1152]{1,0:T(8,128)(2,1)S(1)}, u32[]{:S(2)}, u32[]{:S(2)}) collective-permute-start(bf16[64,1152]{1,0:T(8,128)(2,1)} %shard_map.102.refs_0_.after), channel_id=1, source_target_pairs={{0,4},{2,6},{4,0},{6,2},{8,12},{10,14},{12,8},{14,10},{1,5},{3,7},... | collective-permute-start | bytes 442376 | tf_op jit(solution)/shard_map/ppermute | solution.py:304
  5.2 14.9 %collective-permute-start.1 = (bf16[64,1152]{1,0:T(8,128)(2,1)}, bf16[64,1152]{1,0:T(8,128)(2,1)S(1)}, u32[]{:S(2)}, u32[]{:S(2)}) collective-permute-start(bf16[64,1152]{1,0:T(8,128)(2,1)} %shard_map.102.refs_0_.after), channel_id=1, source_target_pairs={{0,8},{2,10},{4,12},{6,14},{8,0},{10,2},{12,4},{14,6},{1,9},{3,11}... | collective-permute-start | bytes 442376 | tf_op jit(solution)/shard_map/ppermute | solution.py:304
  7.8 12.3 %collective-permute-start.2 = (bf16[64,1152]{1,0:T(8,128)(2,1)}, bf16[64,1152]{1,0:T(8,128)(2,1)S(1)}, u32[]{:S(2)}, u32[]{:S(2)}) collective-permute-start(bf16[64,1152]{1,0:T(8,128)(2,1)} %shard_map.102.refs_0_.after), channel_id=1, source_target_pairs={{0,12},{2,14},{4,8},{6,10},{8,4},{10,6},{12,0},{14,2},{1,13},{3,15... | collective-permute-start | bytes 442376 | tf_op jit(solution)/shard_map/ppermute | solution.py:304
  7.8 14.9 %collective-permute-start.6 = (bf16[64,1024]{1,0:T(8,128)(2,1)}, bf16[64,1024]{1,0:T(8,128)(2,1)S(1)}, u32[]{:S(2)}, u32[]{:S(2)}) collective-permute-start(bf16[64,1024]{1,0:T(8,128)(2,1)} %w_out.1), channel_id=1, source_target_pairs={{0,1},{1,0},{2,3},{3,2},{4,5},{5,4},{6,7},{7,6},{8,9},{9,8},{10,11... | collective-permute-start | bytes 393224 | tf_op jit(solution)/shard_map/ppermute | solution.py:303
  7.8 4.0 %collective-permute-start.7 = (bf16[64,128]{1,0:T(8,128)(2,1)}, bf16[64,128]{1,0:T(8,128)(2,1)S(1)}, u32[]{:S(2)}, u32[]{:S(2)}) collective-permute-start(bf16[64,128]{1,0:T(8,128)(2,1)} %own.3), channel_id=1, source_target_pairs={{0,2},{2,0},{4,6},{6,4},{8,10},{10,8},{12,14},{14,12},{1,3},{3,1},... | collective-permute-start | bytes 49160 | tf_op jit(solution)/shard_map/ppermute | solution.py:304
  12.5 11.2 %collective-permute-start.10 = (bf16[128,128]{1,0:T(8,128)(2,1)S(1)}, bf16[128,128]{1,0:T(8,128)(2,1)S(1)}, u32[]{:S(2)}, u32[]{:S(2)}) collective-permute-start(bf16[128,128]{1,0:T(8,128)(2,1)S(1)} %shard_map.105.refs_0_), channel_id=1, source_target_pairs={{0,12},{2,14},{4,8},{6,10},{8,4},{10,6},{12,0},{14,2},{1,13},{3,15... | collective-permute-start | bytes 98312 | tf_op jit(solution)/shard_map/ppermute | solution.py:304
  16.3 7.3 %collective-permute-start.8 = (bf16[128,128]{1,0:T(8,128)(2,1)S(1)}, bf16[128,128]{1,0:T(8,128)(2,1)S(1)}, u32[]{:S(2)}, u32[]{:S(2)}) collective-permute-start(bf16[128,128]{1,0:T(8,128)(2,1)S(1)} %shard_map.105.refs_0_), channel_id=1, source_target_pairs={{0,4},{2,6},{4,0},{6,2},{8,12},{10,14},{12,8},{14,10},{1,5},{3,7},... | collective-permute-start | bytes 98312 | tf_op jit(solution)/shard_map/ppermute | solution.py:304
  20.1 4.9 %collective-permute-start.9 = (bf16[128,128]{1,0:T(8,128)(2,1)S(1)}, bf16[128,128]{1,0:T(8,128)(2,1)S(1)}, u32[]{:S(2)}, u32[]{:S(2)}) collective-permute-start(bf16[128,128]{1,0:T(8,128)(2,1)S(1)} %shard_map.105.refs_0_), channel_id=1, source_target_pairs={{0,8},{2,10},{4,12},{6,14},{8,0},{10,2},{12,4},{14,6},{1,9},{3,11}... | collective-permute-start | bytes 98312 | tf_op jit(solution)/shard_map/ppermute | solution.py:304
  21.1 12.5 %collective-permute-start.3 = (bf16[256,1152]{1,0:T(8,128)(2,1)S(1)}, bf16[256,1152]{1,0:T(8,128)(2,1)S(1)}, u32[]{:S(2)}, u32[]{:S(2)}) collective-permute-start(bf16[256,1152]{1,0:T(8,128)(2,1)S(1)} %shard_map.103.near_a), channel_id=1, source_target_pairs={{0,2},{2,0},{4,6},{6,4},{8,10},{10,8},{12,14},{14,12},{1,3},{3,1},... | collective-permute-start | bytes 1769480 | tf_op jit(solution)/shard_map/ppermute | solution.py:304
  26.4 12.1 %all-to-all-start = ((bf16[8,64,128]{2,1,0:T(8,128)(2,1)}), bf16[8,64,128]{2,1,0:T(8,128)(2,1)S(1)}, u32[]{:S(2)}, u32[]{:S(2)}) async-start(bf16[8,64,128]{2,1,0:T(8,128)(2,1)} %get-tuple-element.23), calls=%async_computation | async-start | bytes 262144 | tf_op jit(solution)/shard_map/all_to_all | solution.py:305
  31.2 8.7 %collective-permute-start.4 = (bf16[256,1152]{1,0:T(8,128)(2,1)S(1)}, bf16[256,1152]{1,0:T(8,128)(2,1)S(1)}, u32[]{:S(2)}, u32[]{:S(2)}) collective-permute-start(bf16[256,1152]{1,0:T(8,128)(2,1)S(1)} %shard_map.103.near_a), channel_id=1, source_target_pairs={{0,1},{1,0},{2,3},{3,2},{4,5},{5,4},{6,7},{7,6},{8,9},{9,8},{10,11... | collective-permute-start | bytes 1769480 | tf_op jit(solution)/shard_map/ppermute | solution.py:303
  33.6 6.3 %collective-permute-start.5 = (bf16[256,1152]{1,0:T(8,128)(2,1)S(1)}, bf16[256,1152]{1,0:T(8,128)(2,1)S(1)}, u32[]{:S(2)}, u32[]{:S(2)}) collective-permute-start(bf16[256,1152]{1,0:T(8,128)(2,1)S(1)} %collective-permute-done.3.near_b), channel_id=1, source_target_pairs={{0,1},{1,0},{2,3},{3,2},{4,5},{5,4},{6,7},{7,6},{8,9},{9,8},{10,11... | collective-permute-start | bytes 1769480 | tf_op jit(solution)/shard_map/ppermute | solution.py:303
  33.8 4.8 %collective-permute-start.12 = (bf16[64,1024]{0,1:T(8,128)(2,1)S(1)}, bf16[64,1024]{0,1:T(8,128)(2,1)}, u32[]{:S(2)}, u32[]{:S(2)}) collective-permute-start(bf16[64,1024]{0,1:T(8,128)(2,1)S(1)} %copy.17), channel_id=1, source_target_pairs={{0,1},{1,0},{2,3},{3,2},{4,5},{5,4},{6,7},{7,6},{8,9},{9,8},{10,11... | collective-permute-start | bytes 393224 | tf_op jit(solution)/shard_map/ppermute | solution.py:303
  49.3 2.7 %collective-permute-start.14 = (bf16[512,1024]{1,0:T(8,128)(2,1)S(1)}, bf16[512,1024]{1,0:T(8,128)(2,1)S(1)}, u32[]{:S(2)}, u32[]{:S(2)}) collective-permute-start(bf16[512,1024]{1,0:T(8,128)(2,1)S(1)} %get-tuple-element.27), channel_id=1, source_target_pairs={{0,1},{1,0},{2,3},{3,2},{4,5},{5,4},{6,7},{7,6},{8,9},{9,8},{10,11... | collective-permute-start | bytes 3145736 | tf_op jit(solution)/shard_map/ppermute | solution.py:303
  49.7 19.0 %collective-permute-start.15 = (bf16[64,1024]{1,0:T(8,128)(2,1)S(1)}, bf16[64,1024]{1,0:T(8,128)(2,1)S(1)}, u32[]{:S(2)}, u32[]{:S(2)}) collective-permute-start(bf16[64,1024]{1,0:T(8,128)(2,1)S(1)} %get-tuple-element.28.own), channel_id=1, source_target_pairs={{0,1},{1,0},{2,3},{3,2},{4,5},{5,4},{6,7},{7,6},{8,9},{9,8},{10,11... | collective-permute-start | bytes 393224 | tf_op jit(solution)/shard_map/ppermute | solution.py:303
  49.9 3.4 %collective-permute-start.13 = (bf16[8,64,128]{2,1,0:T(8,128)(2,1)S(1)}, bf16[8,64,128]{2,1,0:T(8,128)(2,1)S(1)}, u32[]{:S(2)}, u32[]{:S(2)}) collective-permute-start(bf16[8,64,128]{2,1,0:T(8,128)(2,1)S(1)} %get-tuple-element.25), channel_id=1, source_target_pairs={{0,1},{1,0},{2,3},{3,2},{4,5},{5,4},{6,7},{7,6},{8,9},{9,8},{10,11... | collective-permute-start | bytes 393224 | tf_op jit(solution)/shard_map/ppermute | solution.py:303
  52.5 19.6 %collective-permute-start.18 = (bf16[256,1024]{1,0:T(8,128)(2,1)S(1)}, bf16[256,1024]{1,0:T(8,128)(2,1)S(1)}, u32[]{:S(2)}, u32[]{:S(2)}) collective-permute-start(bf16[256,1024]{1,0:T(8,128)(2,1)S(1)} %shard_map.108.after), channel_id=1, source_target_pairs={{0,2},{2,0},{4,6},{6,4},{8,10},{10,8},{12,14},{14,12},{1,3},{3,1},... | collective-permute-start | bytes 1572872 | tf_op jit(solution)/shard_map/ppermute | solution.py:304
  54.2 14.5 %all-to-all-start.1 = ((bf16[8,64,128]{2,1,0:T(8,128)(2,1)}), bf16[8,64,128]{2,1,0:T(8,128)(2,1)S(1)}, u32[]{:S(2)}, u32[]{:S(2)}) async-start(bf16[8,64,128]{2,1,0:T(8,128)(2,1)} %shard_map.110), calls=%async_computation.1 | async-start | bytes 262144 | tf_op jit(solution)/shard_map/all_to_all | solution.py:305
  70.5 1.5 %collective-permute-start.16 = (bf16[64,1024]{1,0:T(8,128)(2,1)S(1)}, bf16[64,1024]{1,0:T(8,128)(2,1)S(1)}, u32[]{:S(2)}, u32[]{:S(2)}) collective-permute-start(bf16[64,1024]{1,0:T(8,128)(2,1)S(1)} %get-tuple-element.32), channel_id=1, source_target_pairs={{0,1},{1,0},{2,3},{3,2},{4,5},{5,4},{6,7},{7,6},{8,9},{9,8},{10,11... | collective-permute-start | bytes 393224 | tf_op jit(solution)/shard_map/ppermute | solution.py:303
  70.5 8.2 %collective-permute-start.17 = (bf16[8,64,128]{2,1,0:T(8,128)(2,1)}, bf16[8,64,128]{2,1,0:T(8,128)(2,1)S(1)}, u32[]{:S(2)}, u32[]{:S(2)}) collective-permute-start(bf16[8,64,128]{2,1,0:T(8,128)(2,1)} %get-tuple-element.34), channel_id=1, source_target_pairs={{0,1},{1,0},{2,3},{3,2},{4,5},{5,4},{6,7},{7,6},{8,9},{9,8},{10,11... | collective-permute-start | bytes 393224 | tf_op jit(solution)/shard_map/ppermute | solution.py:303
  73.8 11.4 %collective-permute-start.19 = (bf16[64,1024]{1,0:T(8,128)(2,1)S(1)}, bf16[64,1024]{1,0:T(8,128)(2,1)S(1)}, u32[]{:S(2)}, u32[]{:S(2)}) collective-permute-start(bf16[64,1024]{1,0:T(8,128)(2,1)S(1)} %get-tuple-element.36.after), channel_id=1, source_target_pairs={{0,4},{2,6},{4,0},{6,2},{8,12},{10,14},{12,8},{14,10},{1,5},{3,7},... | collective-permute-start | bytes 393224 | tf_op jit(solution)/shard_map/ppermute | solution.py:304
  75.9 13.0 %collective-permute-start.20 = (bf16[64,1024]{1,0:T(8,128)(2,1)S(1)}, bf16[64,1024]{1,0:T(8,128)(2,1)S(1)}, u32[]{:S(2)}, u32[]{:S(2)}) collective-permute-start(bf16[64,1024]{1,0:T(8,128)(2,1)S(1)} %get-tuple-element.39), channel_id=1, source_target_pairs={{0,8},{2,10},{4,12},{6,14},{8,0},{10,2},{12,4},{14,6},{1,9},{3,11}... | collective-permute-start | bytes 393224 | tf_op jit(solution)/shard_map/ppermute | solution.py:304
  78.3 10.5 %collective-permute-start.21 = (bf16[64,1024]{1,0:T(8,128)(2,1)S(1)}, bf16[64,1024]{1,0:T(8,128)(2,1)S(1)}, u32[]{:S(2)}, u32[]{:S(2)}) collective-permute-start(bf16[64,1024]{1,0:T(8,128)(2,1)S(1)} %get-tuple-element.40), channel_id=1, source_target_pairs={{0,12},{2,14},{4,8},{6,10},{8,4},{10,6},{12,0},{14,2},{1,13},{3,15... | collective-permute-start | bytes 393224 | tf_op jit(solution)/shard_map/ppermute | solution.py:304
  79.6 16.7 %all-to-all-start.2 = ((bf16[8,64,256]{2,1,0:T(8,128)(2,1)}), bf16[8,64,256]{2,1,0:T(8,128)(2,1)S(1)}, u32[]{:S(2)}, u32[]{:S(2)}) async-start(bf16[8,64,256]{2,1,0:T(8,128)(2,1)} %shard_map.115.after), calls=%async_computation.2 | async-start | bytes 524288 | tf_op jit(solution)/shard_map/all_to_all | solution.py:305
  (16 other events, 118.4 us)

commit v5 on v4

--- a/solution.py
+++ b/solution.py
@@ -85,10 +85,11 @@
     scale_p, core_ref, features, near_a, near_b, far_a, far_b,
     b_own, b_other, target,
     far, near, s_mine, s_theirs, dz_out,
-    first, second, dz, w_in, w_mid, pairs, b_all, branch, far_all, in_sem, out_sem,
+    first, second, dz, w_in, w_mid, pairs, branch, far_all, in_sem, out_sem,
 ):
     points, hidden = first.shape
-    n_pts, rows, maps = s_mine.shape
+    n_pts, few, rows = s_mine.shape
+    rows, maps = rows // 2, 2 * few
     enc = features.shape[1]
     quarter, half, step = hidden // 4, hidden // 2, points // 4
     width = w_mid.shape[1]
@@ -109,7 +110,6 @@
     for i in range(4):
         block = slice(i * step, (i + 1) * step)
         first[block, :] = jnp.tanh(dot(features[block, :], w_in[...], 1, 1)).astype(BF)
-    few = maps // 2
     for p in range(n_pts):
         cols = slice(2 * p * rows, 2 * (p + 1) * rows)
         branch[pl.ds(core * few, few), cols] = decode(b_own[p])
@@ -133,12 +133,14 @@
         dz[block, :] = (back * (1.0 - s32 * s32)).astype(BF)
     save_dz = pltpu.make_async_copy(dz, dz_out, out_sem.at[1])
     save_dz.start()
-    both = dot(second[...], pairs[...], 0, 0)
-    b_all[...] = both[:, :maps] + both[:, maps:]
+    both = dot(pairs[...], second[...], 0, 0)
+    sums = both[:maps] + both[maps:]
+    zero = core == 0
+    own, other = jnp.where(zero, sums[:few], sums[few:]), jnp.where(zero, sums[few:], sums[:few])
     for p in range(n_pts):
-        at = 2 * p * rows
-        s_mine[p] = b_all[pl.ds(at + core * rows, rows), :]
-        s_theirs[p] = encode(b_all[pl.ds(at + (1 - core) * rows, rows), :])
+        cols = slice(2 * p * rows, 2 * (p + 1) * rows)
+        s_mine[p] = own[:, cols]
+        s_theirs[p] = encode(other[:, cols])
     saves = [save_dz]
     for i in range(4):
         block = slice(i * quarter, (i + 1) * quarter)
@@ -170,20 +172,26 @@
     out[...] = encode(mine[...] + decode(got[...]))
 
 
-def sums_kernel(scale_b, core_ref, got, own, other, w_out, after, grad_out, mine, theirs):
+def sums_kernel(scale_b, got, w_both, after, total_out, part):
     total = decode(got[0])
     for p in range(1, got.shape[0]):
         total += decode(got[p])
-    sh, sl = split(total)
-    w = w_out[...]
+    total_out[...] = total
+    high, low = split(total)
+    w = w_both[...]
+    part[...] = (dot(high, w, 1, 0) + dot(low, w, 1, 0)) * scale_b
+
+
+def grad_out_kernel(scale_b, core_ref, mine, theirs, own, other, after, grad_out):
     zero = core_ref[0] == 0
-    top, bottom = jnp.where(zero, own[...], other[...]), jnp.where(zero, other[...], own[...])
-    b = jnp.concatenate([top, bottom], axis=0)
-    grad_out[...] = (dot(sh, b, 1, 0) + dot(sl, b, 1, 0)) * scale_b
-    part = (dot(sh, w, 0, 0) + dot(sl, w, 0, 0)) * scale_b
-    half = part.shape[0] // 2
-    mine[...] = jnp.where(zero, part[:half], part[half:])
-    theirs[...] = encode(jnp.where(zero, part[half:], part[:half]))
+    rows = grad_out.shape[0]
+    both = lambda a, b: jnp.concatenate(
+        [jnp.where(zero, a[...], b[...]), jnp.where(zero, b[...], a[...])], axis=0
+    )
+    sums = both(mine, theirs)
+    high, low = split(jnp.where(zero, sums[:, :rows], sums[:, rows:]))
+    branch = both(own, other)
+    grad_out[...] = (dot(high, branch, 0, 0) + dot(low, branch, 0, 0)) * scale_b
 
 
 def input_kernel(
@@ -236,8 +244,10 @@
 
 
 def pack_last_kernel(part, mine, got, after, out):
-    enc = part.shape[2]
-    out[:, :, :enc] = encode(part[...])
+    enc = mine.shape[2]
+    for p in range(out.shape[0]):
+        block = part[p] if part.shape == mine.shape else part[:, p * enc : (p + 1) * enc]
+        out[p, :, :enc] = encode(block)
     out[:, :, enc:] = encode(mine[...] + decode(got[...]))
 
 
@@ -352,15 +362,16 @@
     ).T
 
     dma = pltpu.SemaphoreType.DMA
+    sums_block = (n_pts, maps // 2, 2 * rows)
     far, near, s_mine, s_theirs, dz = call(
         functools.partial(main_kernel, scale_p),
-        [((half, width), BF), ((half, width), F32), ((n_pts, rows, maps), F32)]
-        + [((n_pts, rows, maps), BF), ((points, width), BF)],
+        [((half, width), BF), ((half, width), F32), (sums_block, F32), (sums_block, BF)]
+        + [((points, width), BF)],
         [
             pltpu.VMEM((points, hidden), BF), pltpu.VMEM((points, width), BF),
             pltpu.VMEM((points, width), BF), pltpu.VMEM((hidden, enc), BF),
             pltpu.VMEM((hidden, width), BF), pltpu.VMEM((points, 2 * maps), BF),
-            pltpu.VMEM((width, maps), F32), pltpu.VMEM((maps, width), F32),
+            pltpu.VMEM((maps, width), F32),
             pltpu.VMEM((half, width), BF), dma((8,)), dma((4,)),
         ],
         cost(5e10, 8e6), "svhhhhvvv" + "hvvvh",
@@ -377,7 +388,7 @@
     )
 
     (s_code,) = call(
-        pack_sums_kernel, [((n_pts, rows, maps), BF)], [], cost(1, 1), "vva" + "v",
+        pack_sums_kernel, [(sums_block, BF)], [], cost(1, 1), "vva" + "v",
         s_mine, swap_core(s_theirs), own,
     )
     in_mine, in_theirs, in_done = call(
@@ -390,15 +401,14 @@
         cost(5e10, 8e6), "shhhhhha" + "vvv", place, features, *mid, dz, own,
         mib=54,
     )
-    strip = (maps // 2, width)
-    grad_out, p_mine, p_theirs = call(
-        functools.partial(sums_kernel, scale_b), [((rows, width), F32), (strip, F32), (strip, BF)],
-        [], cost(1, 1), "svvvva" + "vvv",
-        core_ref, exchange(s_code), wide_own, wide_other, w_out, in_done,
-    )
-    part = p_mine + decode(swap_core(p_theirs))
-    part = part.reshape(maps // 2, n_pts, width // n_pts).transpose(1, 0, 2)
-    part = part.reshape(n_pts, rows, enc)
+    total, part = call(
+        functools.partial(sums_kernel, scale_b),
+        [((maps // 2, 2 * rows), F32), ((maps // 2, width), F32)],
+        [], cost(1, 1), "vva" + "vv", exchange(s_code), w_both, in_done,
+    )
+    if not square:
+        part = part.reshape(maps // 2, n_pts, width // n_pts).transpose(1, 0, 2)
+        part = part.reshape(n_pts, rows, enc)
 
     wide_row = (rows, width)
     keep, *codes = call(
@@ -411,6 +421,10 @@
         part, in_mine, swap_core(in_theirs), keep,
     )
     (keep,) = call(hold_kernel, [(wide_row, F32)], [], cost(5e10, 1), "va" + "v", keep, last)
+    (grad_out,) = call(
+        functools.partial(grad_out_kernel, scale_b), [((rows, width), F32)], [], cost(1, 1),
+        "svvvva" + "v", core_ref, total, swap_core(total), wide_own, wide_other, keep,
+    )
     codes = [move(code, 2 * (k + 1)) for k, code in enumerate(codes)]
     (grad_mid,) = call(
         last_kernel, [(wide_row, F32)], [], cost(1, 1), "v" * n_hi + "v", keep, *codes

time: 97.7 us -> 96.4 us (0.987)
  waiting for transfers between devices: 26.1 us -> 22.4 us
  local copies, waits for them, and re-layouts: 4.84 us -> 6.23 us
  Pallas kernels: 26.4 us -> 27.7 us
    ppermute x12, waiting for transfers between devices: 12.7 us -> 9.82 us  [per_device(): lax.ppermute(v, 'pts', [(i, i ^ mask) for i in range(n_pts)])]
    unnamed x32 -> x34, local copies, waits for them, and re-layouts: 4.81 us -> 6.2 us
    pallas_call x17 -> x18, Pallas kernels: 26.4 us -> 27.7 us  [call(): pl.pallas_call(kernel, in_specs=specs[:len(args)], out_specs=specs[len(ar...]
    ppermute x10, waiting for transfers between devices: 3.01 us -> 2.02 us  [per_device(): swap_core = lambda v: lax.ppermute(v, 'maps', [(0, 1), (1, 0)])]
  transfers between devices with their start and end apart: 25 -> 25, of which waited for: 10 -> 9; matrix products, arithmetic and copies ran while one was open for 2% -> 3% of each run, Pallas kernels for 15% -> 17%
where the time goes in v5:
time: 96.4 us; the launch traced here: 95.7 us
  starting transfers between devices  36.8 us (38%)
  Pallas kernels  27.7 us (29%)
  waiting for transfers between devices  22.4 us (23%)
  local copies, waits for them, and re-layouts  6.23 us (6%)
  other arithmetic  1.8 us (2%)
    pallas_call x18, Pallas kernels, call(): pl.pallas_call(kernel, in_specs=specs[:len(args)], out_specs=specs[len(ar...  27.7 us
    ppermute x12, starting transfers between devices, per_device(): lax.ppermute(v, 'pts', [(i, i ^ mask) for i in range(n_pts)])  17.6 us
    all_to_all x3, starting transfers between devices, per_device(): exchange = lambda v: lax.all_to_all(v, 'pts', 0, 0, tiled=True)  17.1 us
    all_to_all x3, waiting for transfers between devices, per_device(): exchange = lambda v: lax.all_to_all(v, 'pts', 0, 0, tiled=True)  10.5 us
    ppermute x12, waiting for transfers between devices, per_device(): lax.ppermute(v, 'pts', [(i, i ^ mask) for i in range(n_pts)])  9.82 us
    unnamed x34, local copies, waits for them, and re-layouts  6.2 us
    ppermute x10, starting transfers between devices, per_device(): swap_core = lambda v: lax.ppermute(v, 'maps', [(0, 1), (1, 0)])  2.02 us
    ppermute x10, waiting for transfers between devices, per_device(): swap_core = lambda v: lax.ppermute(v, 'maps', [(0, 1), (1, 0)])  2.02 us
  transfers between devices with their start and end apart: 25, of which 9 were waited for; matrix products, arithmetic and copies ran while one was open for 3% of the time, Pallas kernels for 17%

profile of v5, /device:TPU:0, one launch (start us, length us, event | category | flops | bytes accessed | tf_op | source)
XLA Modules:
  0.0 95.7 jit_solution(4815739210945583464)
XLA Ops:
  0.6 1.6 %shard_map.102.refs_0_.after = bf16[64,1152]{1,0:T(8,128)(2,1)} custom-call(bf16[64,1024]{1,0:T(8,128)(2,1)} %refs_0_.1, bf16[64,128]{1,0:T(8,128)(2,1)} %refs_1_.1), custom_call_target="tpu_custom_call" | custom-call | flops 1 | bytes 1 | tf_op jit(solution)/shard_map/pallas_call | solution.py:290
  2.2 3.0 %collective-permute-start = (bf16[64,1152]{1,0:T(8,128)(2,1)}, bf16[64,1152]{1,0:T(8,128)(2,1)S(1)}, u32[]{:S(2)}, u32[]{:S(2)}) collective-permute-start(bf16[64,1152]{1,0:T(8,128)(2,1)} %shard_map.102.refs_0_.after), channel_id=1, source_target_pairs={{0,4},{2,6},{4,0},{6,2},{8,12},{10,14},{12,8},{14,10},{1,5},{3,7},... | collective-permute-start | bytes 442376 | tf_op jit(solution)/shard_map/ppermute | solution.py:314
  5.2 2.6 %collective-permute-start.1 = (bf16[64,1152]{1,0:T(8,128)(2,1)}, bf16[64,1152]{1,0:T(8,128)(2,1)S(1)}, u32[]{:S(2)}, u32[]{:S(2)}) collective-permute-start(bf16[64,1152]{1,0:T(8,128)(2,1)} %shard_map.102.refs_0_.after), channel_id=1, source_target_pairs={{0,8},{2,10},{4,12},{6,14},{8,0},{10,2},{12,4},{14,6},{1,9},{3,11}... | collective-permute-start | bytes 442376 | tf_op jit(solution)/shard_map/ppermute | solution.py:314
  7.8 1.7 %collective-permute-start.7 = (bf16[64,128]{1,0:T(8,128)(2,1)}, bf16[64,128]{1,0:T(8,128)(2,1)S(1)}, u32[]{:S(2)}, u32[]{:S(2)}) collective-permute-start(bf16[64,128]{1,0:T(8,128)(2,1)} %own.3), channel_id=1, source_target_pairs={{0,2},{2,0},{4,6},{6,4},{8,10},{10,8},{12,14},{14,12},{1,3},{3,1},... | collective-permute-start | bytes 49160 | tf_op jit(solution)/shard_map/ppermute | solution.py:314
  10.2 1.6 %collective-permute-done.7.got = bf16[64,128]{1,0:T(8,128)(2,1)S(1)} collective-permute-done((bf16[64,128]{1,0:T(8,128)(2,1)}, bf16[64,128]{1,0:T(8,128)(2,1)S(1)}, u32[]{:S(2)}, u32[]{:S(2)}) %collective-permute-start.7) | collective-permute-done | bytes 16416 | tf_op jit(solution)/shard_map/ppermute | solution.py:314
  12.5 3.8 %collective-permute-start.10 = (bf16[128,128]{1,0:T(8,128)(2,1)S(1)}, bf16[128,128]{1,0:T(8,128)(2,1)S(1)}, u32[]{:S(2)}, u32[]{:S(2)}) collective-permute-start(bf16[128,128]{1,0:T(8,128)(2,1)S(1)} %shard_map.105.refs_0_), channel_id=1, source_target_pairs={{0,12},{2,14},{4,8},{6,10},{8,4},{10,6},{12,0},{14,2},{1,13},{3,15... | collective-permute-start | bytes 98312 | tf_op jit(solution)/shard_map/ppermute | solution.py:314
  16.3 3.8 %collective-permute-done.1.refs_2_ = bf16[64,1152]{1,0:T(8,128)(2,1)S(1)} collective-permute-done((bf16[64,1152]{1,0:T(8,128)(2,1)}, bf16[64,1152]{1,0:T(8,128)(2,1)S(1)}, u32[]{:S(2)}, u32[]{:S(2)}) %collective-permute-start.1) | collective-permute-done | bytes 147488 | tf_op jit(solution)/shard_map/ppermute | solution.py:314
  21.1 1.6 %collective-permute-start.3 = (bf16[256,1152]{1,0:T(8,128)(2,1)S(1)}, bf16[256,1152]{1,0:T(8,128)(2,1)S(1)}, u32[]{:S(2)}, u32[]{:S(2)}) collective-permute-start(bf16[256,1152]{1,0:T(8,128)(2,1)S(1)} %shard_map.103.near_a), channel_id=1, source_target_pairs={{0,2},{2,0},{4,6},{6,4},{8,10},{10,8},{12,14},{14,12},{1,3},{3,1},... | collective-permute-start | bytes 1769480 | tf_op jit(solution)/shard_map/ppermute | solution.py:314
  23.7 1.3 %collective-permute-done.9.refs_2_ = bf16[128,128]{1,0:T(8,128)(2,1)S(1)} collective-permute-done((bf16[128,128]{1,0:T(8,128)(2,1)S(1)}, bf16[128,128]{1,0:T(8,128)(2,1)S(1)}, u32[]{:S(2)}, u32[]{:S(2)}) %collective-permute-start.9) | collective-permute-done | bytes 32800 | tf_op jit(solution)/shard_map/ppermute | solution.py:314
  25.0 1.4 %shard_map.106 = (bf16[8,64,128]{2,1,0:T(8,128)(2,1)}, bf16[64,1024]{1,0:T(8,128)(2,1)}) custom-call(s32[8]{0:T(128)S(1)} %broadcast_xor_fusion.place_ref, bf16[128,1024]{1,0:T(8,128)(2,1)S(1)} %shard_map.104.w_both, bf16[128,128]{1,0:T(8,128)(2,1)S(1)} %shard_map.105.refs_0_, bf16[128,128]{1,0:T(8,128)(2,1)S(1)} %collective-permute-done.8.refs_1_, ...), custom_call_target="tpu_custom_call" | custom-call | flops 1 | bytes 1 | tf_op jit(solution)/shard_map/pallas_call | solution.py:290
  27.2 4.8 %all-to-all-start = ((bf16[8,64,128]{2,1,0:T(8,128)(2,1)}), bf16[8,64,128]{2,1,0:T(8,128)(2,1)S(1)}, u32[]{:S(2)}, u32[]{:S(2)}) async-start(bf16[8,64,128]{2,1,0:T(8,128)(2,1)} %get-tuple-element.22), calls=%async_computation | async-start | bytes 262144 | tf_op jit(solution)/shard_map/all_to_all | solution.py:315
  32.0 1.5 %collective-permute-done.3.near_b = bf16[256,1152]{1,0:T(8,128)(2,1)S(1)} collective-permute-done((bf16[256,1152]{1,0:T(8,128)(2,1)S(1)}, bf16[256,1152]{1,0:T(8,128)(2,1)S(1)}, u32[]{:S(2)}, u32[]{:S(2)}) %collective-permute-start.3) | collective-permute-done | bytes 589856 | tf_op jit(solution)/shard_map/ppermute | solution.py:314
  35.0 4.3 %all-to-all-done.b_own = bf16[8,64,128]{2,1,0:T(8,128)(2,1)S(1)} async-done(((bf16[8,64,128]{2,1,0:T(8,128)(2,1)}), bf16[8,64,128]{2,1,0:T(8,128)(2,1)S(1)}, u32[]{:S(2)}, u32[]{:S(2)}) %all-to-all-start) | async-done | bytes 131104 | tf_op jit(solution)/shard_map/all_to_all | solution.py:315
  40.7 9.3 %shard_map.107 = (bf16[512,1024]{1,0:T(8,128)(2,1)S(1)}, f32[512,1024]{1,0:T(8,128)S(1)}, f32[8,64,128]{2,1,0:T(8,128)S(1)}, bf16[8,64,128]{2,1,0:T(8,128)(2,1)S(1)}, bf16[1024,1024]{1,0:T(8,128)(2,1)}) custom-call(s32[1]{0:T(128)} %bitcast.core_ref, bf16[1024,128]{1,0:T(8,128)(2,1)S(1)} %copy-done.13, bf16[256,1152]{1,0:T(8,128)(2,1)S(1)} %shard_map.103.near_a, ...), custom_call_target="tpu_custom_call" | custom-call | flops 49999998976 | bytes 8000000 | tf_op jit(solution)/shard_map/pallas_call | solution.py:290
  50.9 1.8 %collective-permute-done.14.got = bf16[512,1024]{1,0:T(8,128)(2,1)S(1)} collective-permute-done((bf16[512,1024]{1,0:T(8,128)(2,1)S(1)}, bf16[512,1024]{1,0:T(8,128)(2,1)S(1)}, u32[]{:S(2)}, u32[]{:S(2)}) %collective-permute-start.14) | collective-permute-done | bytes 1048608 | tf_op jit(solution)/shard_map/ppermute | solution.py:313
  54.9 6.4 %all-to-all-start.1 = ((bf16[8,64,128]{2,1,0:T(8,128)(2,1)}), bf16[8,64,128]{2,1,0:T(8,128)(2,1)S(1)}, u32[]{:S(2)}, u32[]{:S(2)}) async-start(bf16[8,64,128]{2,1,0:T(8,128)(2,1)} %shard_map.110), calls=%async_computation.1 | async-start | bytes 262144 | tf_op jit(solution)/shard_map/all_to_all | solution.py:315
  61.3 8.0 %shard_map.111 = (f32[8,64,128]{2,1,0:T(8,128)}, bf16[8,64,128]{2,1,0:T(8,128)(2,1)}, f32[8,128]{1,0:T(8,128)}) custom-call(s32[8]{0:T(128)} %copy-done.9, bf16[1024,128]{1,0:T(8,128)(2,1)} %features_in.1, bf16[256,1152]{1,0:T(8,128)(2,1)} %copy-done.5, bf16[256,1152]{1,0:T(8,128)(2,1)} %copy-done.10, bf16[256,1152]{1,0:T(8,128)(2,1)} %copy-done.11, ...), custom_call_target="tpu_custom_call" | custom-call | flops 49999998976 | bytes 8000000 | tf_op jit(solution)/shard_map/pallas_call | solution.py:290
  70.9 1.2 %copy-done.1 = f32[256,1024]{1,0:T(8,128)S(1)} copy-done((f32[256,1024]{1,0:T(8,128)S(1)}, f32[256,1024]{1,0:T(8,128)}, u32[]{:S(2)}) %copy-start.1) | copy-done | bytes 1048600
  72.6 2.1 %collective-permute-start.17 = (bf16[64,1024]{1,0:T(8,128)(2,1)S(1)}, bf16[64,1024]{1,0:T(8,128)(2,1)S(1)}, u32[]{:S(2)}, u32[]{:S(2)}) collective-permute-start(bf16[64,1024]{1,0:T(8,128)(2,1)S(1)} %get-tuple-element.33.after), channel_id=1, source_target_pairs={{0,4},{2,6},{4,0},{6,2},{8,12},{10,14},{12,8},{14,10},{1,5},{3,7},... | collective-permute-start | bytes 393224 | tf_op jit(solution)/shard_map/ppermute | solution.py:314
  74.7 2.4 %collective-permute-start.18 = (bf16[64,1024]{1,0:T(8,128)(2,1)S(1)}, bf16[64,1024]{1,0:T(8,128)(2,1)S(1)}, u32[]{:S(2)}, u32[]{:S(2)}) collective-permute-start(bf16[64,1024]{1,0:T(8,128)(2,1)S(1)} %get-tuple-element.36), channel_id=1, source_target_pairs={{0,8},{2,10},{4,12},{6,14},{8,0},{10,2},{12,4},{14,6},{1,9},{3,11}... | collective-permute-start | bytes 393224 | tf_op jit(solution)/shard_map/ppermute | solution.py:314
  78.1 5.9 %all-to-all-start.2 = ((bf16[8,64,256]{2,1,0:T(8,128)(2,1)}), bf16[8,64,256]{2,1,0:T(8,128)(2,1)S(1)}, u32[]{:S(2)}, u32[]{:S(2)}) async-start(bf16[8,64,256]{2,1,0:T(8,128)(2,1)} %shard_map.115.after), calls=%async_computation.2 | async-start | bytes 524288 | tf_op jit(solution)/shard_map/all_to_all | solution.py:315
  84.0 2.0 %shard_map.119 = f32[64,1024]{1,0:T(8,128)} custom-call(s32[1]{0:T(128)} %bitcast.core_ref, f32[64,128]{1,0:T(8,128)S(1)} %get-tuple-element.38.mine, f32[64,128]{1,0:T(8,128)S(1)} %collective-permute-done.20.theirs, bf16[64,1024]{1,0:T(8,128)(2,1)} %get-tuple-element.39.own, bf16[64,1024]{1,0:T(8,128)(2,1)} %collective-permute-done.21.other, ...), custom_call_target="tpu_custom_call" | custom-call | flops 1 | bytes 1 | tf_op jit(solution)/shard_map/pallas_call | solution.py:290
  86.0 1.6 %collective-permute-done.18.refs_1_ = bf16[64,1024]{1,0:T(8,128)(2,1)S(1)} collective-permute-done((bf16[64,1024]{1,0:T(8,128)(2,1)S(1)}, bf16[64,1024]{1,0:T(8,128)(2,1)S(1)}, u32[]{:S(2)}, u32[]{:S(2)}) %collective-permute-start.18) | collective-permute-done | bytes 131104 | tf_op jit(solution)/shard_map/ppermute | solution.py:314
  88.7 6.2 %all-to-all-done.2.got = bf16[8,64,256]{2,1,0:T(8,128)(2,1)S(1)} async-done(((bf16[8,64,256]{2,1,0:T(8,128)(2,1)}), bf16[8,64,256]{2,1,0:T(8,128)(2,1)S(1)}, u32[]{:S(2)}, u32[]{:S(2)}) %all-to-all-start.2) | async-done | bytes 262176 | tf_op jit(solution)/shard_map/all_to_all | solution.py:315
  (82 shorter events, 14.9 us)
Async XLA Ops:
  2.2 14.1 %collective-permute-start = (bf16[64,1152]{1,0:T(8,128)(2,1)}, bf16[64,1152]{1,0:T(8,128)(2,1)S(1)}, u32[]{:S(2)}, u32[]{:S(2)}) collective-permute-start(bf16[64,1152]{1,0:T(8,128)(2,1)} %shard_map.102.refs_0_.after), channel_id=1, source_target_pairs={{0,4},{2,6},{4,0},{6,2},{8,12},{10,14},{12,8},{14,10},{1,5},{3,7},... | collective-permute-start | bytes 442376 | tf_op jit(solution)/shard_map/ppermute | solution.py:314
  5.2 14.9 %collective-permute-start.1 = (bf16[64,1152]{1,0:T(8,128)(2,1)}, bf16[64,1152]{1,0:T(8,128)(2,1)S(1)}, u32[]{:S(2)}, u32[]{:S(2)}) collective-permute-start(bf16[64,1152]{1,0:T(8,128)(2,1)} %shard_map.102.refs_0_.after), channel_id=1, source_target_pairs={{0,8},{2,10},{4,12},{6,14},{8,0},{10,2},{12,4},{14,6},{1,9},{3,11}... | collective-permute-start | bytes 442376 | tf_op jit(solution)/shard_map/ppermute | solution.py:314
  7.8 12.3 %collective-permute-start.2 = (bf16[64,1152]{1,0:T(8,128)(2,1)}, bf16[64,1152]{1,0:T(8,128)(2,1)S(1)}, u32[]{:S(2)}, u32[]{:S(2)}) collective-permute-start(bf16[64,1152]{1,0:T(8,128)(2,1)} %shard_map.102.refs_0_.after), channel_id=1, source_target_pairs={{0,12},{2,14},{4,8},{6,10},{8,4},{10,6},{12,0},{14,2},{1,13},{3,15... | collective-permute-start | bytes 442376 | tf_op jit(solution)/shard_map/ppermute | solution.py:314
  7.8 14.9 %collective-permute-start.6 = (bf16[64,1024]{1,0:T(8,128)(2,1)}, bf16[64,1024]{1,0:T(8,128)(2,1)S(1)}, u32[]{:S(2)}, u32[]{:S(2)}) collective-permute-start(bf16[64,1024]{1,0:T(8,128)(2,1)} %own.2), channel_id=1, source_target_pairs={{0,1},{1,0},{2,3},{3,2},{4,5},{5,4},{6,7},{7,6},{8,9},{9,8},{10,11... | collective-permute-start | bytes 393224 | tf_op jit(solution)/shard_map/ppermute | solution.py:313
  7.8 4.0 %collective-permute-start.7 = (bf16[64,128]{1,0:T(8,128)(2,1)}, bf16[64,128]{1,0:T(8,128)(2,1)S(1)}, u32[]{:S(2)}, u32[]{:S(2)}) collective-permute-start(bf16[64,128]{1,0:T(8,128)(2,1)} %own.3), channel_id=1, source_target_pairs={{0,2},{2,0},{4,6},{6,4},{8,10},{10,8},{12,14},{14,12},{1,3},{3,1},... | collective-permute-start | bytes 49160 | tf_op jit(solution)/shard_map/ppermute | solution.py:314
  12.5 11.2 %collective-permute-start.10 = (bf16[128,128]{1,0:T(8,128)(2,1)S(1)}, bf16[128,128]{1,0:T(8,128)(2,1)S(1)}, u32[]{:S(2)}, u32[]{:S(2)}) collective-permute-start(bf16[128,128]{1,0:T(8,128)(2,1)S(1)} %shard_map.105.refs_0_), channel_id=1, source_target_pairs={{0,12},{2,14},{4,8},{6,10},{8,4},{10,6},{12,0},{14,2},{1,13},{3,15... | collective-permute-start | bytes 98312 | tf_op jit(solution)/shard_map/ppermute | solution.py:314
  16.3 7.3 %collective-permute-start.8 = (bf16[128,128]{1,0:T(8,128)(2,1)S(1)}, bf16[128,128]{1,0:T(8,128)(2,1)S(1)}, u32[]{:S(2)}, u32[]{:S(2)}) collective-permute-start(bf16[128,128]{1,0:T(8,128)(2,1)S(1)} %shard_map.105.refs_0_), channel_id=1, source_target_pairs={{0,4},{2,6},{4,0},{6,2},{8,12},{10,14},{12,8},{14,10},{1,5},{3,7},... | collective-permute-start | bytes 98312 | tf_op jit(solution)/shard_map/ppermute | solution.py:314
  20.1 4.9 %collective-permute-start.9 = (bf16[128,128]{1,0:T(8,128)(2,1)S(1)}, bf16[128,128]{1,0:T(8,128)(2,1)S(1)}, u32[]{:S(2)}, u32[]{:S(2)}) collective-permute-start(bf16[128,128]{1,0:T(8,128)(2,1)S(1)} %shard_map.105.refs_0_), channel_id=1, source_target_pairs={{0,8},{2,10},{4,12},{6,14},{8,0},{10,2},{12,4},{14,6},{1,9},{3,11}... | collective-permute-start | bytes 98312 | tf_op jit(solution)/shard_map/ppermute | solution.py:314
  21.1 12.3 %collective-permute-start.3 = (bf16[256,1152]{1,0:T(8,128)(2,1)S(1)}, bf16[256,1152]{1,0:T(8,128)(2,1)S(1)}, u32[]{:S(2)}, u32[]{:S(2)}) collective-permute-start(bf16[256,1152]{1,0:T(8,128)(2,1)S(1)} %shard_map.103.near_a), channel_id=1, source_target_pairs={{0,2},{2,0},{4,6},{6,4},{8,10},{10,8},{12,14},{14,12},{1,3},{3,1},... | collective-permute-start | bytes 1769480 | tf_op jit(solution)/shard_map/ppermute | solution.py:314
  27.2 12.1 %all-to-all-start = ((bf16[8,64,128]{2,1,0:T(8,128)(2,1)}), bf16[8,64,128]{2,1,0:T(8,128)(2,1)S(1)}, u32[]{:S(2)}, u32[]{:S(2)}) async-start(bf16[8,64,128]{2,1,0:T(8,128)(2,1)} %get-tuple-element.22), calls=%async_computation | async-start | bytes 262144 | tf_op jit(solution)/shard_map/all_to_all | solution.py:315
  32.0 8.7 %collective-permute-start.4 = (bf16[256,1152]{1,0:T(8,128)(2,1)S(1)}, bf16[256,1152]{1,0:T(8,128)(2,1)S(1)}, u32[]{:S(2)}, u32[]{:S(2)}) collective-permute-start(bf16[256,1152]{1,0:T(8,128)(2,1)S(1)} %shard_map.103.near_a), channel_id=1, source_target_pairs={{0,1},{1,0},{2,3},{3,2},{4,5},{5,4},{6,7},{7,6},{8,9},{9,8},{10,11... | collective-permute-start | bytes 1769480 | tf_op jit(solution)/shard_map/ppermute | solution.py:313
  33.4 7.2 %collective-permute-start.5 = (bf16[256,1152]{1,0:T(8,128)(2,1)S(1)}, bf16[256,1152]{1,0:T(8,128)(2,1)S(1)}, u32[]{:S(2)}, u32[]{:S(2)}) collective-permute-start(bf16[256,1152]{1,0:T(8,128)(2,1)S(1)} %collective-permute-done.3.near_b), channel_id=1, source_target_pairs={{0,1},{1,0},{2,3},{3,2},{4,5},{5,4},{6,7},{7,6},{8,9},{9,8},{10,11... | collective-permute-start | bytes 1769480 | tf_op jit(solution)/shard_map/ppermute | solution.py:313
  34.3 5.0 %collective-permute-start.12 = (bf16[64,1024]{0,1:T(8,128)(2,1)}, bf16[64,1024]{0,1:T(8,128)(2,1)}, u32[]{:S(2)}, u32[]{:S(2)}) collective-permute-start(bf16[64,1024]{0,1:T(8,128)(2,1)} %copy.14), channel_id=1, source_target_pairs={{0,1},{1,0},{2,3},{3,2},{4,5},{5,4},{6,7},{7,6},{8,9},{9,8},{10,11... | collective-permute-start | bytes 393224 | tf_op jit(solution)/shard_map/ppermute | solution.py:313
  50.0 2.7 %collective-permute-start.14 = (bf16[512,1024]{1,0:T(8,128)(2,1)S(1)}, bf16[512,1024]{1,0:T(8,128)(2,1)S(1)}, u32[]{:S(2)}, u32[]{:S(2)}) collective-permute-start(bf16[512,1024]{1,0:T(8,128)(2,1)S(1)} %get-tuple-element.26), channel_id=1, source_target_pairs={{0,1},{1,0},{2,3},{3,2},{4,5},{5,4},{6,7},{7,6},{8,9},{9,8},{10,11... | collective-permute-start | bytes 3145736 | tf_op jit(solution)/shard_map/ppermute | solution.py:313
  50.4 33.6 %collective-permute-start.21 = (bf16[64,1024]{1,0:T(8,128)(2,1)}, bf16[64,1024]{1,0:T(8,128)(2,1)}, u32[]{:S(2)}, u32[]{:S(2)}) collective-permute-start(bf16[64,1024]{1,0:T(8,128)(2,1)} %get-tuple-element.39.own), channel_id=1, source_target_pairs={{0,1},{1,0},{2,3},{3,2},{4,5},{5,4},{6,7},{7,6},{8,9},{9,8},{10,11... | collective-permute-start | bytes 393224 | tf_op jit(solution)/shard_map/ppermute | solution.py:313
  50.6 3.4 %collective-permute-start.13 = (bf16[8,64,128]{2,1,0:T(8,128)(2,1)S(1)}, bf16[8,64,128]{2,1,0:T(8,128)(2,1)S(1)}, u32[]{:S(2)}, u32[]{:S(2)}) collective-permute-start(bf16[8,64,128]{2,1,0:T(8,128)(2,1)S(1)} %get-tuple-element.24), channel_id=1, source_target_pairs={{0,1},{1,0},{2,3},{3,2},{4,5},{5,4},{6,7},{7,6},{8,9},{9,8},{10,11... | collective-permute-start | bytes 393224 | tf_op jit(solution)/shard_map/ppermute | solution.py:313
  53.2 17.7 %collective-permute-start.16 = (bf16[256,1024]{1,0:T(8,128)(2,1)S(1)}, bf16[256,1024]{1,0:T(8,128)(2,1)S(1)}, u32[]{:S(2)}, u32[]{:S(2)}) collective-permute-start(bf16[256,1024]{1,0:T(8,128)(2,1)S(1)} %shard_map.108.after), channel_id=1, source_target_pairs={{0,2},{2,0},{4,6},{6,4},{8,10},{10,8},{12,14},{14,12},{1,3},{3,1},... | collective-permute-start | bytes 1572872 | tf_op jit(solution)/shard_map/ppermute | solution.py:314
  54.9 14.4 %all-to-all-start.1 = ((bf16[8,64,128]{2,1,0:T(8,128)(2,1)}), bf16[8,64,128]{2,1,0:T(8,128)(2,1)S(1)}, u32[]{:S(2)}, u32[]{:S(2)}) async-start(bf16[8,64,128]{2,1,0:T(8,128)(2,1)} %shard_map.110), calls=%async_computation.1 | async-start | bytes 262144 | tf_op jit(solution)/shard_map/all_to_all | solution.py:315
  69.2 7.9 %collective-permute-start.15 = (bf16[8,64,128]{2,1,0:T(8,128)(2,1)}, bf16[8,64,128]{2,1,0:T(8,128)(2,1)S(1)}, u32[]{:S(2)}, u32[]{:S(2)}) collective-permute-start(bf16[8,64,128]{2,1,0:T(8,128)(2,1)} %get-tuple-element.31), channel_id=1, source_target_pairs={{0,1},{1,0},{2,3},{3,2},{4,5},{5,4},{6,7},{7,6},{8,9},{9,8},{10,11... | collective-permute-start | bytes 393224 | tf_op jit(solution)/shard_map/ppermute | solution.py:313
  70.3 13.7 %collective-permute-start.20 = (f32[64,128]{1,0:T(8,128)S(1)}, f32[64,128]{1,0:T(8,128)S(1)}, u32[]{:S(2)}, u32[]{:S(2)}) collective-permute-start(f32[64,128]{1,0:T(8,128)S(1)} %get-tuple-element.38.mine), channel_id=1, source_target_pairs={{0,1},{1,0},{2,3},{3,2},{4,5},{5,4},{6,7},{7,6},{8,9},{9,8},{10,11... | collective-permute-start | bytes 98312 | tf_op jit(solution)/shard_map/ppermute | solution.py:313
  72.6 13.4 %collective-permute-start.17 = (bf16[64,1024]{1,0:T(8,128)(2,1)S(1)}, bf16[64,1024]{1,0:T(8,128)(2,1)S(1)}, u32[]{:S(2)}, u32[]{:S(2)}) collective-permute-start(bf16[64,1024]{1,0:T(8,128)(2,1)S(1)} %get-tuple-element.33.after), channel_id=1, source_target_pairs={{0,4},{2,6},{4,0},{6,2},{8,12},{10,14},{12,8},{14,10},{1,5},{3,7},... | collective-permute-start | bytes 393224 | tf_op jit(solution)/shard_map/ppermute | solution.py:314
  74.7 13.0 %collective-permute-start.18 = (bf16[64,1024]{1,0:T(8,128)(2,1)S(1)}, bf16[64,1024]{1,0:T(8,128)(2,1)S(1)}, u32[]{:S(2)}, u32[]{:S(2)}) collective-permute-start(bf16[64,1024]{1,0:T(8,128)(2,1)S(1)} %get-tuple-element.36), channel_id=1, source_target_pairs={{0,8},{2,10},{4,12},{6,14},{8,0},{10,2},{12,4},{14,6},{1,9},{3,11}... | collective-permute-start | bytes 393224 | tf_op jit(solution)/shard_map/ppermute | solution.py:314
  77.1 10.5 %collective-permute-start.19 = (bf16[64,1024]{1,0:T(8,128)(2,1)S(1)}, bf16[64,1024]{1,0:T(8,128)(2,1)S(1)}, u32[]{:S(2)}, u32[]{:S(2)}) collective-permute-start(bf16[64,1024]{1,0:T(8,128)(2,1)S(1)} %get-tuple-element.37), channel_id=1, source_target_pairs={{0,12},{2,14},{4,8},{6,10},{8,4},{10,6},{12,0},{14,2},{1,13},{3,15... | collective-permute-start | bytes 393224 | tf_op jit(solution)/shard_map/ppermute | solution.py:314
  78.1 16.8 %all-to-all-start.2 = ((bf16[8,64,256]{2,1,0:T(8,128)(2,1)}), bf16[8,64,256]{2,1,0:T(8,128)(2,1)S(1)}, u32[]{:S(2)}, u32[]{:S(2)}) async-start(bf16[8,64,256]{2,1,0:T(8,128)(2,1)} %shard_map.115.after), calls=%async_computation.2 | async-start | bytes 524288 | tf_op jit(solution)/shard_map/all_to_all | solution.py:315
  (17 other events, 120.8 us)

commit v6 on v5

--- a/solution.py
+++ b/solution.py
@@ -425,7 +425,7 @@
         functools.partial(grad_out_kernel, scale_b), [((rows, width), F32)], [], cost(1, 1),
         "svvvva" + "v", core_ref, total, swap_core(total), wide_own, wide_other, keep,
     )
-    codes = [move(code, 2 * (k + 1)) for k, code in enumerate(codes)]
+    codes = [move(codes[k], 2 * (k + 1)) for k in reversed(range(len(codes)))]
     (grad_mid,) = call(
         last_kernel, [(wide_row, F32)], [], cost(1, 1), "v" * n_hi + "v", keep, *codes
     )

time: 96.4 us -> 96.1 us (level)
    ppermute x12, waiting for transfers between devices: 9.82 us -> 15.2 us  [per_device(): lax.ppermute(v, 'pts', [(i, i ^ mask) for i in range(n_pts)])]
    all_to_all x3, waiting for transfers between devices: 10.5 us -> 5.68 us  [per_device(): exchange = lambda v: lax.all_to_all(v, 'pts', 0, 0, tiled=True)]
where the time goes in v6:
time: 96.1 us; the launch traced here: 95.4 us
  starting transfers between devices  35.9 us (37%)
  Pallas kernels  27.7 us (29%)
  waiting for transfers between devices  22.9 us (24%)
  local copies, waits for them, and re-layouts  6.23 us (6%)
  other arithmetic  1.8 us (2%)
    pallas_call x18, Pallas kernels, call(): pl.pallas_call(kernel, in_specs=specs[:len(args)], out_specs=specs[len(ar...  27.7 us
    ppermute x12, starting transfers between devices, per_device(): lax.ppermute(v, 'pts', [(i, i ^ mask) for i in range(n_pts)])  17.6 us
    all_to_all x3, starting transfers between devices, per_device(): exchange = lambda v: lax.all_to_all(v, 'pts', 0, 0, tiled=True)  16.2 us
    ppermute x12, waiting for transfers between devices, per_device(): lax.ppermute(v, 'pts', [(i, i ^ mask) for i in range(n_pts)])  15.2 us
    unnamed x34, local copies, waits for them, and re-layouts  6.2 us
    all_to_all x3, waiting for transfers between devices, per_device(): exchange = lambda v: lax.all_to_all(v, 'pts', 0, 0, tiled=True)  5.68 us
    ppermute x10, starting transfers between devices, per_device(): swap_core = lambda v: lax.ppermute(v, 'maps', [(0, 1), (1, 0)])  2.02 us
    ppermute x10, waiting for transfers between devices, per_device(): swap_core = lambda v: lax.ppermute(v, 'maps', [(0, 1), (1, 0)])  2.02 us
  transfers between devices with their start and end apart: 25, of which 9 were waited for; matrix products, arithmetic and copies ran while one was open for 3% of the time, Pallas kernels for 17%

profile of v6, /device:TPU:0, one launch (start us, length us, event | category | flops | bytes accessed | tf_op | source)
XLA Modules:
  0.0 95.4 jit_solution(4267497876590526533)
XLA Ops:
  0.6 1.6 %shard_map.102.refs_0_.after = bf16[64,1152]{1,0:T(8,128)(2,1)} custom-call(bf16[64,1024]{1,0:T(8,128)(2,1)} %refs_0_.1, bf16[64,128]{1,0:T(8,128)(2,1)} %refs_1_.1), custom_call_target="tpu_custom_call" | custom-call | flops 1 | bytes 1 | tf_op jit(solution)/shard_map/pallas_call | solution.py:290
  2.2 3.0 %collective-permute-start = (bf16[64,1152]{1,0:T(8,128)(2,1)}, bf16[64,1152]{1,0:T(8,128)(2,1)S(1)}, u32[]{:S(2)}, u32[]{:S(2)}) collective-permute-start(bf16[64,1152]{1,0:T(8,128)(2,1)} %shard_map.102.refs_0_.after), channel_id=1, source_target_pairs={{0,4},{2,6},{4,0},{6,2},{8,12},{10,14},{12,8},{14,10},{1,5},{3,7},... | collective-permute-start | bytes 442376 | tf_op jit(solution)/shard_map/ppermute | solution.py:314
  5.2 2.6 %collective-permute-start.1 = (bf16[64,1152]{1,0:T(8,128)(2,1)}, bf16[64,1152]{1,0:T(8,128)(2,1)S(1)}, u32[]{:S(2)}, u32[]{:S(2)}) collective-permute-start(bf16[64,1152]{1,0:T(8,128)(2,1)} %shard_map.102.refs_0_.after), channel_id=1, source_target_pairs={{0,8},{2,10},{4,12},{6,14},{8,0},{10,2},{12,4},{14,6},{1,9},{3,11}... | collective-permute-start | bytes 442376 | tf_op jit(solution)/shard_map/ppermute | solution.py:314
  7.8 1.7 %collective-permute-start.7 = (bf16[64,128]{1,0:T(8,128)(2,1)}, bf16[64,128]{1,0:T(8,128)(2,1)S(1)}, u32[]{:S(2)}, u32[]{:S(2)}) collective-permute-start(bf16[64,128]{1,0:T(8,128)(2,1)} %own.3), channel_id=1, source_target_pairs={{0,2},{2,0},{4,6},{6,4},{8,10},{10,8},{12,14},{14,12},{1,3},{3,1},... | collective-permute-start | bytes 49160 | tf_op jit(solution)/shard_map/ppermute | solution.py:314
  10.2 1.6 %collective-permute-done.7.got = bf16[64,128]{1,0:T(8,128)(2,1)S(1)} collective-permute-done((bf16[64,128]{1,0:T(8,128)(2,1)}, bf16[64,128]{1,0:T(8,128)(2,1)S(1)}, u32[]{:S(2)}, u32[]{:S(2)}) %collective-permute-start.7) | collective-permute-done | bytes 16416 | tf_op jit(solution)/shard_map/ppermute | solution.py:314
  12.5 3.8 %collective-permute-start.10 = (bf16[128,128]{1,0:T(8,128)(2,1)S(1)}, bf16[128,128]{1,0:T(8,128)(2,1)S(1)}, u32[]{:S(2)}, u32[]{:S(2)}) collective-permute-start(bf16[128,128]{1,0:T(8,128)(2,1)S(1)} %shard_map.105.refs_0_), channel_id=1, source_target_pairs={{0,12},{2,14},{4,8},{6,10},{8,4},{10,6},{12,0},{14,2},{1,13},{3,15... | collective-permute-start | bytes 98312 | tf_op jit(solution)/shard_map/ppermute | solution.py:314
  16.3 3.8 %collective-permute-done.1.refs_2_ = bf16[64,1152]{1,0:T(8,128)(2,1)S(1)} collective-permute-done((bf16[64,1152]{1,0:T(8,128)(2,1)}, bf16[64,1152]{1,0:T(8,128)(2,1)S(1)}, u32[]{:S(2)}, u32[]{:S(2)}) %collective-permute-start.1) | collective-permute-done | bytes 147488 | tf_op jit(solution)/shard_map/ppermute | solution.py:314
  21.1 1.6 %collective-permute-start.3 = (bf16[256,1152]{1,0:T(8,128)(2,1)S(1)}, bf16[256,1152]{1,0:T(8,128)(2,1)S(1)}, u32[]{:S(2)}, u32[]{:S(2)}) collective-permute-start(bf16[256,1152]{1,0:T(8,128)(2,1)S(1)} %shard_map.103.near_a), channel_id=1, source_target_pairs={{0,2},{2,0},{4,6},{6,4},{8,10},{10,8},{12,14},{14,12},{1,3},{3,1},... | collective-permute-start | bytes 1769480 | tf_op jit(solution)/shard_map/ppermute | solution.py:314
  23.7 1.3 %collective-permute-done.9.refs_2_ = bf16[128,128]{1,0:T(8,128)(2,1)S(1)} collective-permute-done((bf16[128,128]{1,0:T(8,128)(2,1)S(1)}, bf16[128,128]{1,0:T(8,128)(2,1)S(1)}, u32[]{:S(2)}, u32[]{:S(2)}) %collective-permute-start.9) | collective-permute-done | bytes 32800 | tf_op jit(solution)/shard_map/ppermute | solution.py:314
  25.0 1.4 %shard_map.106 = (bf16[8,64,128]{2,1,0:T(8,128)(2,1)}, bf16[64,1024]{1,0:T(8,128)(2,1)}) custom-call(s32[8]{0:T(128)S(1)} %broadcast_xor_fusion.place_ref, bf16[128,1024]{1,0:T(8,128)(2,1)S(1)} %shard_map.104.w_both, bf16[128,128]{1,0:T(8,128)(2,1)S(1)} %shard_map.105.refs_0_, bf16[128,128]{1,0:T(8,128)(2,1)S(1)} %collective-permute-done.8.refs_1_, ...), custom_call_target="tpu_custom_call" | custom-call | flops 1 | bytes 1 | tf_op jit(solution)/shard_map/pallas_call | solution.py:290
  27.2 4.8 %all-to-all-start = ((bf16[8,64,128]{2,1,0:T(8,128)(2,1)}), bf16[8,64,128]{2,1,0:T(8,128)(2,1)S(1)}, u32[]{:S(2)}, u32[]{:S(2)}) async-start(bf16[8,64,128]{2,1,0:T(8,128)(2,1)} %get-tuple-element.22), calls=%async_computation | async-start | bytes 262144 | tf_op jit(solution)/shard_map/all_to_all | solution.py:315
  32.0 1.5 %collective-permute-done.3.near_b = bf16[256,1152]{1,0:T(8,128)(2,1)S(1)} collective-permute-done((bf16[256,1152]{1,0:T(8,128)(2,1)S(1)}, bf16[256,1152]{1,0:T(8,128)(2,1)S(1)}, u32[]{:S(2)}, u32[]{:S(2)}) %collective-permute-start.3) | collective-permute-done | bytes 589856 | tf_op jit(solution)/shard_map/ppermute | solution.py:314
  35.0 4.3 %all-to-all-done.b_own = bf16[8,64,128]{2,1,0:T(8,128)(2,1)S(1)} async-done(((bf16[8,64,128]{2,1,0:T(8,128)(2,1)}), bf16[8,64,128]{2,1,0:T(8,128)(2,1)S(1)}, u32[]{:S(2)}, u32[]{:S(2)}) %all-to-all-start) | async-done | bytes 131104 | tf_op jit(solution)/shard_map/all_to_all | solution.py:315
  40.7 9.3 %shard_map.107 = (bf16[512,1024]{1,0:T(8,128)(2,1)S(1)}, f32[512,1024]{1,0:T(8,128)S(1)}, f32[8,64,128]{2,1,0:T(8,128)S(1)}, bf16[8,64,128]{2,1,0:T(8,128)(2,1)S(1)}, bf16[1024,1024]{1,0:T(8,128)(2,1)}) custom-call(s32[1]{0:T(128)} %bitcast.core_ref, bf16[1024,128]{1,0:T(8,128)(2,1)S(1)} %copy-done.13, bf16[256,1152]{1,0:T(8,128)(2,1)S(1)} %shard_map.103.near_a, ...), custom_call_target="tpu_custom_call" | custom-call | flops 49999998976 | bytes 8000000 | tf_op jit(solution)/shard_map/pallas_call | solution.py:290
  50.9 1.8 %collective-permute-done.14.got = bf16[512,1024]{1,0:T(8,128)(2,1)S(1)} collective-permute-done((bf16[512,1024]{1,0:T(8,128)(2,1)S(1)}, bf16[512,1024]{1,0:T(8,128)(2,1)S(1)}, u32[]{:S(2)}, u32[]{:S(2)}) %collective-permute-start.14) | collective-permute-done | bytes 1048608 | tf_op jit(solution)/shard_map/ppermute | solution.py:313
  54.9 6.4 %all-to-all-start.1 = ((bf16[8,64,128]{2,1,0:T(8,128)(2,1)}), bf16[8,64,128]{2,1,0:T(8,128)(2,1)S(1)}, u32[]{:S(2)}, u32[]{:S(2)}) async-start(bf16[8,64,128]{2,1,0:T(8,128)(2,1)} %shard_map.110), calls=%async_computation.1 | async-start | bytes 262144 | tf_op jit(solution)/shard_map/all_to_all | solution.py:315
  61.3 8.0 %shard_map.111 = (f32[8,64,128]{2,1,0:T(8,128)}, bf16[8,64,128]{2,1,0:T(8,128)(2,1)}, f32[8,128]{1,0:T(8,128)}) custom-call(s32[8]{0:T(128)} %copy-done.9, bf16[1024,128]{1,0:T(8,128)(2,1)} %features_in.1, bf16[256,1152]{1,0:T(8,128)(2,1)} %copy-done.5, bf16[256,1152]{1,0:T(8,128)(2,1)} %copy-done.10, bf16[256,1152]{1,0:T(8,128)(2,1)} %copy-done.11, ...), custom_call_target="tpu_custom_call" | custom-call | flops 49999998976 | bytes 8000000 | tf_op jit(solution)/shard_map/pallas_call | solution.py:290
  70.9 1.2 %copy-done.1 = f32[256,1024]{1,0:T(8,128)S(1)} copy-done((f32[256,1024]{1,0:T(8,128)S(1)}, f32[256,1024]{1,0:T(8,128)}, u32[]{:S(2)}) %copy-start.1) | copy-done | bytes 1048600
  72.6 2.1 %collective-permute-start.19 = (bf16[64,1024]{1,0:T(8,128)(2,1)S(1)}, bf16[64,1024]{1,0:T(8,128)(2,1)S(1)}, u32[]{:S(2)}, u32[]{:S(2)}) collective-permute-start(bf16[64,1024]{1,0:T(8,128)(2,1)S(1)} %get-tuple-element.33.after), channel_id=1, source_target_pairs={{0,4},{2,6},{4,0},{6,2},{8,12},{10,14},{12,8},{14,10},{1,5},{3,7},... | collective-permute-start | bytes 393224 | tf_op jit(solution)/shard_map/ppermute | solution.py:314
  74.7 2.4 %collective-permute-start.17 = (bf16[64,1024]{1,0:T(8,128)(2,1)S(1)}, bf16[64,1024]{1,0:T(8,128)(2,1)S(1)}, u32[]{:S(2)}, u32[]{:S(2)}) collective-permute-start(bf16[64,1024]{1,0:T(8,128)(2,1)S(1)} %get-tuple-element.36), channel_id=1, source_target_pairs={{0,12},{2,14},{4,8},{6,10},{8,4},{10,6},{12,0},{14,2},{1,13},{3,15... | collective-permute-start | bytes 393224 | tf_op jit(solution)/shard_map/ppermute | solution.py:314
  78.1 5.0 %all-to-all-start.2 = ((bf16[8,64,256]{2,1,0:T(8,128)(2,1)}), bf16[8,64,256]{2,1,0:T(8,128)(2,1)S(1)}, u32[]{:S(2)}, u32[]{:S(2)}) async-start(bf16[8,64,256]{2,1,0:T(8,128)(2,1)} %shard_map.115.after), calls=%async_computation.2 | async-start | bytes 524288 | tf_op jit(solution)/shard_map/all_to_all | solution.py:315
  83.2 2.0 %shard_map.119 = f32[64,1024]{1,0:T(8,128)} custom-call(s32[1]{0:T(128)} %bitcast.core_ref, f32[64,128]{1,0:T(8,128)S(1)} %get-tuple-element.38.mine, f32[64,128]{1,0:T(8,128)S(1)} %collective-permute-done.20.theirs, bf16[64,1024]{1,0:T(8,128)(2,1)} %get-tuple-element.39.own, bf16[64,1024]{1,0:T(8,128)(2,1)} %collective-permute-done.21.other, ...), custom_call_target="tpu_custom_call" | custom-call | flops 1 | bytes 1 | tf_op jit(solution)/shard_map/pallas_call | solution.py:290
  85.2 7.0 %collective-permute-done.18.refs_1_ = bf16[64,1024]{1,0:T(8,128)(2,1)S(1)} collective-permute-done((bf16[64,1024]{1,0:T(8,128)(2,1)S(1)}, bf16[64,1024]{1,0:T(8,128)(2,1)S(1)}, u32[]{:S(2)}, u32[]{:S(2)}) %collective-permute-start.18) | collective-permute-done | bytes 131104 | tf_op jit(solution)/shard_map/ppermute | solution.py:314
  93.2 1.4 %all-to-all-done.2.got = bf16[8,64,256]{2,1,0:T(8,128)(2,1)S(1)} async-done(((bf16[8,64,256]{2,1,0:T(8,128)(2,1)}), bf16[8,64,256]{2,1,0:T(8,128)(2,1)S(1)}, u32[]{:S(2)}, u32[]{:S(2)}) %all-to-all-start.2) | async-done | bytes 262176 | tf_op jit(solution)/shard_map/all_to_all | solution.py:315
  (82 shorter events, 14.9 us)
Async XLA Ops:
  2.2 14.1 %collective-permute-start = (bf16[64,1152]{1,0:T(8,128)(2,1)}, bf16[64,1152]{1,0:T(8,128)(2,1)S(1)}, u32[]{:S(2)}, u32[]{:S(2)}) collective-permute-start(bf16[64,1152]{1,0:T(8,128)(2,1)} %shard_map.102.refs_0_.after), channel_id=1, source_target_pairs={{0,4},{2,6},{4,0},{6,2},{8,12},{10,14},{12,8},{14,10},{1,5},{3,7},... | collective-permute-start | bytes 442376 | tf_op jit(solution)/shard_map/ppermute | solution.py:314
  5.2 14.9 %collective-permute-start.1 = (bf16[64,1152]{1,0:T(8,128)(2,1)}, bf16[64,1152]{1,0:T(8,128)(2,1)S(1)}, u32[]{:S(2)}, u32[]{:S(2)}) collective-permute-start(bf16[64,1152]{1,0:T(8,128)(2,1)} %shard_map.102.refs_0_.after), channel_id=1, source_target_pairs={{0,8},{2,10},{4,12},{6,14},{8,0},{10,2},{12,4},{14,6},{1,9},{3,11}... | collective-permute-start | bytes 442376 | tf_op jit(solution)/shard_map/ppermute | solution.py:314
  7.8 12.3 %collective-permute-start.2 = (bf16[64,1152]{1,0:T(8,128)(2,1)}, bf16[64,1152]{1,0:T(8,128)(2,1)S(1)}, u32[]{:S(2)}, u32[]{:S(2)}) collective-permute-start(bf16[64,1152]{1,0:T(8,128)(2,1)} %shard_map.102.refs_0_.after), channel_id=1, source_target_pairs={{0,12},{2,14},{4,8},{6,10},{8,4},{10,6},{12,0},{14,2},{1,13},{3,15... | collective-permute-start | bytes 442376 | tf_op jit(solution)/shard_map/ppermute | solution.py:314
  7.8 14.9 %collective-permute-start.6 = (bf16[64,1024]{1,0:T(8,128)(2,1)}, bf16[64,1024]{1,0:T(8,128)(2,1)S(1)}, u32[]{:S(2)}, u32[]{:S(2)}) collective-permute-start(bf16[64,1024]{1,0:T(8,128)(2,1)} %own.2), channel_id=1, source_target_pairs={{0,1},{1,0},{2,3},{3,2},{4,5},{5,4},{6,7},{7,6},{8,9},{9,8},{10,11... | collective-permute-start | bytes 393224 | tf_op jit(solution)/shard_map/ppermute | solution.py:313
  7.8 4.0 %collective-permute-start.7 = (bf16[64,128]{1,0:T(8,128)(2,1)}, bf16[64,128]{1,0:T(8,128)(2,1)S(1)}, u32[]{:S(2)}, u32[]{:S(2)}) collective-permute-start(bf16[64,128]{1,0:T(8,128)(2,1)} %own.3), channel_id=1, source_target_pairs={{0,2},{2,0},{4,6},{6,4},{8,10},{10,8},{12,14},{14,12},{1,3},{3,1},... | collective-permute-start | bytes 49160 | tf_op jit(solution)/shard_map/ppermute | solution.py:314
  12.5 11.2 %collective-permute-start.10 = (bf16[128,128]{1,0:T(8,128)(2,1)S(1)}, bf16[128,128]{1,0:T(8,128)(2,1)S(1)}, u32[]{:S(2)}, u32[]{:S(2)}) collective-permute-start(bf16[128,128]{1,0:T(8,128)(2,1)S(1)} %shard_map.105.refs_0_), channel_id=1, source_target_pairs={{0,12},{2,14},{4,8},{6,10},{8,4},{10,6},{12,0},{14,2},{1,13},{3,15... | collective-permute-start | bytes 98312 | tf_op jit(solution)/shard_map/ppermute | solution.py:314
  16.3 7.3 %collective-permute-start.8 = (bf16[128,128]{1,0:T(8,128)(2,1)S(1)}, bf16[128,128]{1,0:T(8,128)(2,1)S(1)}, u32[]{:S(2)}, u32[]{:S(2)}) collective-permute-start(bf16[128,128]{1,0:T(8,128)(2,1)S(1)} %shard_map.105.refs_0_), channel_id=1, source_target_pairs={{0,4},{2,6},{4,0},{6,2},{8,12},{10,14},{12,8},{14,10},{1,5},{3,7},... | collective-permute-start | bytes 98312 | tf_op jit(solution)/shard_map/ppermute | solution.py:314
  20.1 4.9 %collective-permute-start.9 = (bf16[128,128]{1,0:T(8,128)(2,1)S(1)}, bf16[128,128]{1,0:T(8,128)(2,1)S(1)}, u32[]{:S(2)}, u32[]{:S(2)}) collective-permute-start(bf16[128,128]{1,0:T(8,128)(2,1)S(1)} %shard_map.105.refs_0_), channel_id=1, source_target_pairs={{0,8},{2,10},{4,12},{6,14},{8,0},{10,2},{12,4},{14,6},{1,9},{3,11}... | collective-permute-start | bytes 98312 | tf_op jit(solution)/shard_map/ppermute | solution.py:314
  21.1 12.3 %collective-permute-start.3 = (bf16[256,1152]{1,0:T(8,128)(2,1)S(1)}, bf16[256,1152]{1,0:T(8,128)(2,1)S(1)}, u32[]{:S(2)}, u32[]{:S(2)}) collective-permute-start(bf16[256,1152]{1,0:T(8,128)(2,1)S(1)} %shard_map.103.near_a), channel_id=1, source_target_pairs={{0,2},{2,0},{4,6},{6,4},{8,10},{10,8},{12,14},{14,12},{1,3},{3,1},... | collective-permute-start | bytes 1769480 | tf_op jit(solution)/shard_map/ppermute | solution.py:314
  27.2 12.1 %all-to-all-start = ((bf16[8,64,128]{2,1,0:T(8,128)(2,1)}), bf16[8,64,128]{2,1,0:T(8,128)(2,1)S(1)}, u32[]{:S(2)}, u32[]{:S(2)}) async-start(bf16[8,64,128]{2,1,0:T(8,128)(2,1)} %get-tuple-element.22), calls=%async_computation | async-start | bytes 262144 | tf_op jit(solution)/shard_map/all_to_all | solution.py:315
  32.0 8.7 %collective-permute-start.4 = (bf16[256,1152]{1,0:T(8,128)(2,1)S(1)}, bf16[256,1152]{1,0:T(8,128)(2,1)S(1)}, u32[]{:S(2)}, u32[]{:S(2)}) collective-permute-start(bf16[256,1152]{1,0:T(8,128)(2,1)S(1)} %shard_map.103.near_a), channel_id=1, source_target_pairs={{0,1},{1,0},{2,3},{3,2},{4,5},{5,4},{6,7},{7,6},{8,9},{9,8},{10,11... | collective-permute-start | bytes 1769480 | tf_op jit(solution)/shard_map/ppermute | solution.py:313
  33.4 7.2 %collective-permute-start.5 = (bf16[256,1152]{1,0:T(8,128)(2,1)S(1)}, bf16[256,1152]{1,0:T(8,128)(2,1)S(1)}, u32[]{:S(2)}, u32[]{:S(2)}) collective-permute-start(bf16[256,1152]{1,0:T(8,128)(2,1)S(1)} %collective-permute-done.3.near_b), channel_id=1, source_target_pairs={{0,1},{1,0},{2,3},{3,2},{4,5},{5,4},{6,7},{7,6},{8,9},{9,8},{10,11... | collective-permute-start | bytes 1769480 | tf_op jit(solution)/shard_map/ppermute | solution.py:313
  34.3 5.0 %collective-permute-start.12 = (bf16[64,1024]{0,1:T(8,128)(2,1)}, bf16[64,1024]{0,1:T(8,128)(2,1)}, u32[]{:S(2)}, u32[]{:S(2)}) collective-permute-start(bf16[64,1024]{0,1:T(8,128)(2,1)} %copy.14), channel_id=1, source_target_pairs={{0,1},{1,0},{2,3},{3,2},{4,5},{5,4},{6,7},{7,6},{8,9},{9,8},{10,11... | collective-permute-start | bytes 393224 | tf_op jit(solution)/shard_map/ppermute | solution.py:313
  50.0 2.7 %collective-permute-start.14 = (bf16[512,1024]{1,0:T(8,128)(2,1)S(1)}, bf16[512,1024]{1,0:T(8,128)(2,1)S(1)}, u32[]{:S(2)}, u32[]{:S(2)}) collective-permute-start(bf16[512,1024]{1,0:T(8,128)(2,1)S(1)} %get-tuple-element.26), channel_id=1, source_target_pairs={{0,1},{1,0},{2,3},{3,2},{4,5},{5,4},{6,7},{7,6},{8,9},{9,8},{10,11... | collective-permute-start | bytes 3145736 | tf_op jit(solution)/shard_map/ppermute | solution.py:313
  50.4 32.8 %collective-permute-start.21 = (bf16[64,1024]{1,0:T(8,128)(2,1)}, bf16[64,1024]{1,0:T(8,128)(2,1)}, u32[]{:S(2)}, u32[]{:S(2)}) collective-permute-start(bf16[64,1024]{1,0:T(8,128)(2,1)} %get-tuple-element.39.own), channel_id=1, source_target_pairs={{0,1},{1,0},{2,3},{3,2},{4,5},{5,4},{6,7},{7,6},{8,9},{9,8},{10,11... | collective-permute-start | bytes 393224 | tf_op jit(solution)/shard_map/ppermute | solution.py:313
  50.6 3.4 %collective-permute-start.13 = (bf16[8,64,128]{2,1,0:T(8,128)(2,1)S(1)}, bf16[8,64,128]{2,1,0:T(8,128)(2,1)S(1)}, u32[]{:S(2)}, u32[]{:S(2)}) collective-permute-start(bf16[8,64,128]{2,1,0:T(8,128)(2,1)S(1)} %get-tuple-element.24), channel_id=1, source_target_pairs={{0,1},{1,0},{2,3},{3,2},{4,5},{5,4},{6,7},{7,6},{8,9},{9,8},{10,11... | collective-permute-start | bytes 393224 | tf_op jit(solution)/shard_map/ppermute | solution.py:313
  53.2 17.7 %collective-permute-start.16 = (bf16[256,1024]{1,0:T(8,128)(2,1)S(1)}, bf16[256,1024]{1,0:T(8,128)(2,1)S(1)}, u32[]{:S(2)}, u32[]{:S(2)}) collective-permute-start(bf16[256,1024]{1,0:T(8,128)(2,1)S(1)} %shard_map.108.after), channel_id=1, source_target_pairs={{0,2},{2,0},{4,6},{6,4},{8,10},{10,8},{12,14},{14,12},{1,3},{3,1},... | collective-permute-start | bytes 1572872 | tf_op jit(solution)/shard_map/ppermute | solution.py:314
  54.9 14.4 %all-to-all-start.1 = ((bf16[8,64,128]{2,1,0:T(8,128)(2,1)}), bf16[8,64,128]{2,1,0:T(8,128)(2,1)S(1)}, u32[]{:S(2)}, u32[]{:S(2)}) async-start(bf16[8,64,128]{2,1,0:T(8,128)(2,1)} %shard_map.110), calls=%async_computation.1 | async-start | bytes 262144 | tf_op jit(solution)/shard_map/all_to_all | solution.py:315
  69.2 7.9 %collective-permute-start.15 = (bf16[8,64,128]{2,1,0:T(8,128)(2,1)}, bf16[8,64,128]{2,1,0:T(8,128)(2,1)S(1)}, u32[]{:S(2)}, u32[]{:S(2)}) collective-permute-start(bf16[8,64,128]{2,1,0:T(8,128)(2,1)} %get-tuple-element.31), channel_id=1, source_target_pairs={{0,1},{1,0},{2,3},{3,2},{4,5},{5,4},{6,7},{7,6},{8,9},{9,8},{10,11... | collective-permute-start | bytes 393224 | tf_op jit(solution)/shard_map/ppermute | solution.py:313
  70.3 12.8 %collective-permute-start.20 = (f32[64,128]{1,0:T(8,128)S(1)}, f32[64,128]{1,0:T(8,128)S(1)}, u32[]{:S(2)}, u32[]{:S(2)}) collective-permute-start(f32[64,128]{1,0:T(8,128)S(1)} %get-tuple-element.38.mine), channel_id=1, source_target_pairs={{0,1},{1,0},{2,3},{3,2},{4,5},{5,4},{6,7},{7,6},{8,9},{9,8},{10,11... | collective-permute-start | bytes 98312 | tf_op jit(solution)/shard_map/ppermute | solution.py:313
  72.6 19.6 %collective-permute-start.19 = (bf16[64,1024]{1,0:T(8,128)(2,1)S(1)}, bf16[64,1024]{1,0:T(8,128)(2,1)S(1)}, u32[]{:S(2)}, u32[]{:S(2)}) collective-permute-start(bf16[64,1024]{1,0:T(8,128)(2,1)S(1)} %get-tuple-element.33.after), channel_id=1, source_target_pairs={{0,4},{2,6},{4,0},{6,2},{8,12},{10,14},{12,8},{14,10},{1,5},{3,7},... | collective-permute-start | bytes 393224 | tf_op jit(solution)/shard_map/ppermute | solution.py:314
  74.7 10.5 %collective-permute-start.17 = (bf16[64,1024]{1,0:T(8,128)(2,1)S(1)}, bf16[64,1024]{1,0:T(8,128)(2,1)S(1)}, u32[]{:S(2)}, u32[]{:S(2)}) collective-permute-start(bf16[64,1024]{1,0:T(8,128)(2,1)S(1)} %get-tuple-element.36), channel_id=1, source_target_pairs={{0,12},{2,14},{4,8},{6,10},{8,4},{10,6},{12,0},{14,2},{1,13},{3,15... | collective-permute-start | bytes 393224 | tf_op jit(solution)/shard_map/ppermute | solution.py:314
  77.1 15.1 %collective-permute-start.18 = (bf16[64,1024]{1,0:T(8,128)(2,1)S(1)}, bf16[64,1024]{1,0:T(8,128)(2,1)S(1)}, u32[]{:S(2)}, u32[]{:S(2)}) collective-permute-start(bf16[64,1024]{1,0:T(8,128)(2,1)S(1)} %get-tuple-element.37), channel_id=1, source_target_pairs={{0,8},{2,10},{4,12},{6,14},{8,0},{10,2},{12,4},{14,6},{1,9},{3,11}... | collective-permute-start | bytes 393224 | tf_op jit(solution)/shard_map/ppermute | solution.py:314
  78.1 16.5 %all-to-all-start.2 = ((bf16[8,64,256]{2,1,0:T(8,128)(2,1)}), bf16[8,64,256]{2,1,0:T(8,128)(2,1)S(1)}, u32[]{:S(2)}, u32[]{:S(2)}) async-start(bf16[8,64,256]{2,1,0:T(8,128)(2,1)} %shard_map.115.after), calls=%async_computation.2 | async-start | bytes 524288 | tf_op jit(solution)/shard_map/all_to_all | solution.py:315
  (17 other events, 120.8 us)

commit v7 on v6

--- a/solution.py
+++ b/solution.py
@@ -399,7 +399,7 @@
             pltpu.VMEM((points, width), BF), dma((13,)),
         ],
         cost(5e10, 8e6), "shhhhhha" + "vvv", place, features, *mid, dz, own,
-        mib=54,
+        mib=58,
     )
     total, part = call(
         functools.partial(sums_kernel, scale_b),

time: 96.1 us -> 96.1 us (level)
  no operation moved by 1% of the time
where the time goes in v7:
time: 96.1 us; the launch traced here: 95.4 us
  starting transfers between devices  35.9 us (37%)
  Pallas kernels  27.7 us (29%)
  waiting for transfers between devices  22.9 us (24%)
  local copies, waits for them, and re-layouts  6.23 us (6%)
  other arithmetic  1.8 us (2%)
    pallas_call x18, Pallas kernels, call(): pl.pallas_call(kernel, in_specs=specs[:len(args)], out_specs=specs[len(ar...  27.7 us
    ppermute x12, starting transfers between devices, per_device(): lax.ppermute(v, 'pts', [(i, i ^ mask) for i in range(n_pts)])  17.6 us
    all_to_all x3, starting transfers between devices, per_device(): exchange = lambda v: lax.all_to_all(v, 'pts', 0, 0, tiled=True)  16.2 us
    ppermute x12, waiting for transfers between devices, per_device(): lax.ppermute(v, 'pts', [(i, i ^ mask) for i in range(n_pts)])  15.2 us
    unnamed x34, local copies, waits for them, and re-layouts  6.2 us
    all_to_all x3, waiting for transfers between devices, per_device(): exchange = lambda v: lax.all_to_all(v, 'pts', 0, 0, tiled=True)  5.68 us
    ppermute x10, starting transfers between devices, per_device(): swap_core = lambda v: lax.ppermute(v, 'maps', [(0, 1), (1, 0)])  2.02 us
    ppermute x10, waiting for transfers between devices, per_device(): swap_core = lambda v: lax.ppermute(v, 'maps', [(0, 1), (1, 0)])  2.02 us
  transfers between devices with their start and end apart: 25, of which 9 were waited for; matrix products, arithmetic and copies ran while one was open for 3% of the time, Pallas kernels for 17%

profile of v7, /device:TPU:0, one launch (start us, length us, event | category | flops | bytes accessed | tf_op | source)
XLA Modules:
  0.0 95.4 jit_solution(4267497876590526533)
XLA Ops:
  0.6 1.6 %shard_map.102.refs_0_.after = bf16[64,1152]{1,0:T(8,128)(2,1)} custom-call(bf16[64,1024]{1,0:T(8,128)(2,1)} %refs_0_.1, bf16[64,128]{1,0:T(8,128)(2,1)} %refs_1_.1), custom_call_target="tpu_custom_call" | custom-call | flops 1 | bytes 1 | tf_op jit(solution)/shard_map/pallas_call | solution.py:290
  2.2 3.0 %collective-permute-start = (bf16[64,1152]{1,0:T(8,128)(2,1)}, bf16[64,1152]{1,0:T(8,128)(2,1)S(1)}, u32[]{:S(2)}, u32[]{:S(2)}) collective-permute-start(bf16[64,1152]{1,0:T(8,128)(2,1)} %shard_map.102.refs_0_.after), channel_id=1, source_target_pairs={{0,4},{2,6},{4,0},{6,2},{8,12},{10,14},{12,8},{14,10},{1,5},{3,7},... | collective-permute-start | bytes 442376 | tf_op jit(solution)/shard_map/ppermute | solution.py:314
  5.2 2.6 %collective-permute-start.1 = (bf16[64,1152]{1,0:T(8,128)(2,1)}, bf16[64,1152]{1,0:T(8,128)(2,1)S(1)}, u32[]{:S(2)}, u32[]{:S(2)}) collective-permute-start(bf16[64,1152]{1,0:T(8,128)(2,1)} %shard_map.102.refs_0_.after), channel_id=1, source_target_pairs={{0,8},{2,10},{4,12},{6,14},{8,0},{10,2},{12,4},{14,6},{1,9},{3,11}... | collective-permute-start | bytes 442376 | tf_op jit(solution)/shard_map/ppermute | solution.py:314
  7.8 1.7 %collective-permute-start.7 = (bf16[64,128]{1,0:T(8,128)(2,1)}, bf16[64,128]{1,0:T(8,128)(2,1)S(1)}, u32[]{:S(2)}, u32[]{:S(2)}) collective-permute-start(bf16[64,128]{1,0:T(8,128)(2,1)} %own.3), channel_id=1, source_target_pairs={{0,2},{2,0},{4,6},{6,4},{8,10},{10,8},{12,14},{14,12},{1,3},{3,1},... | collective-permute-start | bytes 49160 | tf_op jit(solution)/shard_map/ppermute | solution.py:314
  10.2 1.6 %collective-permute-done.7.got = bf16[64,128]{1,0:T(8,128)(2,1)S(1)} collective-permute-done((bf16[64,128]{1,0:T(8,128)(2,1)}, bf16[64,128]{1,0:T(8,128)(2,1)S(1)}, u32[]{:S(2)}, u32[]{:S(2)}) %collective-permute-start.7) | collective-permute-done | bytes 16416 | tf_op jit(solution)/shard_map/ppermute | solution.py:314
  12.5 3.8 %collective-permute-start.10 = (bf16[128,128]{1,0:T(8,128)(2,1)S(1)}, bf16[128,128]{1,0:T(8,128)(2,1)S(1)}, u32[]{:S(2)}, u32[]{:S(2)}) collective-permute-start(bf16[128,128]{1,0:T(8,128)(2,1)S(1)} %shard_map.105.refs_0_), channel_id=1, source_target_pairs={{0,12},{2,14},{4,8},{6,10},{8,4},{10,6},{12,0},{14,2},{1,13},{3,15... | collective-permute-start | bytes 98312 | tf_op jit(solution)/shard_map/ppermute | solution.py:314
  16.3 3.8 %collective-permute-done.1.refs_2_ = bf16[64,1152]{1,0:T(8,128)(2,1)S(1)} collective-permute-done((bf16[64,1152]{1,0:T(8,128)(2,1)}, bf16[64,1152]{1,0:T(8,128)(2,1)S(1)}, u32[]{:S(2)}, u32[]{:S(2)}) %collective-permute-start.1) | collective-permute-done | bytes 147488 | tf_op jit(solution)/shard_map/ppermute | solution.py:314
  21.1 1.6 %collective-permute-start.3 = (bf16[256,1152]{1,0:T(8,128)(2,1)S(1)}, bf16[256,1152]{1,0:T(8,128)(2,1)S(1)}, u32[]{:S(2)}, u32[]{:S(2)}) collective-permute-start(bf16[256,1152]{1,0:T(8,128)(2,1)S(1)} %shard_map.103.near_a), channel_id=1, source_target_pairs={{0,2},{2,0},{4,6},{6,4},{8,10},{10,8},{12,14},{14,12},{1,3},{3,1},... | collective-permute-start | bytes 1769480 | tf_op jit(solution)/shard_map/ppermute | solution.py:314
  23.7 1.3 %collective-permute-done.9.refs_2_ = bf16[128,128]{1,0:T(8,128)(2,1)S(1)} collective-permute-done((bf16[128,128]{1,0:T(8,128)(2,1)S(1)}, bf16[128,128]{1,0:T(8,128)(2,1)S(1)}, u32[]{:S(2)}, u32[]{:S(2)}) %collective-permute-start.9) | collective-permute-done | bytes 32800 | tf_op jit(solution)/shard_map/ppermute | solution.py:314
  25.0 1.4 %shard_map.106 = (bf16[8,64,128]{2,1,0:T(8,128)(2,1)}, bf16[64,1024]{1,0:T(8,128)(2,1)}) custom-call(s32[8]{0:T(128)S(1)} %broadcast_xor_fusion.place_ref, bf16[128,1024]{1,0:T(8,128)(2,1)S(1)} %shard_map.104.w_both, bf16[128,128]{1,0:T(8,128)(2,1)S(1)} %shard_map.105.refs_0_, bf16[128,128]{1,0:T(8,128)(2,1)S(1)} %collective-permute-done.8.refs_1_, ...), custom_call_target="tpu_custom_call" | custom-call | flops 1 | bytes 1 | tf_op jit(solution)/shard_map/pallas_call | solution.py:290
  27.2 4.8 %all-to-all-start = ((bf16[8,64,128]{2,1,0:T(8,128)(2,1)}), bf16[8,64,128]{2,1,0:T(8,128)(2,1)S(1)}, u32[]{:S(2)}, u32[]{:S(2)}) async-start(bf16[8,64,128]{2,1,0:T(8,128)(2,1)} %get-tuple-element.22), calls=%async_computation | async-start | bytes 262144 | tf_op jit(solution)/shard_map/all_to_all | solution.py:315
  32.0 1.5 %collective-permute-done.3.near_b = bf16[256,1152]{1,0:T(8,128)(2,1)S(1)} collective-permute-done((bf16[256,1152]{1,0:T(8,128)(2,1)S(1)}, bf16[256,1152]{1,0:T(8,128)(2,1)S(1)}, u32[]{:S(2)}, u32[]{:S(2)}) %collective-permute-start.3) | collective-permute-done | bytes 589856 | tf_op jit(solution)/shard_map/ppermute | solution.py:314
  35.0 4.3 %all-to-all-done.b_own = bf16[8,64,128]{2,1,0:T(8,128)(2,1)S(1)} async-done(((bf16[8,64,128]{2,1,0:T(8,128)(2,1)}), bf16[8,64,128]{2,1,0:T(8,128)(2,1)S(1)}, u32[]{:S(2)}, u32[]{:S(2)}) %all-to-all-start) | async-done | bytes 131104 | tf_op jit(solution)/shard_map/all_to_all | solution.py:315
  40.7 9.3 %shard_map.107 = (bf16[512,1024]{1,0:T(8,128)(2,1)S(1)}, f32[512,1024]{1,0:T(8,128)S(1)}, f32[8,64,128]{2,1,0:T(8,128)S(1)}, bf16[8,64,128]{2,1,0:T(8,128)(2,1)S(1)}, bf16[1024,1024]{1,0:T(8,128)(2,1)}) custom-call(s32[1]{0:T(128)} %bitcast.core_ref, bf16[1024,128]{1,0:T(8,128)(2,1)S(1)} %copy-done.13, bf16[256,1152]{1,0:T(8,128)(2,1)S(1)} %shard_map.103.near_a, ...), custom_call_target="tpu_custom_call" | custom-call | flops 49999998976 | bytes 8000000 | tf_op jit(solution)/shard_map/pallas_call | solution.py:290
  50.9 1.8 %collective-permute-done.14.got = bf16[512,1024]{1,0:T(8,128)(2,1)S(1)} collective-permute-done((bf16[512,1024]{1,0:T(8,128)(2,1)S(1)}, bf16[512,1024]{1,0:T(8,128)(2,1)S(1)}, u32[]{:S(2)}, u32[]{:S(2)}) %collective-permute-start.14) | collective-permute-done | bytes 1048608 | tf_op jit(solution)/shard_map/ppermute | solution.py:313
  54.9 6.4 %all-to-all-start.1 = ((bf16[8,64,128]{2,1,0:T(8,128)(2,1)}), bf16[8,64,128]{2,1,0:T(8,128)(2,1)S(1)}, u32[]{:S(2)}, u32[]{:S(2)}) async-start(bf16[8,64,128]{2,1,0:T(8,128)(2,1)} %shard_map.110), calls=%async_computation.1 | async-start | bytes 262144 | tf_op jit(solution)/shard_map/all_to_all | solution.py:315
  61.3 8.0 %shard_map.111 = (f32[8,64,128]{2,1,0:T(8,128)}, bf16[8,64,128]{2,1,0:T(8,128)(2,1)}, f32[8,128]{1,0:T(8,128)}) custom-call(s32[8]{0:T(128)} %copy-done.9, bf16[1024,128]{1,0:T(8,128)(2,1)} %features_in.1, bf16[256,1152]{1,0:T(8,128)(2,1)} %copy-done.5, bf16[256,1152]{1,0:T(8,128)(2,1)} %copy-done.10, bf16[256,1152]{1,0:T(8,128)(2,1)} %copy-done.11, ...), custom_call_target="tpu_custom_call" | custom-call | flops 49999998976 | bytes 8000000 | tf_op jit(solution)/shard_map/pallas_call | solution.py:290
  70.9 1.2 %copy-done.1 = f32[256,1024]{1,0:T(8,128)S(1)} copy-done((f32[256,1024]{1,0:T(8,128)S(1)}, f32[256,1024]{1,0:T(8,128)}, u32[]{:S(2)}) %copy-start.1) | copy-done | bytes 1048600
  72.6 2.1 %collective-permute-start.19 = (bf16[64,1024]{1,0:T(8,128)(2,1)S(1)}, bf16[64,1024]{1,0:T(8,128)(2,1)S(1)}, u32[]{:S(2)}, u32[]{:S(2)}) collective-permute-start(bf16[64,1024]{1,0:T(8,128)(2,1)S(1)} %get-tuple-element.33.after), channel_id=1, source_target_pairs={{0,4},{2,6},{4,0},{6,2},{8,12},{10,14},{12,8},{14,10},{1,5},{3,7},... | collective-permute-start | bytes 393224 | tf_op jit(solution)/shard_map/ppermute | solution.py:314
  74.7 2.4 %collective-permute-start.17 = (bf16[64,1024]{1,0:T(8,128)(2,1)S(1)}, bf16[64,1024]{1,0:T(8,128)(2,1)S(1)}, u32[]{:S(2)}, u32[]{:S(2)}) collective-permute-start(bf16[64,1024]{1,0:T(8,128)(2,1)S(1)} %get-tuple-element.36), channel_id=1, source_target_pairs={{0,12},{2,14},{4,8},{6,10},{8,4},{10,6},{12,0},{14,2},{1,13},{3,15... | collective-permute-start | bytes 393224 | tf_op jit(solution)/shard_map/ppermute | solution.py:314
  78.1 5.0 %all-to-all-start.2 = ((bf16[8,64,256]{2,1,0:T(8,128)(2,1)}), bf16[8,64,256]{2,1,0:T(8,128)(2,1)S(1)}, u32[]{:S(2)}, u32[]{:S(2)}) async-start(bf16[8,64,256]{2,1,0:T(8,128)(2,1)} %shard_map.115.after), calls=%async_computation.2 | async-start | bytes 524288 | tf_op jit(solution)/shard_map/all_to_all | solution.py:315
  83.2 2.0 %shard_map.119 = f32[64,1024]{1,0:T(8,128)} custom-call(s32[1]{0:T(128)} %bitcast.core_ref, f32[64,128]{1,0:T(8,128)S(1)} %get-tuple-element.38.mine, f32[64,128]{1,0:T(8,128)S(1)} %collective-permute-done.20.theirs, bf16[64,1024]{1,0:T(8,128)(2,1)} %get-tuple-element.39.own, bf16[64,1024]{1,0:T(8,128)(2,1)} %collective-permute-done.21.other, ...), custom_call_target="tpu_custom_call" | custom-call | flops 1 | bytes 1 | tf_op jit(solution)/shard_map/pallas_call | solution.py:290
  85.2 7.0 %collective-permute-done.18.refs_1_ = bf16[64,1024]{1,0:T(8,128)(2,1)S(1)} collective-permute-done((bf16[64,1024]{1,0:T(8,128)(2,1)S(1)}, bf16[64,1024]{1,0:T(8,128)(2,1)S(1)}, u32[]{:S(2)}, u32[]{:S(2)}) %collective-permute-start.18) | collective-permute-done | bytes 131104 | tf_op jit(solution)/shard_map/ppermute | solution.py:314
  93.2 1.4 %all-to-all-done.2.got = bf16[8,64,256]{2,1,0:T(8,128)(2,1)S(1)} async-done(((bf16[8,64,256]{2,1,0:T(8,128)(2,1)}), bf16[8,64,256]{2,1,0:T(8,128)(2,1)S(1)}, u32[]{:S(2)}, u32[]{:S(2)}) %all-to-all-start.2) | async-done | bytes 262176 | tf_op jit(solution)/shard_map/all_to_all | solution.py:315
  (82 shorter events, 14.9 us)
Async XLA Ops:
  2.2 14.1 %collective-permute-start = (bf16[64,1152]{1,0:T(8,128)(2,1)}, bf16[64,1152]{1,0:T(8,128)(2,1)S(1)}, u32[]{:S(2)}, u32[]{:S(2)}) collective-permute-start(bf16[64,1152]{1,0:T(8,128)(2,1)} %shard_map.102.refs_0_.after), channel_id=1, source_target_pairs={{0,4},{2,6},{4,0},{6,2},{8,12},{10,14},{12,8},{14,10},{1,5},{3,7},... | collective-permute-start | bytes 442376 | tf_op jit(solution)/shard_map/ppermute | solution.py:314
  5.2 14.9 %collective-permute-start.1 = (bf16[64,1152]{1,0:T(8,128)(2,1)}, bf16[64,1152]{1,0:T(8,128)(2,1)S(1)}, u32[]{:S(2)}, u32[]{:S(2)}) collective-permute-start(bf16[64,1152]{1,0:T(8,128)(2,1)} %shard_map.102.refs_0_.after), channel_id=1, source_target_pairs={{0,8},{2,10},{4,12},{6,14},{8,0},{10,2},{12,4},{14,6},{1,9},{3,11}... | collective-permute-start | bytes 442376 | tf_op jit(solution)/shard_map/ppermute | solution.py:314
  7.8 12.3 %collective-permute-start.2 = (bf16[64,1152]{1,0:T(8,128)(2,1)}, bf16[64,1152]{1,0:T(8,128)(2,1)S(1)}, u32[]{:S(2)}, u32[]{:S(2)}) collective-permute-start(bf16[64,1152]{1,0:T(8,128)(2,1)} %shard_map.102.refs_0_.after), channel_id=1, source_target_pairs={{0,12},{2,14},{4,8},{6,10},{8,4},{10,6},{12,0},{14,2},{1,13},{3,15... | collective-permute-start | bytes 442376 | tf_op jit(solution)/shard_map/ppermute | solution.py:314
  7.8 14.9 %collective-permute-start.6 = (bf16[64,1024]{1,0:T(8,128)(2,1)}, bf16[64,1024]{1,0:T(8,128)(2,1)S(1)}, u32[]{:S(2)}, u32[]{:S(2)}) collective-permute-start(bf16[64,1024]{1,0:T(8,128)(2,1)} %own.2), channel_id=1, source_target_pairs={{0,1},{1,0},{2,3},{3,2},{4,5},{5,4},{6,7},{7,6},{8,9},{9,8},{10,11... | collective-permute-start | bytes 393224 | tf_op jit(solution)/shard_map/ppermute | solution.py:313
  7.8 4.0 %collective-permute-start.7 = (bf16[64,128]{1,0:T(8,128)(2,1)}, bf16[64,128]{1,0:T(8,128)(2,1)S(1)}, u32[]{:S(2)}, u32[]{:S(2)}) collective-permute-start(bf16[64,128]{1,0:T(8,128)(2,1)} %own.3), channel_id=1, source_target_pairs={{0,2},{2,0},{4,6},{6,4},{8,10},{10,8},{12,14},{14,12},{1,3},{3,1},... | collective-permute-start | bytes 49160 | tf_op jit(solution)/shard_map/ppermute | solution.py:314
  12.5 11.2 %collective-permute-start.10 = (bf16[128,128]{1,0:T(8,128)(2,1)S(1)}, bf16[128,128]{1,0:T(8,128)(2,1)S(1)}, u32[]{:S(2)}, u32[]{:S(2)}) collective-permute-start(bf16[128,128]{1,0:T(8,128)(2,1)S(1)} %shard_map.105.refs_0_), channel_id=1, source_target_pairs={{0,12},{2,14},{4,8},{6,10},{8,4},{10,6},{12,0},{14,2},{1,13},{3,15... | collective-permute-start | bytes 98312 | tf_op jit(solution)/shard_map/ppermute | solution.py:314
  16.3 7.3 %collective-permute-start.8 = (bf16[128,128]{1,0:T(8,128)(2,1)S(1)}, bf16[128,128]{1,0:T(8,128)(2,1)S(1)}, u32[]{:S(2)}, u32[]{:S(2)}) collective-permute-start(bf16[128,128]{1,0:T(8,128)(2,1)S(1)} %shard_map.105.refs_0_), channel_id=1, source_target_pairs={{0,4},{2,6},{4,0},{6,2},{8,12},{10,14},{12,8},{14,10},{1,5},{3,7},... | collective-permute-start | bytes 98312 | tf_op jit(solution)/shard_map/ppermute | solution.py:314
  20.1 4.9 %collective-permute-start.9 = (bf16[128,128]{1,0:T(8,128)(2,1)S(1)}, bf16[128,128]{1,0:T(8,128)(2,1)S(1)}, u32[]{:S(2)}, u32[]{:S(2)}) collective-permute-start(bf16[128,128]{1,0:T(8,128)(2,1)S(1)} %shard_map.105.refs_0_), channel_id=1, source_target_pairs={{0,8},{2,10},{4,12},{6,14},{8,0},{10,2},{12,4},{14,6},{1,9},{3,11}... | collective-permute-start | bytes 98312 | tf_op jit(solution)/shard_map/ppermute | solution.py:314
  21.1 12.3 %collective-permute-start.3 = (bf16[256,1152]{1,0:T(8,128)(2,1)S(1)}, bf16[256,1152]{1,0:T(8,128)(2,1)S(1)}, u32[]{:S(2)}, u32[]{:S(2)}) collective-permute-start(bf16[256,1152]{1,0:T(8,128)(2,1)S(1)} %shard_map.103.near_a), channel_id=1, source_target_pairs={{0,2},{2,0},{4,6},{6,4},{8,10},{10,8},{12,14},{14,12},{1,3},{3,1},... | collective-permute-start | bytes 1769480 | tf_op jit(solution)/shard_map/ppermute | solution.py:314
  27.2 12.1 %all-to-all-start = ((bf16[8,64,128]{2,1,0:T(8,128)(2,1)}), bf16[8,64,128]{2,1,0:T(8,128)(2,1)S(1)}, u32[]{:S(2)}, u32[]{:S(2)}) async-start(bf16[8,64,128]{2,1,0:T(8,128)(2,1)} %get-tuple-element.22), calls=%async_computation | async-start | bytes 262144 | tf_op jit(solution)/shard_map/all_to_all | solution.py:315
  32.0 8.7 %collective-permute-start.4 = (bf16[256,1152]{1,0:T(8,128)(2,1)S(1)}, bf16[256,1152]{1,0:T(8,128)(2,1)S(1)}, u32[]{:S(2)}, u32[]{:S(2)}) collective-permute-start(bf16[256,1152]{1,0:T(8,128)(2,1)S(1)} %shard_map.103.near_a), channel_id=1, source_target_pairs={{0,1},{1,0},{2,3},{3,2},{4,5},{5,4},{6,7},{7,6},{8,9},{9,8},{10,11... | collective-permute-start | bytes 1769480 | tf_op jit(solution)/shard_map/ppermute | solution.py:313
  33.4 7.2 %collective-permute-start.5 = (bf16[256,1152]{1,0:T(8,128)(2,1)S(1)}, bf16[256,1152]{1,0:T(8,128)(2,1)S(1)}, u32[]{:S(2)}, u32[]{:S(2)}) collective-permute-start(bf16[256,1152]{1,0:T(8,128)(2,1)S(1)} %collective-permute-done.3.near_b), channel_id=1, source_target_pairs={{0,1},{1,0},{2,3},{3,2},{4,5},{5,4},{6,7},{7,6},{8,9},{9,8},{10,11... | collective-permute-start | bytes 1769480 | tf_op jit(solution)/shard_map/ppermute | solution.py:313
  34.3 5.0 %collective-permute-start.12 = (bf16[64,1024]{0,1:T(8,128)(2,1)}, bf16[64,1024]{0,1:T(8,128)(2,1)}, u32[]{:S(2)}, u32[]{:S(2)}) collective-permute-start(bf16[64,1024]{0,1:T(8,128)(2,1)} %copy.14), channel_id=1, source_target_pairs={{0,1},{1,0},{2,3},{3,2},{4,5},{5,4},{6,7},{7,6},{8,9},{9,8},{10,11... | collective-permute-start | bytes 393224 | tf_op jit(solution)/shard_map/ppermute | solution.py:313
  50.0 2.7 %collective-permute-start.14 = (bf16[512,1024]{1,0:T(8,128)(2,1)S(1)}, bf16[512,1024]{1,0:T(8,128)(2,1)S(1)}, u32[]{:S(2)}, u32[]{:S(2)}) collective-permute-start(bf16[512,1024]{1,0:T(8,128)(2,1)S(1)} %get-tuple-element.26), channel_id=1, source_target_pairs={{0,1},{1,0},{2,3},{3,2},{4,5},{5,4},{6,7},{7,6},{8,9},{9,8},{10,11... | collective-permute-start | bytes 3145736 | tf_op jit(solution)/shard_map/ppermute | solution.py:313
  50.4 32.8 %collective-permute-start.21 = (bf16[64,1024]{1,0:T(8,128)(2,1)}, bf16[64,1024]{1,0:T(8,128)(2,1)}, u32[]{:S(2)}, u32[]{:S(2)}) collective-permute-start(bf16[64,1024]{1,0:T(8,128)(2,1)} %get-tuple-element.39.own), channel_id=1, source_target_pairs={{0,1},{1,0},{2,3},{3,2},{4,5},{5,4},{6,7},{7,6},{8,9},{9,8},{10,11... | collective-permute-start | bytes 393224 | tf_op jit(solution)/shard_map/ppermute | solution.py:313
  50.6 3.4 %collective-permute-start.13 = (bf16[8,64,128]{2,1,0:T(8,128)(2,1)S(1)}, bf16[8,64,128]{2,1,0:T(8,128)(2,1)S(1)}, u32[]{:S(2)}, u32[]{:S(2)}) collective-permute-start(bf16[8,64,128]{2,1,0:T(8,128)(2,1)S(1)} %get-tuple-element.24), channel_id=1, source_target_pairs={{0,1},{1,0},{2,3},{3,2},{4,5},{5,4},{6,7},{7,6},{8,9},{9,8},{10,11... | collective-permute-start | bytes 393224 | tf_op jit(solution)/shard_map/ppermute | solution.py:313
  53.2 17.7 %collective-permute-start.16 = (bf16[256,1024]{1,0:T(8,128)(2,1)S(1)}, bf16[256,1024]{1,0:T(8,128)(2,1)S(1)}, u32[]{:S(2)}, u32[]{:S(2)}) collective-permute-start(bf16[256,1024]{1,0:T(8,128)(2,1)S(1)} %shard_map.108.after), channel_id=1, source_target_pairs={{0,2},{2,0},{4,6},{6,4},{8,10},{10,8},{12,14},{14,12},{1,3},{3,1},... | collective-permute-start | bytes 1572872 | tf_op jit(solution)/shard_map/ppermute | solution.py:314
  54.9 14.4 %all-to-all-start.1 = ((bf16[8,64,128]{2,1,0:T(8,128)(2,1)}), bf16[8,64,128]{2,1,0:T(8,128)(2,1)S(1)}, u32[]{:S(2)}, u32[]{:S(2)}) async-start(bf16[8,64,128]{2,1,0:T(8,128)(2,1)} %shard_map.110), calls=%async_computation.1 | async-start | bytes 262144 | tf_op jit(solution)/shard_map/all_to_all | solution.py:315
  69.2 7.9 %collective-permute-start.15 = (bf16[8,64,128]{2,1,0:T(8,128)(2,1)}, bf16[8,64,128]{2,1,0:T(8,128)(2,1)S(1)}, u32[]{:S(2)}, u32[]{:S(2)}) collective-permute-start(bf16[8,64,128]{2,1,0:T(8,128)(2,1)} %get-tuple-element.31), channel_id=1, source_target_pairs={{0,1},{1,0},{2,3},{3,2},{4,5},{5,4},{6,7},{7,6},{8,9},{9,8},{10,11... | collective-permute-start | bytes 393224 | tf_op jit(solution)/shard_map/ppermute | solution.py:313
  70.3 12.8 %collective-permute-start.20 = (f32[64,128]{1,0:T(8,128)S(1)}, f32[64,128]{1,0:T(8,128)S(1)}, u32[]{:S(2)}, u32[]{:S(2)}) collective-permute-start(f32[64,128]{1,0:T(8,128)S(1)} %get-tuple-element.38.mine), channel_id=1, source_target_pairs={{0,1},{1,0},{2,3},{3,2},{4,5},{5,4},{6,7},{7,6},{8,9},{9,8},{10,11... | collective-permute-start | bytes 98312 | tf_op jit(solution)/shard_map/ppermute | solution.py:313
  72.6 19.6 %collective-permute-start.19 = (bf16[64,1024]{1,0:T(8,128)(2,1)S(1)}, bf16[64,1024]{1,0:T(8,128)(2,1)S(1)}, u32[]{:S(2)}, u32[]{:S(2)}) collective-permute-start(bf16[64,1024]{1,0:T(8,128)(2,1)S(1)} %get-tuple-element.33.after), channel_id=1, source_target_pairs={{0,4},{2,6},{4,0},{6,2},{8,12},{10,14},{12,8},{14,10},{1,5},{3,7},... | collective-permute-start | bytes 393224 | tf_op jit(solution)/shard_map/ppermute | solution.py:314
  74.7 10.5 %collective-permute-start.17 = (bf16[64,1024]{1,0:T(8,128)(2,1)S(1)}, bf16[64,1024]{1,0:T(8,128)(2,1)S(1)}, u32[]{:S(2)}, u32[]{:S(2)}) collective-permute-start(bf16[64,1024]{1,0:T(8,128)(2,1)S(1)} %get-tuple-element.36), channel_id=1, source_target_pairs={{0,12},{2,14},{4,8},{6,10},{8,4},{10,6},{12,0},{14,2},{1,13},{3,15... | collective-permute-start | bytes 393224 | tf_op jit(solution)/shard_map/ppermute | solution.py:314
  77.1 15.1 %collective-permute-start.18 = (bf16[64,1024]{1,0:T(8,128)(2,1)S(1)}, bf16[64,1024]{1,0:T(8,128)(2,1)S(1)}, u32[]{:S(2)}, u32[]{:S(2)}) collective-permute-start(bf16[64,1024]{1,0:T(8,128)(2,1)S(1)} %get-tuple-element.37), channel_id=1, source_target_pairs={{0,8},{2,10},{4,12},{6,14},{8,0},{10,2},{12,4},{14,6},{1,9},{3,11}... | collective-permute-start | bytes 393224 | tf_op jit(solution)/shard_map/ppermute | solution.py:314
  78.1 16.5 %all-to-all-start.2 = ((bf16[8,64,256]{2,1,0:T(8,128)(2,1)}), bf16[8,64,256]{2,1,0:T(8,128)(2,1)S(1)}, u32[]{:S(2)}, u32[]{:S(2)}) async-start(bf16[8,64,256]{2,1,0:T(8,128)(2,1)} %shard_map.115.after), calls=%async_computation.2 | async-start | bytes 524288 | tf_op jit(solution)/shard_map/all_to_all | solution.py:315
  (17 other events, 120.8 us)
